TPU v7x, 32 devices: a whole 2x2x4 slice. The times are simulated.
32 devices in a mesh: row: 8 (over z, y), col: 4 (over x, core).
Axes of the slice: x: 2, y: 2, z: 4, core: 2. Of those that a mesh axis runs over, the one named last changes fastest.
Arguments:
- density: bfloat16 [2, 256, 3, 128, 128], P(None, ('row', 'col')), may hold values from -1 to 3, as said below
- core_hamiltonian: bfloat16 [2, 256, 3, 128, 128], P(None, ('row', 'col')), may hold values from -2 to 2, as said below
- grid_term_old: float32 [256, 128, 128], P(('row', 'col')), may hold values from -0.25 to 0.25
- lead_blocks: int32 [8], replicated, may hold values from 0 to 255, as said below
- absorption: float32 [8], replicated, may hold values from 0.5 to 2
- collocation: bfloat16 [768, 2048, 128], P(('row', 'col')), may hold values from -0.5 to 0.5
- brick_block: int32 [8, 96], P(None, 'col'), may hold values from 0 to 255, as said below
Outputs:
- density_next: bfloat16 [2, 256, 3, 128, 128], P(None, ('row', 'col'))
- grid_term: float32 [256, 128, 128], P(('row', 'col'))
Inputs may be any that keep to these rules, and one draw needn't show every extreme that they name: density is Hermitian: block (j, i) is the conjugate transpose of block (i, j); slots outside the matrix are zero. core_hamiltonian is Hermitian: block (j, i) is the conjugate transpose of block (i, j); slots outside the matrix are zero. `lead_blocks`: Distinct; 4 of them among the first 16 block rows and the others among the last 16. `brick_block`: entry [r, c * 24 + t] is the block of brick t of device (row r, col c); that block is held by a device of the same col. Among the bricks of one device at most 3 have blocks on devices of one row index, and in every device some row index has exactly 3.
All inputs are finite; a program needn't handle non-finite values.
Results may differ from a plain program's by a relative error of at most 0.007.
Values may be sent and summed in bfloat16 or wider, within the bound.
No kernel may reach another device: no remote copies, remote signals or barrier semaphores. Data moves between devices by JAX's collectives and lax.ppermute only.
A program may use at most 128 MiB of HBM per device.

v0:
```python
import functools

import jax
import jax.numpy as jnp
from jax import lax
from jax.experimental import pallas as pl
from jax.experimental.pallas import tpu as pltpu
from jax.sharding import PartitionSpec as P

CAP = 3
HALF_STEP = 0.2
SECOND_ORDER = 0.5 * HALF_STEP * HALF_STEP
GRID_FACTOR = 0.1
F32 = jnp.float32
BF16 = jnp.bfloat16
VMEM_LIMIT = 60 * 1024 * 1024


def call(kernel, out_shape, flops, scalars=0, grid=(), in_specs=None, out_specs=None, scratch=()):
    whole = pl.BlockSpec(memory_space=pltpu.VMEM)
    return pl.pallas_call(
        kernel,
        out_shape=out_shape,
        grid_spec=pltpu.PrefetchScalarGridSpec(
            num_scalar_prefetch=scalars,
            grid=grid,
            in_specs=in_specs,
            out_specs=jax.tree.map(lambda _: whole, out_shape) if out_specs is None else out_specs,
            scratch_shapes=scratch,
        ),
        compiler_params=pltpu.CompilerParams(vmem_limit_bytes=VMEM_LIMIT),
        cost_estimate=pl.CostEstimate(flops=flops, bytes_accessed=4 << 20, transcendentals=0),
    )


def block_spec(shape, index):
    return pl.BlockSpec(shape, lambda *_: index)


def joined(re, im):
    return jnp.concatenate([re, im], axis=1)


def dagger(value):
    width = value.shape[0]
    re = value[:, :width].astype(F32).T
    im = value[:, width:].astype(F32).T
    return joined(re, -im).astype(BF16)


def as_right(value):
    width = value.shape[0]
    return jnp.concatenate([value, joined(-value[:, width:], value[:, :width])], axis=0)


def band_column(left, right, j, low, high):
    total = {}
    for mid in (j - 1, j, j + 1):
        rows = [i for i in range(max(mid, j) - 1, min(mid, j) + 2) if low <= i <= high]
        if not rows:
            continue
        stacked = jnp.concatenate([left(i, mid) for i in rows], axis=0)
        result = jnp.dot(stacked, as_right(right(mid, j)), preferred_element_type=F32)
        width = result.shape[0] // len(rows)
        for n, i in enumerate(rows):
            part = result[n * width : (n + 1) * width]
            total[i] = part if i not in total else total[i] + part
    return total


def times_i(value):
    width = value.shape[0]
    return joined(-value[:, width:], value[:, :width])


def propagate(count, get_q, get_left, get_right, hp_ref, moved_ref, wh_ref, write):
    def get(ref):
        return lambda i, j: ref[i + 1, j - i + 1]

    for j in range(-1, count + 1):
        for i, value in band_column(get_left, get_q, j, -1, count).items():
            hp_ref[i + 1, j - i + 1] = value.astype(BF16)
    for j in range(-1, count + 1):
        for i, value in band_column(get_left, get(hp_ref), j, 0, count - 1).items():
            hp = hp_ref[i + 1, j - i + 1].astype(F32)
            moved = get_q(i, j).astype(F32) - HALF_STEP * times_i(hp) - SECOND_ORDER * value
            moved_ref[i + 1, j - i + 1] = moved.astype(BF16)
    for j in range(-1, count + 1):
        for i, value in band_column(get(moved_ref), get_right, j, 0, count - 1).items():
            wh_ref[i + 1, j - i + 1] = value.astype(BF16)
    for j in range(-1, count + 1):
        for i, value in band_column(get(wh_ref), get_right, j, 0, count - 1).items():
            moved = moved_ref[i + 1, j - i + 1].astype(F32)
            wh = wh_ref[i + 1, j - i + 1].astype(F32)
            out = moved + HALF_STEP * times_i(wh) - SECOND_ORDER * value
            write(i, j, out.astype(BF16))


def symmetric(value):
    return 0.5 * (value + value.T)


def send_kernel(parity, q_hi, q_hi2, q_lo, q_lo2, h_hi, h_hi2, h_lo, h_lo2, g_hi, g_lo, send_a, send_b):
    def h_diag(h_ref, g_ref):
        return (h_ref[0, 0, 0].astype(F32) + symmetric(g_ref[0])).astype(BF16)

    right = [q_hi[0, 0, 0], q_hi[1, 0, 0], q_hi2[0, 0, 0], q_hi2[1, 0, 0],
             h_diag(h_hi, g_hi), h_hi[1, 0, 0], h_hi2[0, 0, 0], h_hi2[1, 0, 0], h_hi[0, 0, 0]]
    left = [q_lo[0, 0, 0], q_lo[1, 0, 0], q_lo2[0, 0, 0], q_lo2[1, 0, 0],
            h_diag(h_lo, g_lo), h_lo[1, 0, 0], h_lo2[0, 0, 0], h_lo2[1, 0, 0], h_lo[0, 0, 0]]
    even = parity[0] == 0

    @pl.when(even)
    def _():
        for n, (x, y) in enumerate(zip(right, left)):
            send_a[n] = x
            send_b[n] = y

    @pl.when(jnp.logical_not(even))
    def _():
        for n, (x, y) in enumerate(zip(right, left)):
            send_a[n] = y
            send_b[n] = x


def halo_reader(parity, got_a, got_b):
    even = parity[0] == 0

    def low(n):
        return jnp.where(even, got_b[n], got_a[n])

    def high(n):
        return jnp.where(even, got_a[n], got_b[n])

    return low, high


def set_diagonals(count, gamma, diag_re, diag_im, left_ref, right_ref):
    width = diag_re(0).shape[0]
    rows = lax.broadcasted_iota(jnp.int32, (width, width), 0)
    columns = lax.broadcasted_iota(jnp.int32, (width, width), 1)
    for i in range(-1, count + 1):
        re = diag_re(i)
        im = diag_im(i).astype(F32)
        shift = jnp.where(rows == columns, gamma[i + 1], 0.0)
        left_ref[i + 1] = joined(re, (im - shift).astype(BF16))
        right_ref[i + 1] = joined(re, (im + shift).astype(BF16))


def band_access(count, core, far_low, far_high, low_edge, high_edge, diag_ref):
    def get(i, j):
        if i == j:
            return diag_ref[i + 1]
        if i == -1:
            return far_low() if j == -2 else low_edge[...]
        if i == count:
            return far_high() if j == count + 1 else high_edge[...]
        return joined(core[0, i, j - i + 1], core[1, i, j - i + 1])

    return get


def first_kernel(count, parity, gamma, pick, dens, core, grid_old, got_a, got_b,
                 half, outgoing, send_a, send_b,
                 hp_ref, moved_ref, wh_ref, left_ref, right_ref, edges):
    low, high = halo_reader(parity, got_a, got_b)

    def band(ref, i, j):
        return joined(ref[0, i, j - i + 1], ref[1, i, j - i + 1])

    edges[0] = dagger(band(dens, 0, -1))
    edges[1] = dagger(band(dens, count - 1, count))
    edges[2] = dagger(band(core, 0, -1))
    edges[3] = dagger(band(core, count - 1, count))

    def get_q(i, j):
        if i == -2:
            return joined(low(2), low(3))
        if i == -1:
            return joined(low(0), low(1)) if j == -1 else edges[0]
        if i == count:
            return joined(high(0), high(1)) if j == count else edges[1]
        if i == count + 1:
            return joined(high(2), high(3))
        return band(dens, i, j)

    def diag_re(i):
        if i == -1:
            return low(4)
        if i == count:
            return high(4)
        return (core[0, i, 1].astype(F32) + symmetric(grid_old[i])).astype(BF16)

    def diag_im(i):
        return low(5) if i == -1 else high(5) if i == count else core[1, i, 1]

    set_diagonals(count, gamma, diag_re, diag_im, left_ref, right_ref)

    def far_low():
        return joined(low(6), low(7))

    def far_high():
        return joined(high(6), high(7))

    get_left = band_access(count, core, far_low, far_high, edges.at[2], edges.at[3], left_ref)
    get_right = band_access(count, core, far_low, far_high, edges.at[2], edges.at[3], right_ref)

    def write(i, j, value):
        width = value.shape[0]
        half[0, i, j - i + 1] = value[:, :width]
        half[1, i, j - i + 1] = value[:, width:]

    propagate(count, get_q, get_left, get_right, hp_ref, moved_ref, wh_ref, write)

    right = [(count - 1, 1), (count - 1, 2), (count - 2, 2)]
    left = [(0, 1), (0, 0), (1, 0)]

    def send(to_a, to_b):
        for n in range(3):
            for part in range(2):
                send_a[2 * n + part] = half[part, to_a[n][0], to_a[n][1]]
                send_b[2 * n + part] = half[part, to_b[n][0], to_b[n][1]]

    @pl.when(parity[0] == 0)
    def _():
        send(right, left)

    @pl.when(parity[0] != 0)
    def _():
        send(left, right)

    def place(n, carry):
        outgoing[n] = half[0, pick[n], 1]
        return carry

    lax.fori_loop(0, outgoing.shape[0], place, 0)


def brick_kernel(bricks, where_ref, colloc, incoming, returned):
    step = pl.program_id(0)
    points, width = colloc.shape[1:]
    slots = returned.shape[0]
    scale = GRID_FACTOR * width / points

    @pl.when(step == 0)
    def _():
        if slots > bricks:
            returned[...] = jnp.zeros_like(returned)

    c0, c1 = colloc[0], colloc[1]
    s0 = where_ref[2 * step]
    s1 = where_ref[2 * step + 1]
    q0 = incoming[s0].astype(F32).T
    q1 = incoming[s1].astype(F32).T
    zero = jnp.zeros_like(q0)
    both = jnp.concatenate([joined(q0, zero), joined(zero, q1)], axis=0).astype(BF16)
    turned = jnp.concatenate([c0.T, c1.T], axis=0)
    wide = turned.astype(F32)
    projected = jnp.dot(both, turned, preferred_element_type=F32) * wide
    weighted = []
    for n in range(2):
        rows = slice(n * width, (n + 1) * width)
        dens = jnp.sum(projected[rows], axis=0, keepdims=True)
        potential = dens * lax.rsqrt(1.0 + dens * dens)
        weighted.append((potential * wide[rows]).astype(BF16))
    result = jnp.dot(jnp.concatenate(weighted, axis=0), joined(c0, c1), preferred_element_type=F32)
    returned[s0] = (scale * result[:width, :width]).T.astype(BF16)
    returned[s1] = (scale * result[width:, width:]).T.astype(BF16)


def collect_kernel(count, parity, place, arriving, core, grid_term, send_a, send_b):
    grid_term[...] = jnp.zeros_like(grid_term)

    def add(n, carry):
        @pl.when(place[n] >= 0)
        def _():
            grid_term[place[n]] += arriving[n].astype(F32)

        return carry

    lax.fori_loop(0, arriving.shape[0], add, 0)
    right = (core[0, count - 1, 0].astype(F32) + grid_term[count - 1]).astype(BF16)
    left = (core[0, 0, 0].astype(F32) + grid_term[0]).astype(BF16)
    even = parity[0] == 0
    send_a[0] = jnp.where(even, right, left)
    send_b[0] = jnp.where(even, left, right)


def second_kernel(count, parity, gamma, half, core, grid_term, core_a, core_b, half_a, half_b, diag_a, diag_b,
                  out, hp_ref, moved_ref, wh_ref, left_ref, right_ref, edges):
    core_low, core_high = halo_reader(parity, core_a, core_b)
    half_low, half_high = halo_reader(parity, half_a, half_b)
    diag_low, diag_high = halo_reader(parity, diag_a, diag_b)

    def band(ref, i, j):
        return joined(ref[0, i, j - i + 1], ref[1, i, j - i + 1])

    edges[0] = dagger(band(core, 0, -1))
    edges[1] = dagger(band(core, count - 1, count))

    def get_q(i, j):
        if i < 0:
            n = 0 if i == -1 and j == -1 else 2 if i == -1 else 4
            return joined(half_low(n), half_low(n + 1))
        if i >= count:
            n = 0 if i == count and j == count else 2 if i == count else 4
            return joined(half_high(n), half_high(n + 1))
        return band(half, i, j)

    def diag_re(i):
        if i == -1:
            return diag_low(0)
        if i == count:
            return diag_high(0)
        return (core[0, i, 1].astype(F32) + grid_term[i]).astype(BF16)

    def diag_im(i):
        return core_low(5) if i == -1 else core_high(5) if i == count else core[1, i, 1]

    set_diagonals(count, gamma, diag_re, diag_im, left_ref, right_ref)

    def far_low():
        return joined(core_low(6), core_low(7))

    def far_high():
        return joined(core_high(6), core_high(7))

    get_left = band_access(count, core, far_low, far_high, edges.at[0], edges.at[1], left_ref)
    get_right = band_access(count, core, far_low, far_high, edges.at[0], edges.at[1], right_ref)

    def write(i, j, value):
        width = value.shape[0]
        out[0, i, j - i + 1] = value[:, :width]
        out[1, i, j - i + 1] = value[:, width:]

    propagate(count, get_q, get_left, get_right, hp_ref, moved_ref, wh_ref, write)


def rows_gamma(lead_blocks, absorption, first_row, row_count):
    rows_here = first_row + jnp.arange(row_count, dtype=jnp.int32)
    equal = lead_blocks[None, :] == rows_here[:, None]
    return jnp.sum(jnp.where(equal, absorption[None, :], 0.0), axis=1)


def exchange(send_a, send_b, total):
    first = [(i, i ^ 1) for i in range(total)]
    second = [(i, i + 1) if i % 2 else (i, i - 1) for i in range(1, total - 1)]
    axes = ("row", "col")
    return lax.ppermute(send_a, axes, first), lax.ppermute(send_b, axes, second)


def shards(density, core, grid_old, lead_blocks, absorption, collocation, brick_block):
    count = density.shape[1]
    width = density.shape[-1]
    row_size = lax.axis_size("row")
    col_size = lax.axis_size("col")
    total = row_size * col_size
    position = lax.axis_index(("row", "col"))
    parity = (position % 2).astype(jnp.int32).reshape(1)
    gamma = rows_gamma(lead_blocks, absorption, position * count - 1, count + 2)
    bricks = brick_block.shape[1]
    slots = row_size * CAP
    vmem = pl.BlockSpec(memory_space=pltpu.VMEM)

    own_row = lax.axis_index("row")
    source_row = brick_block // count // col_size
    local_block = brick_block % count
    earlier = jnp.arange(bricks)[None, :] < jnp.arange(bricks)[:, None]
    same_source = source_row[:, :, None] == source_row[:, None, :]
    slot_number = jnp.sum((same_source & earlier[None]).astype(jnp.int32), axis=2)
    own_source = lax.dynamic_index_in_dim(source_row, own_row, 0, keepdims=False)
    own_slot = lax.dynamic_index_in_dim(slot_number, own_row, 0, keepdims=False)
    where_own = own_source * CAP + own_slot
    mine = (source_row == own_row)[:, :, None] & (
        slot_number[:, :, None] == jnp.arange(CAP, dtype=jnp.int32)[None, None, :]
    )
    place = jnp.max(jnp.where(mine, local_block[:, :, None], -1), axis=1).reshape(slots)
    pick = jnp.maximum(place, 0)

    block = (2, 1, 1, width, width)
    grid_block = (1, width, width)
    last = count - 1
    message = jax.ShapeDtypeStruct((9, width, width), BF16)
    send_a, send_b = call(
        send_kernel,
        (message, message),
        flops=1 << 20,
        scalars=1,
        grid=(1,),
        in_specs=[block_spec(block, (0, i, k, 0, 0)) for i, k in
                  ((last, 1), (last - 1, 2), (0, 1), (1, 0), (last, 1), (last, 0), (0, 1), (0, 2))]
        + [block_spec(grid_block, (last, 0, 0)), block_spec(grid_block, (0, 0, 0))],
    )(parity, *([density] * 4), *([core] * 4), grid_old, grid_old)
    got_a, got_b = exchange(send_a, send_b, total)

    def band_scratch(rows):
        return pltpu.VMEM((rows, 3, width, 2 * width), BF16)

    prop_scratch = [band_scratch(count + 2)] * 3 + [pltpu.VMEM((count + 2, width, 2 * width), BF16)] * 2
    prop_flops = 8 * 7 * 4 * count * width**3
    half_message = jax.ShapeDtypeStruct((6, width, width), BF16)
    half, outgoing, send_a, send_b = call(
        functools.partial(first_kernel, count),
        (
            jax.ShapeDtypeStruct(density.shape, BF16),
            jax.ShapeDtypeStruct((slots, width, width), BF16),
            half_message,
            half_message,
        ),
        flops=prop_flops,
        scalars=3,
        in_specs=[vmem] * 5,
        scratch=prop_scratch + [pltpu.VMEM((4, width, 2 * width), BF16)],
    )(parity, gamma, pick, density, core, grid_old, got_a, got_b)

    incoming = lax.all_to_all(outgoing, "row", split_axis=0, concat_axis=0, tiled=True)
    half_a, half_b = exchange(send_a, send_b, total)

    points = collocation.shape[1]
    returned = call(
        functools.partial(brick_kernel, bricks),
        jax.ShapeDtypeStruct((slots, width, width), BF16),
        flops=4 * bricks * points * width**2,
        scalars=1,
        grid=(bricks // 2,),
        in_specs=[pl.BlockSpec((2, points, width), lambda t, *_: (t, 0, 0)), vmem],
    )(where_own, collocation, incoming)
    arriving = lax.all_to_all(returned, "row", split_axis=0, concat_axis=0, tiled=True)

    diag_message = jax.ShapeDtypeStruct((1, width, width), BF16)
    grid_term, send_a, send_b = call(
        functools.partial(collect_kernel, count),
        (jax.ShapeDtypeStruct((count, width, width), F32), diag_message, diag_message),
        flops=1 << 20,
        scalars=2,
        grid=(1,),
        in_specs=[vmem, block_spec((1, count, 1, width, width), (0, 0, 1, 0, 0))],
    )(parity, place, arriving, core)
    diag_a, diag_b = exchange(send_a, send_b, total)

    density_next = call(
        functools.partial(second_kernel, count),
        jax.ShapeDtypeStruct(density.shape, BF16),
        flops=prop_flops,
        scalars=2,
        in_specs=[vmem] * 9,
        scratch=prop_scratch + [pltpu.VMEM((2, width, 2 * width), BF16)],
    )(parity, gamma, half, core, grid_term, got_a, got_b, half_a, half_b, diag_a, diag_b)
    return (density_next, grid_term)


def solution(mesh):
    band = P(None, ("row", "col"), None, None, None)
    blocks = P(("row", "col"), None, None)
    return jax.shard_map(
        shards,
        mesh=mesh,
        in_specs=(band, band, blocks, P(), P(), blocks, P(None, "col")),
        out_specs=(band, blocks),
        check_vma=False,
    )
```

profile of v0, /device:TPU:1, one launch (start us, length us, event | category | flops | bytes accessed | tf_op | source)
XLA Modules:
  0.0 112.5 jit_solution(5016181032392981611)
XLA Ops:
  0.6 0.0 copy-start.2
  0.7 0.0 copy-start.4
  0.7 0.0 copy-start.5
  0.7 2.2 %shard_map.86 = (bf16[9,128,128]{2,1,0:T(8,128)(2,1)}, bf16[9,128,128]{2,1,0:T(8,128)(2,1)}) custom-call(s32[1]{0:T(128)} %bitcast.parity, bf16[2,8,3,128,128]{4,3,2,1,0:T(8,128)(2,1)} %dens.1, bf16[2,8,3,128,128]{4,3,2,1,0:T(8,128)(2,1)} %dens.1, bf16[2,8,3,128,128]{4,3,2,1,0:T(8,128)(2,1)} %dens.1, bf16[2,8,3,128,128]{4,3,2,1,0:T(8,128)(2,1)} %dens.1, ...), custom_call_target="tpu_custom_call" | custom-call | flops 1048576 | bytes 4194304 | tf_op jit(solution)/shard_map/pallas_call | solution.py:384
  2.9 0.0 collective-permute-start
  2.9 4.4 %collective-permute-start.1 = (bf16[9,128,128]{2,1,0:T(8,128)(2,1)}, bf16[9,128,128]{2,1,0:T(8,128)(2,1)S(1)}, u32[]{:S(2)}, u32[]{:S(2)}) collective-permute-start(bf16[9,128,128]{2,1,0:T(8,128)(2,1)} %get-tuple-element.12), channel_id=1, source_target_pairs={{1,2},{2,1},{3,4},{4,3},{5,6},{6,5},{7,8},{8,7},{9,10},{10,9},{11,... | collective-permute-start | bytes 884744 | tf_op jit(solution)/shard_map/ppermute | solution.py:349
  7.4 0.0 copy-done.2
  7.4 0.3 convert_reduce_fusion
  7.7 0.2 select_reduce_fusion
  7.9 0.1 copy.9
  8.0 0.1 reshape.37.place
  8.1 0.0 copy-done.4
  8.1 0.0 copy-done.5
  8.1 0.0 copy-start.3
  8.1 0.7 select_reduce_fusion.1.gamma
  8.8 0.6 broadcast_maximum_fusion.pick
  9.3 0.0 collective-permute-done.got_a.core_a
  9.3 0.0 copy-start.6
  9.3 5.2 %collective-permute-done.1.got_b.core_b = bf16[9,128,128]{2,1,0:T(8,128)(2,1)S(1)} collective-permute-done((bf16[9,128,128]{2,1,0:T(8,128)(2,1)}, bf16[9,128,128]{2,1,0:T(8,128)(2,1)S(1)}, u32[]{:S(2)}, u32[]{:S(2)}) %collective-permute-start.1) | collective-permute-done | bytes 294944 | tf_op jit(solution)/shard_map/ppermute | solution.py:349
  14.5 0.0 copy-done.6
  14.5 0.0 copy-start.7
  14.5 0.7 copy-done.7
  15.2 8.9 %shard_map.87 = (bf16[2,8,3,128,128]{4,3,2,1,0:T(8,128)(2,1)}, bf16[24,128,128]{2,1,0:T(8,128)(2,1)}, bf16[6,128,128]{2,1,0:T(8,128)(2,1)}, bf16[6,128,128]{2,1,0:T(8,128)(2,1)}) custom-call(s32[1]{0:T(128)} %bitcast.parity, f32[10]{0:T(128)} %select_reduce_fusion.1.gamma, s32[24]{0:T(128)} %broadcast_maximum_fusion.pick, bf16[2,8,3,128,128]{4,3,2,1,0:T(8,128)(2,1)} %dens.1, ...), custom_call_target="tpu_custom_call" | custom-call | flops 3758096384 | bytes 4194304 | tf_op jit(solution)/shard_map/pallas_call | solution.py:402
  24.1 0.0 copy-done.3
  24.1 7.0 %all-to-all-start = ((bf16[24,128,128]{2,1,0:T(8,128)(2,1)}), bf16[24,128,128]{2,1,0:T(8,128)(2,1)S(1)}, u32[]{:S(2)}, u32[]{:S(2)}) async-start(bf16[24,128,128]{2,1,0:T(8,128)(2,1)} %get-tuple-element.14), calls=%async_computation | async-start | bytes 1572864 | tf_op jit(solution)/shard_map/all_to_all | solution.py:416
  31.2 0.5 add_bitcast_fusion.where_ref
  31.7 18.8 %all-to-all-done.incoming = bf16[24,128,128]{2,1,0:T(8,128)(2,1)S(1)} async-done(((bf16[24,128,128]{2,1,0:T(8,128)(2,1)}), bf16[24,128,128]{2,1,0:T(8,128)(2,1)S(1)}, u32[]{:S(2)}, u32[]{:S(2)}) %all-to-all-start) | async-done | bytes 786464 | tf_op jit(solution)/shard_map/all_to_all | solution.py:416
  50.5 0.0 copy-start
  50.5 0.9 copy-done
  51.4 16.4 %shard_map.88 = bf16[24,128,128]{2,1,0:T(8,128)(2,1)} custom-call(s32[24]{0:T(128)} %add_bitcast_fusion.where_ref, bf16[24,2048,128]{2,1,0:T(8,128)(2,1)} %colloc.1, bf16[24,128,128]{2,1,0:T(8,128)(2,1)} %copy-done), custom_call_target="tpu_custom_call" | custom-call | flops 3221225472 | bytes 4194304 | tf_op jit(solution)/shard_map/pallas_call | solution.py:420
  67.8 0.0 copy-start.9
  67.8 0.0 copy-start.8
  67.8 4.7 %all-to-all-start.1 = ((bf16[24,128,128]{2,1,0:T(8,128)(2,1)}), bf16[24,128,128]{2,1,0:T(8,128)(2,1)S(1)}, u32[]{:S(2)}, u32[]{:S(2)}) async-start(bf16[24,128,128]{2,1,0:T(8,128)(2,1)} %shard_map.88), calls=%async_computation.1 | async-start | bytes 1572864 | tf_op jit(solution)/shard_map/all_to_all | solution.py:428
  72.6 0.0 copy-done.9
  72.6 0.8 collective-permute-start.2
  73.4 0.0 copy-done.8
  73.4 2.1 %collective-permute-start.3 = (bf16[6,128,128]{2,1,0:T(8,128)(2,1)S(1)}, bf16[6,128,128]{2,1,0:T(8,128)(2,1)S(1)}, u32[]{:S(2)}, u32[]{:S(2)}) collective-permute-start(bf16[6,128,128]{2,1,0:T(8,128)(2,1)S(1)} %copy-done.8), channel_id=1, source_target_pairs={{1,2},{2,1},{3,4},{4,3},{5,6},{6,5},{7,8},{8,7},{9,10},{10,9},{11,... | collective-permute-start | bytes 589832 | tf_op jit(solution)/shard_map/ppermute | solution.py:349
  75.6 16.3 %all-to-all-done.1.arriving = bf16[24,128,128]{2,1,0:T(8,128)(2,1)S(1)} async-done(((bf16[24,128,128]{2,1,0:T(8,128)(2,1)}), bf16[24,128,128]{2,1,0:T(8,128)(2,1)S(1)}, u32[]{:S(2)}, u32[]{:S(2)}) %all-to-all-start.1) | async-done | bytes 786464 | tf_op jit(solution)/shard_map/all_to_all | solution.py:428
  91.9 0.0 copy-start.1
  91.9 0.9 copy-done.1
  92.7 3.2 %shard_map.89 = (f32[8,128,128]{2,1,0:T(8,128)}, bf16[1,128,128]{2,1,0:T(8,128)(2,1)}, bf16[1,128,128]{2,1,0:T(8,128)(2,1)}) custom-call(s32[1]{0:T(128)} %bitcast.parity, s32[24]{0:T(128)} %copy-done.3, bf16[24,128,128]{2,1,0:T(8,128)(2,1)} %copy-done.1, bf16[2,8,3,128,128]{4,3,2,1,0:T(8,128)(2,1)} %core.5), custom_call_target="tpu_custom_call" | custom-call | flops 1048576 | bytes 4194304 | tf_op jit(solution)/shard_map/pallas_call | solution.py:431
  95.9 1.9 %collective-permute-start.4 = (bf16[1,128,128]{2,1,0:T(8,128)(2,1)}, bf16[1,128,128]{2,1,0:T(8,128)(2,1)S(1)}, u32[]{:S(2)}, u32[]{:S(2)}) collective-permute-start(bf16[1,128,128]{2,1,0:T(8,128)(2,1)} %get-tuple-element.18), channel_id=1, source_target_pairs={{0,1},{1,0},{2,3},{3,2},{4,5},{5,4},{6,7},{7,6},{8,9},{9,8},{10,11... | collective-permute-start | bytes 98312 | tf_op jit(solution)/shard_map/ppermute | solution.py:349
  97.7 2.1 %collective-permute-start.5 = (bf16[1,128,128]{2,1,0:T(8,128)(2,1)}, bf16[1,128,128]{2,1,0:T(8,128)(2,1)S(1)}, u32[]{:S(2)}, u32[]{:S(2)}) collective-permute-start(bf16[1,128,128]{2,1,0:T(8,128)(2,1)} %get-tuple-element.19), channel_id=1, source_target_pairs={{1,2},{2,1},{3,4},{4,3},{5,6},{6,5},{7,8},{8,7},{9,10},{10,9},{11,... | collective-permute-start | bytes 98312 | tf_op jit(solution)/shard_map/ppermute | solution.py:349
  99.9 0.0 collective-permute-done.2.half_a
  99.9 0.0 copy-start.10
  99.9 0.0 collective-permute-done.3.half_b
  99.9 0.0 copy-start.11
  99.9 0.0 collective-permute-done.4.diag_a
  99.9 0.0 copy-start.12
  99.9 3.5 %collective-permute-done.5.diag_b = bf16[1,128,128]{2,1,0:T(8,128)(2,1)S(1)} collective-permute-done((bf16[1,128,128]{2,1,0:T(8,128)(2,1)}, bf16[1,128,128]{2,1,0:T(8,128)(2,1)S(1)}, u32[]{:S(2)}, u32[]{:S(2)}) %collective-permute-start.5) | collective-permute-done | bytes 32800 | tf_op jit(solution)/shard_map/ppermute | solution.py:349
  103.4 0.0 copy-start.13
  103.4 0.0 copy-done.10
  103.4 0.0 copy-done.11
  103.4 0.0 copy-done.12
  103.4 0.6 copy-done.13
  104.0 8.5 %shard_map.90 = bf16[2,8,3,128,128]{4,3,2,1,0:T(8,128)(2,1)} custom-call(s32[1]{0:T(128)} %bitcast.parity, f32[10]{0:T(128)} %select_reduce_fusion.1.gamma, bf16[2,8,3,128,128]{4,3,2,1,0:T(8,128)(2,1)} %get-tuple-element.13.half, bf16[2,8,3,128,128]{4,3,2,1,0:T(8,128)(2,1)} %core.5, f32[8,128,128]{2,1,0:T(8,128)} %get-tuple-element.10.grid_term, ...), custom_call_target="tpu_custom_call" | custom-call | flops 3758096384 | bytes 4194304 | tf_op jit(solution)/shard_map/pallas_call | solution.py:441
  (4 shorter events, 0.0 us)
Async XLA Ops:
  0.6 6.7 %copy-start.2 = (s32[8,24]{1,0:T(8,128)S(1)}, s32[8,24]{1,0:T(8,128)}, u32[]{:S(2)}) copy-start(s32[8,24]{1,0:T(8,128)} %param.13) | copy-start | bytes 2308
  0.7 7.4 %copy-start.4 = (f32[8]{0:T(128)S(1)}, f32[8]{0:T(128)}, u32[]{:S(2)}) copy-start(f32[8]{0:T(128)} %param.11) | copy-start | bytes 100
  0.7 7.4 %copy-start.5 = (s32[8]{0:T(128)S(1)}, s32[8]{0:T(128)}, u32[]{:S(2)}) copy-start(s32[8]{0:T(128)} %param.10) | copy-start | bytes 100
  2.9 6.5 %collective-permute-start = (bf16[9,128,128]{2,1,0:T(8,128)(2,1)}, bf16[9,128,128]{2,1,0:T(8,128)(2,1)S(1)}, u32[]{:S(2)}, u32[]{:S(2)}) collective-permute-start(bf16[9,128,128]{2,1,0:T(8,128)(2,1)} %get-tuple-element.11), channel_id=1, source_target_pairs={{0,1},{1,0},{2,3},{3,2},{4,5},{5,4},{6,7},{7,6},{8,9},{9,8},{10,11... | collective-permute-start | bytes 884744 | tf_op jit(solution)/shard_map/ppermute | solution.py:349
  2.9 11.6 %collective-permute-start.1 = (bf16[9,128,128]{2,1,0:T(8,128)(2,1)}, bf16[9,128,128]{2,1,0:T(8,128)(2,1)S(1)}, u32[]{:S(2)}, u32[]{:S(2)}) collective-permute-start(bf16[9,128,128]{2,1,0:T(8,128)(2,1)} %get-tuple-element.12), channel_id=1, source_target_pairs={{1,2},{2,1},{3,4},{4,3},{5,6},{6,5},{7,8},{8,7},{9,10},{10,9},{11,... | collective-permute-start | bytes 884744 | tf_op jit(solution)/shard_map/ppermute | solution.py:349
  8.1 16.1 %copy-start.3 = (s32[24]{0:T(128)}, s32[24]{0:T(128)S(1)}, u32[]{:S(2)}) copy-start(s32[24]{0:T(128)S(1)} %reshape.37.place) | copy-start | bytes 292
  9.3 5.2 %copy-start.6 = (bf16[9,128,128]{2,1,0:T(8,128)(2,1)}, bf16[9,128,128]{2,1,0:T(8,128)(2,1)S(1)}, u32[]{:S(2)}) copy-start(bf16[9,128,128]{2,1,0:T(8,128)(2,1)S(1)} %collective-permute-done.got_a.core_a) | copy-start | bytes 884740
  14.5 0.7 copy-start.7
  24.1 26.3 %all-to-all-start = ((bf16[24,128,128]{2,1,0:T(8,128)(2,1)}), bf16[24,128,128]{2,1,0:T(8,128)(2,1)S(1)}, u32[]{:S(2)}, u32[]{:S(2)}) async-start(bf16[24,128,128]{2,1,0:T(8,128)(2,1)} %get-tuple-element.14), calls=%async_computation | async-start | bytes 1572864 | tf_op jit(solution)/shard_map/all_to_all | solution.py:416
  50.5 0.9 copy-start
  67.8 4.8 %copy-start.9 = (bf16[6,128,128]{2,1,0:T(8,128)(2,1)S(1)}, bf16[6,128,128]{2,1,0:T(8,128)(2,1)}, u32[]{:S(2)}) copy-start(bf16[6,128,128]{2,1,0:T(8,128)(2,1)} %get-tuple-element.16) | copy-start | bytes 589828
  67.8 5.6 %copy-start.8 = (bf16[6,128,128]{2,1,0:T(8,128)(2,1)S(1)}, bf16[6,128,128]{2,1,0:T(8,128)(2,1)}, u32[]{:S(2)}) copy-start(bf16[6,128,128]{2,1,0:T(8,128)(2,1)} %get-tuple-element.17) | copy-start | bytes 589828
  67.8 24.0 %all-to-all-start.1 = ((bf16[24,128,128]{2,1,0:T(8,128)(2,1)}), bf16[24,128,128]{2,1,0:T(8,128)(2,1)S(1)}, u32[]{:S(2)}, u32[]{:S(2)}) async-start(bf16[24,128,128]{2,1,0:T(8,128)(2,1)} %shard_map.88), calls=%async_computation.1 | async-start | bytes 1572864 | tf_op jit(solution)/shard_map/all_to_all | solution.py:428
  72.6 27.3 %collective-permute-start.2 = (bf16[6,128,128]{2,1,0:T(8,128)(2,1)S(1)}, bf16[6,128,128]{2,1,0:T(8,128)(2,1)S(1)}, u32[]{:S(2)}, u32[]{:S(2)}) collective-permute-start(bf16[6,128,128]{2,1,0:T(8,128)(2,1)S(1)} %copy-done.9), channel_id=1, source_target_pairs={{0,1},{1,0},{2,3},{3,2},{4,5},{5,4},{6,7},{7,6},{8,9},{9,8},{10,11... | collective-permute-start | bytes 589832 | tf_op jit(solution)/shard_map/ppermute | solution.py:349
  73.4 26.5 %collective-permute-start.3 = (bf16[6,128,128]{2,1,0:T(8,128)(2,1)S(1)}, bf16[6,128,128]{2,1,0:T(8,128)(2,1)S(1)}, u32[]{:S(2)}, u32[]{:S(2)}) collective-permute-start(bf16[6,128,128]{2,1,0:T(8,128)(2,1)S(1)} %copy-done.8), channel_id=1, source_target_pairs={{1,2},{2,1},{3,4},{4,3},{5,6},{6,5},{7,8},{8,7},{9,10},{10,9},{11,... | collective-permute-start | bytes 589832 | tf_op jit(solution)/shard_map/ppermute | solution.py:349
  91.9 0.9 copy-start.1
  95.9 4.0 %collective-permute-start.4 = (bf16[1,128,128]{2,1,0:T(8,128)(2,1)}, bf16[1,128,128]{2,1,0:T(8,128)(2,1)S(1)}, u32[]{:S(2)}, u32[]{:S(2)}) collective-permute-start(bf16[1,128,128]{2,1,0:T(8,128)(2,1)} %get-tuple-element.18), channel_id=1, source_target_pairs={{0,1},{1,0},{2,3},{3,2},{4,5},{5,4},{6,7},{7,6},{8,9},{9,8},{10,11... | collective-permute-start | bytes 98312 | tf_op jit(solution)/shard_map/ppermute | solution.py:349
  97.7 5.7 %collective-permute-start.5 = (bf16[1,128,128]{2,1,0:T(8,128)(2,1)}, bf16[1,128,128]{2,1,0:T(8,128)(2,1)S(1)}, u32[]{:S(2)}, u32[]{:S(2)}) collective-permute-start(bf16[1,128,128]{2,1,0:T(8,128)(2,1)} %get-tuple-element.19), channel_id=1, source_target_pairs={{1,2},{2,1},{3,4},{4,3},{5,6},{6,5},{7,8},{8,7},{9,10},{10,9},{11,... | collective-permute-start | bytes 98312 | tf_op jit(solution)/shard_map/ppermute | solution.py:349
  99.9 3.5 %copy-start.10 = (bf16[6,128,128]{2,1,0:T(8,128)(2,1)}, bf16[6,128,128]{2,1,0:T(8,128)(2,1)S(1)}, u32[]{:S(2)}) copy-start(bf16[6,128,128]{2,1,0:T(8,128)(2,1)S(1)} %collective-permute-done.2.half_a) | copy-start | bytes 589828
  99.9 3.5 %copy-start.11 = (bf16[6,128,128]{2,1,0:T(8,128)(2,1)}, bf16[6,128,128]{2,1,0:T(8,128)(2,1)S(1)}, u32[]{:S(2)}) copy-start(bf16[6,128,128]{2,1,0:T(8,128)(2,1)S(1)} %collective-permute-done.3.half_b) | copy-start | bytes 589828
  99.9 3.5 %copy-start.12 = (bf16[1,128,128]{2,1,0:T(8,128)(2,1)}, bf16[1,128,128]{2,1,0:T(8,128)(2,1)S(1)}, u32[]{:S(2)}) copy-start(bf16[1,128,128]{2,1,0:T(8,128)(2,1)S(1)} %collective-permute-done.4.diag_a) | copy-start | bytes 98308
  103.4 0.6 copy-start.13
where the time goes:
time: 113 us; the launch traced here: 112 us
  waiting for transfers between devices  43.7 us (39%)
  Pallas kernels  39.1 us (35%)
  starting transfers between devices  23.2 us (21%)
  local copies, waits for them, and re-layouts  3.29 us (3%)
  other arithmetic  2.27 us (2%)
    all_to_all x1, waiting for transfers between devices, shards(): lax.all_to_all(outgoing, 'row', split_axis=0, concat_axis=0, tiled=True)  18.8 us
    pallas_call x1, Pallas kernels, shards(): call(functools.partial(brick_kernel, bricks), jax.ShapeDtypeStruct((slots...  16.4 us
    all_to_all x1, waiting for transfers between devices, shards(): lax.all_to_all(returned, 'row', split_axis=0, concat_axis=0, tiled=True)  16.3 us
    pallas_call x1, Pallas kernels, shards(): call(functools.partial(first_kernel, count), (jax.ShapeDtypeStruct(densit...  8.89 us
    ppermute x3, starting transfers between devices, exchange(): lax.ppermute(send_b, axes, second)  8.72 us
    ppermute x3, waiting for transfers between devices, exchange(): lax.ppermute(send_b, axes, second)  8.65 us
    pallas_call x1, Pallas kernels, shards(): call(functools.partial(second_kernel, count), jax.ShapeDtypeStruct(densit...  8.46 us
    all_to_all x1, starting transfers between devices, shards(): lax.all_to_all(outgoing, 'row', split_axis=0, concat_axis=0, tiled=True)  7.03 us
  transfers between devices with their start and end apart: 8, of which 4 were waited for; matrix products, arithmetic and copies ran while one was open for 2% of the time, Pallas kernels for 3%

commit v1 on v0

v1 whole, which is shorter than its diff:
```python
import functools

import jax
import jax.numpy as jnp
from jax import lax
from jax.experimental import pallas as pl
from jax.experimental.pallas import tpu as pltpu
from jax.sharding import PartitionSpec as P

CAP = 3
HALF_STEP = 0.2
SECOND_ORDER = 0.5 * HALF_STEP * HALF_STEP
GRID_FACTOR = 0.1
F32 = jnp.float32
BF16 = jnp.bfloat16
PROP_FLOPS = 1 << 32
MIB = 1024 * 1024
TILE = 16


def call(kernel, out_shape, flops, vmem, scalars=0, grid=(), in_specs=None, out_specs=None, scratch=(), aliases={}):
    whole = pl.BlockSpec(memory_space=pltpu.VMEM)
    return pl.pallas_call(
        kernel,
        out_shape=out_shape,
        grid_spec=pltpu.PrefetchScalarGridSpec(
            num_scalar_prefetch=scalars,
            grid=grid,
            in_specs=in_specs,
            out_specs=jax.tree.map(lambda _: whole, out_shape) if out_specs is None else out_specs,
            scratch_shapes=scratch,
        ),
        input_output_aliases=aliases,
        compiler_params=pltpu.CompilerParams(vmem_limit_bytes=vmem * MIB),
        cost_estimate=pl.CostEstimate(flops=flops, bytes_accessed=4 << 20, transcendentals=0),
    )


def in_hbm(x):
    return pltpu.with_memory_space_constraint(x, pltpu.HBM)


def block_spec(shape, index):
    return pl.BlockSpec(shape, lambda *_: index)


def joined(re, im):
    return jnp.concatenate([re, im], axis=1)


def dagger(value):
    width = value.shape[0]
    re = value[:, :width].astype(F32).T
    im = value[:, width:].astype(F32).T
    return joined(re, -im).astype(BF16)


def as_right(value):
    width = value.shape[0]
    return jnp.concatenate([value, joined(-value[:, width:], value[:, :width])], axis=0)


def band_column(left, right, j, low, high):
    total = {}
    for mid in (j - 1, j, j + 1):
        rows = [i for i in range(max(mid, j) - 1, min(mid, j) + 2) if low <= i <= high]
        if not rows:
            continue
        stacked = jnp.concatenate([left(i, mid) for i in rows], axis=0)
        result = jnp.dot(stacked, as_right(right(mid, j)), preferred_element_type=F32)
        width = result.shape[0] // len(rows)
        for n, i in enumerate(rows):
            part = result[n * width : (n + 1) * width]
            total[i] = part if i not in total else total[i] + part
    return total


def times_i(value):
    width = value.shape[0]
    return joined(-value[:, width:], value[:, :width])


def taylor_first(columns, low, high, get_left, get_q, hp_ref):
    for j in columns:
        for i, value in band_column(get_left, get_q, j, low, high).items():
            hp_ref[i + 1, j - i + 1] = value.astype(BF16)


def propagate(low, high, get_q, get_hp, get_left, get_right, moved_ref, wh_ref, write):
    def get(ref):
        return lambda i, j: ref[i + 1, j - i + 1]

    columns = range(low - 1, high + 2)
    for j in columns:
        for i, value in band_column(get_left, get_hp, j, low, high).items():
            moved = get_q(i, j).astype(F32) - HALF_STEP * times_i(get_hp(i, j).astype(F32)) - SECOND_ORDER * value
            moved_ref[i + 1, j - i + 1] = moved.astype(BF16)
    for j in columns:
        for i, value in band_column(get(moved_ref), get_right, j, low, high).items():
            wh_ref[i + 1, j - i + 1] = value.astype(BF16)
    for j in columns:
        for i, value in band_column(get(wh_ref), get_right, j, low, high).items():
            moved = moved_ref[i + 1, j - i + 1].astype(F32)
            wh = wh_ref[i + 1, j - i + 1].astype(F32)
            write(i, j, (moved + HALF_STEP * times_i(wh) - SECOND_ORDER * value).astype(BF16))


def lanes_rows(shape):
    return lax.broadcasted_iota(jnp.int32, shape, 1), lax.broadcasted_iota(jnp.int32, shape, 0)


def pack_hermitian(re, im):
    lane, row = lanes_rows(re.shape)
    return jnp.where(row <= lane, re, im)


def unpack_hermitian(packed):
    lane, row = lanes_rows(packed.shape)
    packed = packed.astype(F32)
    turned = packed.T
    re = jnp.where(row <= lane, packed, turned)
    im = jnp.where(row > lane, packed, jnp.where(row < lane, -turned, 0.0))
    return joined(re, im).astype(BF16)


def pack_symmetric(block, folded):
    lane, row = lanes_rows(block.shape)
    half = block.shape[0] // 2
    both = jnp.where(lane == row, block, block + block.T) if folded else block
    lane, row = lanes_rows((half, block.shape[1]))
    packed = jnp.where(lane >= row, both[:half], pltpu.roll(both[half:], half, 1))
    diagonal = jnp.sum(jnp.where(lane == row + half, both[half:], 0.0), axis=0, keepdims=True)
    return packed, diagonal


def unpack_triangle(packed, diagonal):
    half, width = packed.shape
    lane, row = lanes_rows(packed.shape)
    top = jnp.where(lane >= row, packed, 0.0)
    below = jnp.where(lane < row + half, pltpu.roll(packed, half, 1), jnp.where(lane == row + half, diagonal, 0.0))
    return jnp.concatenate([top, jnp.where(lane < half, 0.0, below)], axis=0)


def symmetric(value):
    return 0.5 * (value + value.T)


def send_kernel(count, dens, core, grid_old, owners, send_a, send_b, place, sources, slots, bands, grids, sems):
    last = count - 1
    places = [(dens, last, 1), (dens, last - 1, 2), (core, last, 1), (core, last, 0),
              (dens, 0, 1), (dens, 1, 0), (core, 0, 1), (core, 0, 2)]
    copies = [
        pltpu.make_async_copy(ref.at[:, i, k], bands.at[n], sems.at[n]) for n, (ref, i, k) in enumerate(places)
    ]
    copies += [
        pltpu.make_async_copy(grid_old.at[i], grids.at[n], sems.at[8 + n]) for n, i in enumerate((last, 0))
    ]
    for copy in copies:
        copy.start()

    lane, _ = lanes_rows(owners.shape)
    source = owners[...] // count // lax.axis_size("col")
    slot = jnp.zeros(owners.shape, jnp.int32)
    for t in range(owners.shape[1] - 1):
        slot += jnp.where((lane > t) & (source == source[:, t : t + 1]), 1, 0)
    mine = jnp.where(source == lax.axis_index("row"), owners[...] % count, -1)
    table = jnp.zeros(owners.shape, jnp.int32)
    for n in range(CAP):
        table = jnp.where(lane == n, jnp.max(jnp.where(slot == n, mine, -1), axis=1, keepdims=True), table)
    place[...] = table
    sources[...] = source
    slots[...] = slot
    for copy in copies:
        copy.wait()

    def message(first, grid):
        h_re = (bands[first + 2, 0].astype(F32) + symmetric(grids[grid])).astype(BF16)
        return [pack_hermitian(bands[first, 0], bands[first, 1]), bands[first + 1, 0], bands[first + 1, 1],
                pack_hermitian(h_re, bands[first + 2, 1]), bands[first + 3, 0], bands[first + 3, 1]]

    right = message(0, 0)
    left = message(4, 1)
    even = lax.axis_index("col") % 2 == 0

    @pl.when(even)
    def _():
        for n, (x, y) in enumerate(zip(right, left)):
            send_a[n] = x
            send_b[n] = y

    @pl.when(jnp.logical_not(even))
    def _():
        for n, (x, y) in enumerate(zip(right, left)):
            send_a[n] = y
            send_b[n] = x


def halo_reader(got_a, got_b):
    even = lax.axis_index("col") % 2 == 0

    def low(n):
        return jnp.where(even, got_b[n], got_a[n])

    def high(n):
        return jnp.where(even, got_a[n], got_b[n])

    return low, high


def set_diagonals(rows, count, leads, absorption, diag_re, diag_im, left_ref, right_ref):
    width = left_ref.shape[1]
    lane, row = lanes_rows((width, width))
    first = (lax.axis_index("row") * lax.axis_size("col") + lax.axis_index("col")) * count
    for i in rows:
        re = diag_re(i)
        im = diag_im(i).astype(F32)
        gamma = jnp.float32(0.0)
        for n in range(leads.shape[0]):
            gamma += jnp.where(leads[n] == first + i, absorption[n], 0.0)
        shift = jnp.where(lane == row, gamma, 0.0)
        left_ref[i + 1] = joined(re, (im - shift).astype(BF16))
        right_ref[i + 1] = joined(re, (im + shift).astype(BF16))


def band_at(ref):
    return lambda i, j: joined(ref[0, i, j - i + 1], ref[1, i, j - i + 1])


def band_writer(ref):
    def write(i, j, value):
        width = value.shape[0]
        ref[0, i, j - i + 1] = value[:, :width]
        ref[1, i, j - i + 1] = value[:, width:]

    return write


def old_diagonals(rows, count, leads, absorption, core, grid_old, left_ref, right_ref, ends=None):
    width = core.shape[-1]

    def diag_re(i):
        if i == -1:
            return ends[0][:, :width]
        if i == count:
            return ends[1][:, :width]
        return (core[0, i, 1].astype(F32) + symmetric(grid_old[i])).astype(BF16)

    def diag_im(i):
        return ends[0][:, width:] if i == -1 else ends[1][:, width:] if i == count else core[1, i, 1]

    set_diagonals(rows, count, leads, absorption, diag_re, diag_im, left_ref, right_ref)


def new_diagonals(rows, count, leads, absorption, core, grid_term, left_ref, right_ref, ends=None, ends_re=None):
    width = core.shape[-1]

    def diag_re(i):
        if i == -1:
            return ends_re[0]
        if i == count:
            return ends_re[1]
        return (core[0, i, 1].astype(F32) + grid_term[i]).astype(BF16)

    def diag_im(i):
        return ends[0][:, width:] if i == -1 else ends[1][:, width:] if i == count else core[1, i, 1]

    set_diagonals(rows, count, leads, absorption, diag_re, diag_im, left_ref, right_ref)


def band_access(count, core, far_low, far_high, low_edge, high_edge, diag_ref):
    def get(i, j):
        if i == j:
            return diag_ref[i + 1]
        if i == -1:
            return far_low() if j == -2 else low_edge[...]
        if i == count:
            return far_high() if j == count + 1 else high_edge[...]
        return joined(core[0, i, j - i + 1], core[1, i, j - i + 1])

    return get


def first_inner_kernel(count, leads, absorption, dens, core, grid_old, hp_ref, half, moved_ref, wh_ref, left_ref, right_ref):
    old_diagonals(range(count), count, leads, absorption, core, grid_old, left_ref, right_ref)
    get_left = band_access(count, core, None, None, None, None, left_ref)
    get_right = band_access(count, core, None, None, None, None, right_ref)
    get_q = band_at(dens)

    def get_hp(i, j):
        return hp_ref[i + 1, j - i + 1]

    taylor_first(range(count), 1, count - 2, get_left, get_q, hp_ref)
    propagate(2, count - 3, get_q, get_hp, get_left, get_right, moved_ref, wh_ref, band_writer(half))


def first_outer_kernel(count, leads, absorption, place, dens, core, grid_old, got_a, got_b, hp_in, half_in,
                       half_out, outgoing, send_a_out, send_b_out,
                       hp_ref, moved_ref, wh_ref, left_ref, right_ref, edges, packed, diagonals, half, out_buf, send_a, send_b, sems):
    low, high = halo_reader(got_a, got_b)
    last = count - 1
    edges[0] = dagger(band_at(dens)(0, -1))
    edges[1] = dagger(band_at(dens)(last, count))
    edges[2] = dagger(band_at(core)(0, -1))
    edges[3] = dagger(band_at(core)(last, count))
    edges[4] = unpack_hermitian(low(0))
    edges[5] = unpack_hermitian(high(0))
    ends = unpack_hermitian(low(3)), unpack_hermitian(high(3))
    rows = [-1, 0, 1, 2, count - 3, count - 2, last, count]
    old_diagonals(rows, count, leads, absorption, core, grid_old, left_ref, right_ref, ends)
    half[:, 2 : count - 2] = half_in[:, 2 : count - 2]

    def get_q(i, j):
        if i == -2:
            return joined(low(1), low(2))
        if i == -1:
            return edges[4] if j == -1 else edges[0]
        if i == count:
            return edges[5] if j == count else edges[1]
        if i == count + 1:
            return joined(high(1), high(2))
        return band_at(dens)(i, j)

    def get_hp(i, j):
        ref = hp_in if 1 <= i <= count - 2 else hp_ref
        return ref[i + 1, j - i + 1]

    def far_low():
        return joined(low(4), low(5))

    def far_high():
        return joined(high(4), high(5))

    get_left = band_access(count, core, far_low, far_high, edges.at[2], edges.at[3], left_ref)
    get_right = band_access(count, core, far_low, far_high, edges.at[2], edges.at[3], right_ref)
    write = band_writer(half)
    taylor_first(range(-1, 2), -1, 0, get_left, get_q, hp_ref)
    taylor_first(range(last - 1, count + 1), last, count, get_left, get_q, hp_ref)
    propagate(0, 1, get_q, get_hp, get_left, get_right, moved_ref, wh_ref, write)
    propagate(last - 1, last, get_q, get_hp, get_left, get_right, moved_ref, wh_ref, write)
    copies = [pltpu.make_async_copy(half, half_out, sems.at[0])]
    copies[0].start()

    right = [(last, 1), (last, 2), (last - 1, 2)]
    left = [(0, 1), (0, 0), (1, 0)]

    def send(to_a, to_b):
        for n in range(3):
            for part in range(2):
                send_a[2 * n + part] = half[part, to_a[n][0], to_a[n][1]]
                send_b[2 * n + part] = half[part, to_b[n][0], to_b[n][1]]

    even = lax.axis_index("col") % 2 == 0

    @pl.when(even)
    def _():
        send(right, left)

    @pl.when(jnp.logical_not(even))
    def _():
        send(left, right)

    for source, target, n in ((send_a, send_a_out, 1), (send_b, send_b_out, 2)):
        copies.append(pltpu.make_async_copy(source, target, sems.at[n]))
        copies[-1].start()

    for i in range(count):
        top, diagonal = pack_symmetric(half[0, i, 1].astype(F32), True)
        packed[i] = top.astype(BF16)
        diagonals[i] = jnp.broadcast_to(diagonal, diagonals.shape[1:])

    height, width = packed.shape[1:]
    _, row = lanes_rows((TILE, width))

    def put(p, carry):
        tail = jnp.zeros((TILE, width), F32)
        for n in range(CAP):
            source = jnp.maximum(place[p, n], 0)
            out_buf[p, n * height : (n + 1) * height] = packed[source]
            tail = jnp.where(row == n, diagonals[source][:1], tail)
        out_buf[p, CAP * height :] = tail.astype(BF16)
        return carry

    lax.fori_loop(0, out_buf.shape[0], put, 0)
    copies.append(pltpu.make_async_copy(out_buf, outgoing, sems.at[3]))
    copies[-1].start()
    for copy in copies:
        copy.wait()


def brick_kernel(chunk, groups, sources, slots, far, incoming, returned, colloc, sems):
    bricks, points, width = colloc.shape
    own = lax.axis_index("row")
    scale = GRID_FACTOR * width / points
    height = width // 2
    tail = CAP * height
    _, tail_row = lanes_rows((TILE, width))

    loads = {
        start: pltpu.make_async_copy(far.at[pl.ds(start, size)], colloc.at[pl.ds(start, size)], sems.at[n])
        for n, (start, size) in enumerate(groups)
    }
    for load in loads.values():
        load.start()
    returned[...] = jnp.zeros_like(returned)

    def block(t):
        start = pl.multiple_of(slots[own, t] * height, height)
        diagonal = jnp.sum(
            jnp.where(tail_row == slots[own, t], incoming[sources[own, t], tail : tail + TILE].astype(F32), 0.0),
            axis=0,
            keepdims=True,
        )
        return unpack_triangle(incoming[sources[own, t], pl.ds(start, height)].astype(F32), diagonal)

    def put(t, result):
        start = pl.multiple_of(slots[own, t] * height, height)
        packed, diagonal = pack_symmetric(scale * result, False)
        returned[sources[own, t], pl.ds(start, height)] = packed.astype(BF16)
        old = returned[sources[own, t], tail : tail + TILE].astype(F32)
        returned[sources[own, t], tail : tail + TILE] = jnp.where(tail_row == slots[own, t], diagonal, old).astype(BF16)

    for t in range(0, bricks, 2):
        q0, q1 = block(t), block(t + 1)
        zero = jnp.zeros_like(q0)
        both = jnp.concatenate([joined(q0, zero), joined(zero, q1)], axis=0).astype(BF16)
        columns = []
        if t in loads:
            loads[t].wait()
        for g in range(0, points, chunk):
            turned = jnp.concatenate([colloc[t, g : g + chunk].T, colloc[t + 1, g : g + chunk].T], axis=0)
            wide = turned.astype(F32)
            projected = jnp.dot(both, turned, preferred_element_type=F32) * wide
            weighted = []
            for n in range(2):
                rows = slice(n * width, (n + 1) * width)
                dens = jnp.sum(projected[rows], axis=0, keepdims=True)
                potential = dens * lax.rsqrt(1.0 + dens * dens)
                weighted.append((potential * wide[rows]).astype(BF16))
            columns.append(jnp.concatenate(weighted, axis=0))
        result = jnp.dot(
            jnp.concatenate(columns, axis=1), joined(colloc[t], colloc[t + 1]), preferred_element_type=F32
        )
        put(t, result[:width, :width])
        put(t + 1, result[width:, width:])


def collect_kernel(count, place, arriving, core, grid_term, send_a, send_b, total, tails):
    width = arriving.shape[-1]
    height = width // 2
    total[...] = jnp.zeros_like(total)
    tails[...] = jnp.zeros_like(tails)

    def add(p, carry):
        last = arriving[p, CAP * height :].astype(F32)
        for n in range(CAP):
            at = place[p, n]

            @pl.when(at >= 0)
            def _():
                total[at] += arriving[p, n * height : (n + 1) * height].astype(F32)
                tails[at] += jnp.broadcast_to(last[n : n + 1], tails.shape[1:])

        return carry

    lax.fori_loop(0, arriving.shape[0], add, 0)
    lane, row = lanes_rows((width, width))
    for i in range(count):
        triangle = unpack_triangle(total[i], tails[i][:1])
        grid_term[i] = jnp.where(lane == row, triangle, triangle + triangle.T)
    right = (core[0, count - 1, 0].astype(F32) + grid_term[count - 1]).astype(BF16)
    left = (core[0, 0, 0].astype(F32) + grid_term[0]).astype(BF16)
    even = lax.axis_index("col") % 2 == 0
    send_a[0] = jnp.where(even, right, left)
    send_b[0] = jnp.where(even, left, right)


def half_access(count, half, half_a, half_b):
    low, high = halo_reader(half_a, half_b)

    def get_q(i, j):
        if i < 0:
            n = 0 if i == -1 and j == -1 else 2 if i == -1 else 4
            return joined(low(n), low(n + 1))
        if i >= count:
            n = 0 if i == count and j == count else 2 if i == count else 4
            return joined(high(n), high(n + 1))
        return band_at(half)(i, j)

    return get_q


def second_inner_kernel(count, leads, absorption, half, core, grid_term, half_a, half_b,
                        out, hp_ref, moved_ref, wh_ref, left_ref, right_ref):
    new_diagonals(range(count), count, leads, absorption, core, grid_term, left_ref, right_ref)
    get_left = band_access(count, core, None, None, None, None, left_ref)
    get_right = band_access(count, core, None, None, None, None, right_ref)
    get_q = half_access(count, half, half_a, half_b)

    def get_hp(i, j):
        return hp_ref[i + 1, j - i + 1]

    taylor_first(range(-1, count + 1), 0, count - 1, get_left, get_q, hp_ref)
    propagate(1, count - 2, get_q, get_hp, get_left, get_right, moved_ref, wh_ref, band_writer(out))


def second_outer_kernel(count, leads, absorption, half, core, grid_term, core_a, core_b, half_a, half_b, diag_a, diag_b,
                        hp_in, out_in, out, hp_ref, moved_ref, wh_ref, left_ref, right_ref, edges, ready, sems):
    core_low, core_high = halo_reader(core_a, core_b)
    diag_low, diag_high = halo_reader(diag_a, diag_b)
    last = count - 1
    edges[0] = dagger(band_at(core)(0, -1))
    edges[1] = dagger(band_at(core)(last, count))
    ends = unpack_hermitian(core_low(3)), unpack_hermitian(core_high(3))
    rows = [-1, 0, 1, count - 2, last, count]
    new_diagonals(rows, count, leads, absorption, core, grid_term, left_ref, right_ref, ends, (diag_low(0), diag_high(0)))
    get_q = half_access(count, half, half_a, half_b)

    def far_low():
        return joined(core_low(4), core_low(5))

    def far_high():
        return joined(core_high(4), core_high(5))

    get_left = band_access(count, core, far_low, far_high, edges.at[0], edges.at[1], left_ref)
    get_right = band_access(count, core, far_low, far_high, edges.at[0], edges.at[1], right_ref)

    def get_hp(i, j):
        ref = hp_in if 0 <= i < count else hp_ref
        return ref[i + 1, j - i + 1]

    def write(i, j, value):
        width = value.shape[0]
        n = 0 if i == 0 else 1
        ready[0, n, j - i + 1] = value[:, :width]
        ready[1, n, j - i + 1] = value[:, width:]

    taylor_first(range(-1, 1), -1, -1, get_left, get_q, hp_ref)
    taylor_first(range(last, count + 1), count, count, get_left, get_q, hp_ref)
    copies = []
    for n, i in enumerate((0, last)):
        propagate(i, i, get_q, get_hp, get_left, get_right, moved_ref, wh_ref, write)
        copies.append(pltpu.make_async_copy(ready.at[:, n], out.at[:, i], sems.at[n]))
        copies[-1].start()
    for copy in copies:
        copy.wait()


def exchange(send_a, send_b, total):
    first = [(i, i ^ 1) for i in range(total)]
    second = [(i, i + 1) if i % 2 else (i, i - 1) for i in range(1, total - 1)]
    axes = ("row", "col")
    return lax.ppermute(send_a, axes, first), lax.ppermute(send_b, axes, second)


def shards(density, core, grid_old, lead_blocks, absorption, collocation, brick_block):
    count = density.shape[1]
    width = density.shape[-1]
    row_size = lax.axis_size("row")
    total = row_size * lax.axis_size("col")
    bricks = brick_block.shape[1]
    vmem = pl.BlockSpec(memory_space=pltpu.VMEM)
    hbm = pl.BlockSpec(memory_space=pltpu.HBM)

    message = jax.ShapeDtypeStruct((6, width, width), BF16)
    table = jax.ShapeDtypeStruct(brick_block.shape, jnp.int32)
    send_a, send_b, place, sources, slots = call(
        functools.partial(send_kernel, count),
        (message, message, table, table, table),
        flops=1 << 20,
        vmem=8,
        in_specs=[hbm] * 3 + [vmem],
        scratch=[
            pltpu.VMEM((8, 2, width, width), BF16),
            pltpu.VMEM((2, width, width), F32),
            pltpu.SemaphoreType.DMA((10,)),
        ],
    )(*(in_hbm(x) for x in (density, core, grid_old)), brick_block)
    got_a, got_b = exchange(send_a, send_b, total)

    def band_scratch(rows):
        return pltpu.VMEM((rows, 3, width, 2 * width), BF16)

    def sides(n):
        return pltpu.VMEM((n, width, 2 * width), BF16)

    hp_shape = jax.ShapeDtypeStruct((count + 2, 3, width, 2 * width), BF16)
    inner_scratch = [band_scratch(count + 2)] * 2 + [sides(count + 2)] * 2
    outer_scratch = [band_scratch(count + 2)] * 3 + [sides(count + 2)] * 2
    hp, half_inner = call(
        functools.partial(first_inner_kernel, count),
        (hp_shape, jax.ShapeDtypeStruct(density.shape, BF16)),
        flops=PROP_FLOPS,
        vmem=16,
        scalars=2,
        in_specs=[vmem] * 3,
        scratch=inner_scratch,
    )(lead_blocks, absorption, density, core, grid_old)
    packed_rows = CAP * width // 2 + TILE
    packed_shape = jax.ShapeDtypeStruct((row_size, packed_rows, width), BF16)
    half_message = pltpu.HBM((6, width, width), BF16)
    half, outgoing, send_a, send_b = call(
        functools.partial(first_outer_kernel, count),
        (
            pltpu.HBM(density.shape, BF16),
            pltpu.HBM(packed_shape.shape, BF16),
            half_message,
            half_message,
        ),
        flops=PROP_FLOPS,
        vmem=20,
        scalars=3,
        in_specs=[vmem] * 7,
        scratch=outer_scratch
        + [
            pltpu.VMEM((6, width, 2 * width), BF16),
            pltpu.VMEM((count, width // 2, width), BF16),
            pltpu.VMEM((count, 8, width), F32),
            pltpu.VMEM(density.shape, BF16),
            pltpu.VMEM(packed_shape.shape, BF16),
            pltpu.VMEM(half_message.shape, BF16),
            pltpu.VMEM(half_message.shape, BF16),
            pltpu.SemaphoreType.DMA((4,)),
        ],
        out_specs=(hbm,) * 4,
    )(lead_blocks, absorption, place, density, core, grid_old, got_a, got_b, hp, half_inner)

    incoming = lax.all_to_all(outgoing, "row", split_axis=0, concat_axis=0, tiled=True)
    half_a, half_b = exchange(send_a, send_b, total)

    points = collocation.shape[1]
    ends = [0, bricks // 6, bricks // 2, bricks]
    groups = [(a, b - a) for a, b in zip(ends, ends[1:])]
    returned = call(
        functools.partial(brick_kernel, points // 4, groups),
        packed_shape,
        flops=4 * bricks * points * width**2,
        vmem=20,
        scalars=2,
        in_specs=[hbm, vmem],
        scratch=[pltpu.VMEM(collocation.shape, BF16), pltpu.SemaphoreType.DMA((3,))],
    )(sources, slots, in_hbm(collocation), incoming)
    arriving = lax.all_to_all(returned, "row", split_axis=0, concat_axis=0, tiled=True)

    diag_message = jax.ShapeDtypeStruct((1, width, width), BF16)
    grid_term, send_a, send_b = call(
        functools.partial(collect_kernel, count),
        (jax.ShapeDtypeStruct((count, width, width), F32), diag_message, diag_message),
        flops=1 << 20,
        vmem=8,
        scalars=1,
        grid=(1,),
        in_specs=[vmem, block_spec((1, count, 1, width, width), (0, 0, 1, 0, 0))],
        scratch=[pltpu.VMEM((count, width // 2, width), F32), pltpu.VMEM((count, 8, width), F32)],
    )(place, arriving, core)
    diag_a, diag_b = exchange(send_a, send_b, total)

    inner, hp = call(
        functools.partial(second_inner_kernel, count),
        (jax.ShapeDtypeStruct(density.shape, BF16), hp_shape),
        flops=PROP_FLOPS,
        vmem=16,
        scalars=2,
        in_specs=[vmem] * 5,
        scratch=inner_scratch,
    )(lead_blocks, absorption, half, core, grid_term, half_a, half_b)
    density_next = call(
        functools.partial(second_outer_kernel, count),
        pltpu.HBM(density.shape, BF16),
        flops=PROP_FLOPS,
        vmem=16,
        scalars=2,
        in_specs=[vmem] * 10 + [hbm],
        out_specs=hbm,
        scratch=outer_scratch + [sides(2), pltpu.VMEM((2, 2, 3, width, width), BF16), pltpu.SemaphoreType.DMA((2,))],
        aliases={12: 0},
    )(lead_blocks, absorption, half, core, grid_term, got_a, got_b, half_a, half_b, diag_a, diag_b, hp, in_hbm(inner))
    return (density_next, grid_term)


def solution(mesh):
    band = P(None, ("row", "col"), None, None, None)
    blocks = P(("row", "col"), None, None)
    return jax.shard_map(
        shards,
        mesh=mesh,
        in_specs=(band, band, blocks, P(), P(), blocks, P(None, "col")),
        out_specs=(band, blocks),
        check_vma=False,
    )
```

time: 113 us -> 78.8 us (0.70)
  waiting for transfers between devices: 43.7 us -> 7.27 us
  blocking collectives: 0 us -> 19.1 us
  Pallas kernels: 39.1 us -> 30.4 us
  starting transfers between devices: 23.2 us -> 18.7 us
  other arithmetic: 2.27 us -> 0 us
  local copies, waits for them, and re-layouts: 3.29 us -> 1.9 us
    all_to_all x0 -> x1, blocking collectives: none -> 19.1 us  [shards(): lax.all_to_all(outgoing, 'row', split_axis=0, concat_axis=0, tiled=True)]
    all_to_all x1 -> x0, waiting for transfers between devices: 18.8 us -> none  [shards(): lax.all_to_all(outgoing, 'row', split_axis=0, concat_axis=0, tiled=True)]
    all_to_all x1, waiting for transfers between devices: 16.3 us -> 5.85 us  [shards(): lax.all_to_all(returned, 'row', split_axis=0, concat_axis=0, tiled=True)]
    pallas_call x4 -> x6, Pallas kernels: 36 us -> 28.5 us  [the longest x1 11.1 us: shards(): call(functools.partial(brick_kernel, points // 4, groups), packed_shape,...]
    ppermute x3, waiting for transfers between devices: 8.65 us -> 1.42 us  [exchange(): lax.ppermute(send_b, axes, second)]
    all_to_all x1 -> x0, starting transfers between devices: 7.03 us -> none  [shards(): lax.all_to_all(outgoing, 'row', split_axis=0, concat_axis=0, tiled=True)]
    ppermute x3, starting transfers between devices: 2.73 us -> 5.5 us  [exchange(): lax.ppermute(send_a, axes, first)]
    unnamed x28 -> x22, local copies, waits for them, and re-layouts: 3.12 us -> 1.9 us
  transfers between devices with their start and end apart: 8 -> 7, of which waited for: 4 -> 2; matrix products, arithmetic and copies ran while one was open for 2% -> 0% of each run, Pallas kernels for 3% -> 13%
where the time goes in v1:
time: 78.8 us; the launch traced here: 78.4 us
  Pallas kernels  30.4 us (39%)
  blocking collectives  19.1 us (24%)
  starting transfers between devices  18.7 us (24%)
  waiting for transfers between devices  7.27 us (9%)
  local copies, waits for them, and re-layouts  1.9 us (2%)
  between operations  0.99 us (1%)
    all_to_all x1, blocking collectives, shards(): lax.all_to_all(outgoing, 'row', split_axis=0, concat_axis=0, tiled=True)  19.1 us
    pallas_call x1, Pallas kernels, shards(): call(functools.partial(brick_kernel, points // 4, groups), packed_shape,...  11.1 us
    ppermute x3, starting transfers between devices, exchange(): lax.ppermute(send_b, axes, second)  9.18 us
    all_to_all x1, waiting for transfers between devices, shards(): lax.all_to_all(returned, 'row', split_axis=0, concat_axis=0, tiled=True)  5.85 us
    ppermute x3, starting transfers between devices, exchange(): lax.ppermute(send_a, axes, first)  5.5 us
    pallas_call x1, Pallas kernels, shards(): call(functools.partial(second_inner_kernel, count), (jax.ShapeDtypeStruct...  5.22 us
    pallas_call x1, Pallas kernels, shards(): call(functools.partial(first_outer_kernel, count), (pltpu.HBM(density.sha...  4.42 us
    all_to_all x1, starting transfers between devices, shards(): lax.all_to_all(returned, 'row', split_axis=0, concat_axis=0, tiled=True)  4.02 us
  transfers between devices with their start and end apart: 7, of which 2 were waited for; matrix products, arithmetic and copies ran while one was open for 0% of the time, Pallas kernels for 13%

profile of v1, /device:TPU:1, one launch (start us, length us, event | category | flops | bytes accessed | tf_op | source)
XLA Modules:
  0.0 78.4 jit_solution(8143628723405135857)
XLA Ops:
  0.6 0.0 copy-start
  0.6 0.0 copy-start.2
  0.7 0.0 copy-start.1
  0.7 0.0 copy-start.3
  0.7 0.8 %copy-done.3 = s32[8,24]{1,0:T(8,128)S(1)} copy-done((s32[8,24]{1,0:T(8,128)S(1)}, s32[8,24]{1,0:T(8,128)}, u32[]{:S(2)}) %copy-start.3) | copy-done | bytes 792
  1.5 0.0 copy-start.6
  1.5 0.0 copy-start.7
  1.5 1.7 %shard_map.86 = (bf16[6,128,128]{2,1,0:T(8,128)(2,1)S(1)}, bf16[6,128,128]{2,1,0:T(8,128)(2,1)S(1)}, s32[8,24]{1,0:T(8,128)S(1)}, s32[8,24]{1,0:T(8,128)S(1)}, s32[8,24]{1,0:T(8,128)S(1)}) custom-call(bf16[2,8,3,128,128]{4,3,2,1,0:T(8,128)(2,1)} %dens.5, bf16[2,8,3,128,128]{4,3,2,1,0:T(8,128)(2,1)} %core.11, f32[8,128,128]{2,1,0:T(8,128)} %grid_old.5, ...), custom_call_target="tpu_custom_call" | custom-call | flops 1048576 | bytes 4194304 | tf_op jit(solution)/shard_map/pallas_call | solution.py:566
  3.2 0.1 collective-permute-start
  3.3 4.5 %collective-permute-start.1 = (bf16[6,128,128]{2,1,0:T(8,128)(2,1)S(1)}, bf16[6,128,128]{2,1,0:T(8,128)(2,1)S(1)}, u32[]{:S(2)}, u32[]{:S(2)}) collective-permute-start(bf16[6,128,128]{2,1,0:T(8,128)(2,1)S(1)} %get-tuple-element.20), channel_id=1, source_target_pairs={{1,2},{2,1},{3,4},{4,3},{5,6},{6,5},{7,8},{8,7},{9,10},{10,9},{11,... | collective-permute-start | bytes 589832 | tf_op jit(solution)/shard_map/ppermute | solution.py:552
  7.8 0.0 copy-done
  7.8 0.0 copy-done.2
  7.8 0.0 copy-done.1
  7.8 0.0 copy-done.6
  7.8 0.0 copy-done.7
  7.8 3.1 %shard_map.87 = (bf16[10,3,128,256]{3,2,1,0:T(8,128)(2,1)S(1)}, bf16[2,8,3,128,128]{4,3,2,1,0:T(8,128)(2,1)S(1)}) custom-call(s32[8]{0:T(128)S(1)} %copy-done.6, f32[8]{0:T(128)S(1)} %copy-done.7, bf16[2,8,3,128,128]{4,3,2,1,0:T(8,128)(2,1)S(1)} %copy-done.1, bf16[2,8,3,128,128]{4,3,2,1,0:T(8,128)(2,1)S(1)} %copy-done, f32[8,128,128]{2,1,0:T(8,128)S(1)} %copy-done.2), custom_call_target="tpu_custom_call" | custom-call | flops 4294967296 | bytes 4194304 | tf_op jit(solution)/shard_map/pallas_call | solution.py:589
  10.9 0.0 collective-permute-done.got_a.core_a
  10.9 1.4 %collective-permute-done.1.got_b.core_b = bf16[6,128,128]{2,1,0:T(8,128)(2,1)S(1)} collective-permute-done((bf16[6,128,128]{2,1,0:T(8,128)(2,1)S(1)}, bf16[6,128,128]{2,1,0:T(8,128)(2,1)S(1)}, u32[]{:S(2)}, u32[]{:S(2)}) %collective-permute-start.1) | collective-permute-done | bytes 196640 | tf_op jit(solution)/shard_map/ppermute | solution.py:552
  12.3 4.4 %shard_map.88 = (bf16[2,8,3,128,128]{4,3,2,1,0:T(8,128)(2,1)}, bf16[8,208,128]{2,1,0:T(8,128)(2,1)}, bf16[6,128,128]{2,1,0:T(8,128)(2,1)}, bf16[6,128,128]{2,1,0:T(8,128)(2,1)}) custom-call(s32[8]{0:T(128)S(1)} %copy-done.6, f32[8]{0:T(128)S(1)} %copy-done.7, s32[8,24]{1,0:T(8,128)S(1)} %get-tuple-element.18.place, ...), custom_call_target="tpu_custom_call" | custom-call | flops 4294967296 | bytes 4194304 | tf_op jit(solution)/shard_map/pallas_call | solution.py:601
  16.8 19.1 %all_to_all.10.incoming = bf16[8,208,128]{2,1,0:T(8,128)(2,1)S(1)} all-to-all(bf16[8,208,128]{2,1,0:T(8,128)(2,1)} %get-tuple-element.26), channel_id=1, replica_groups=mesh['row'=8,'col'=4] {'row'}, dimensions={0} | all-to-all | bytes 851968 | tf_op jit(solution)/shard_map/all_to_all | solution.py:627
  35.8 0.0 copy-start.10
  35.8 0.0 copy-start.9
  35.8 11.1 %shard_map.89 = bf16[8,208,128]{2,1,0:T(8,128)(2,1)} custom-call(s32[8,24]{1,0:T(8,128)S(1)} %get-tuple-element.24.sources, s32[8,24]{1,0:T(8,128)S(1)} %get-tuple-element.25.slots, bf16[24,2048,128]{2,1,0:T(8,128)(2,1)} %far.1, bf16[8,208,128]{2,1,0:T(8,128)(2,1)S(1)} %all_to_all.10.incoming), custom_call_target="tpu_custom_call" | custom-call | flops 3221225472 | bytes 4194304 | tf_op jit(solution)/shard_map/pallas_call | solution.py:633
  47.0 4.0 %all-to-all-start.1 = ((bf16[8,208,128]{2,1,0:T(8,128)(2,1)}), bf16[8,208,128]{2,1,0:T(8,128)(2,1)S(1)}, u32[]{:S(2)}, u32[]{:S(2)}) async-start(bf16[8,208,128]{2,1,0:T(8,128)(2,1)} %shard_map.89), calls=%async_computation.1 | async-start | bytes 851968 | tf_op jit(solution)/shard_map/all_to_all | solution.py:642
  51.0 0.0 copy-done.10
  51.0 1.3 %collective-permute-start.2 = (bf16[6,128,128]{2,1,0:T(8,128)(2,1)S(1)}, bf16[6,128,128]{2,1,0:T(8,128)(2,1)S(1)}, u32[]{:S(2)}, u32[]{:S(2)}) collective-permute-start(bf16[6,128,128]{2,1,0:T(8,128)(2,1)S(1)} %copy-done.10), channel_id=1, source_target_pairs={{0,1},{1,0},{2,3},{3,2},{4,5},{5,4},{6,7},{7,6},{8,9},{9,8},{10,11... | collective-permute-start | bytes 589832 | tf_op jit(solution)/shard_map/ppermute | solution.py:552
  52.3 0.0 copy-done.9
  52.3 2.1 %collective-permute-start.3 = (bf16[6,128,128]{2,1,0:T(8,128)(2,1)S(1)}, bf16[6,128,128]{2,1,0:T(8,128)(2,1)S(1)}, u32[]{:S(2)}, u32[]{:S(2)}) collective-permute-start(bf16[6,128,128]{2,1,0:T(8,128)(2,1)S(1)} %copy-done.9), channel_id=1, source_target_pairs={{1,2},{2,1},{3,4},{4,3},{5,6},{6,5},{7,8},{8,7},{9,10},{10,9},{11,... | collective-permute-start | bytes 589832 | tf_op jit(solution)/shard_map/ppermute | solution.py:552
  54.5 5.8 %all-to-all-done.1.arriving = bf16[8,208,128]{2,1,0:T(8,128)(2,1)S(1)} async-done(((bf16[8,208,128]{2,1,0:T(8,128)(2,1)}), bf16[8,208,128]{2,1,0:T(8,128)(2,1)S(1)}, u32[]{:S(2)}, u32[]{:S(2)}) %all-to-all-start.1) | async-done | bytes 426016 | tf_op jit(solution)/shard_map/all_to_all | solution.py:642
  60.3 0.0 copy-start.8
  60.3 2.0 %shard_map.90 = (f32[8,128,128]{2,1,0:T(8,128)}, bf16[1,128,128]{2,1,0:T(8,128)(2,1)S(1)}, bf16[1,128,128]{2,1,0:T(8,128)(2,1)S(1)}) custom-call(s32[8,24]{1,0:T(8,128)S(1)} %get-tuple-element.18.place, bf16[8,208,128]{2,1,0:T(8,128)(2,1)S(1)} %all-to-all-done.1.arriving, bf16[2,8,3,128,128]{4,3,2,1,0:T(8,128)(2,1)S(1)} %copy-done), custom_call_target="tpu_custom_call" | custom-call | flops 1048576 | bytes 4194304 | tf_op jit(solution)/shard_map/pallas_call | solution.py:645
  62.3 4.1 %collective-permute-start.4 = (bf16[1,128,128]{2,1,0:T(8,128)(2,1)S(1)}, bf16[1,128,128]{2,1,0:T(8,128)(2,1)S(1)}, u32[]{:S(2)}, u32[]{:S(2)}) collective-permute-start(bf16[1,128,128]{2,1,0:T(8,128)(2,1)S(1)} %get-tuple-element.30), channel_id=1, source_target_pairs={{0,1},{1,0},{2,3},{3,2},{4,5},{5,4},{6,7},{7,6},{8,9},{9,8},{10,11... | collective-permute-start | bytes 98312 | tf_op jit(solution)/shard_map/ppermute | solution.py:552
  66.4 2.6 %collective-permute-start.5 = (bf16[1,128,128]{2,1,0:T(8,128)(2,1)S(1)}, bf16[1,128,128]{2,1,0:T(8,128)(2,1)S(1)}, u32[]{:S(2)}, u32[]{:S(2)}) collective-permute-start(bf16[1,128,128]{2,1,0:T(8,128)(2,1)S(1)} %get-tuple-element.31), channel_id=1, source_target_pairs={{1,2},{2,1},{3,4},{4,3},{5,6},{6,5},{7,8},{8,7},{9,10},{10,9},{11,... | collective-permute-start | bytes 98312 | tf_op jit(solution)/shard_map/ppermute | solution.py:552
  69.0 0.0 collective-permute-done.2.half_a
  69.0 0.0 collective-permute-done.3.half_b
  69.0 0.0 copy-done.8
  69.0 0.0 copy-start.4
  69.0 1.0 %copy-done.4 = f32[8,128,128]{2,1,0:T(8,128)S(1)} copy-done((f32[8,128,128]{2,1,0:T(8,128)S(1)}, f32[8,128,128]{2,1,0:T(8,128)}, u32[]{:S(2)}) %copy-start.4) | copy-done | bytes 524312
  70.1 0.0 copy-start.5
  70.1 5.2 %shard_map.91 = (bf16[2,8,3,128,128]{4,3,2,1,0:T(8,128)(2,1)}, bf16[10,3,128,256]{3,2,1,0:T(8,128)(2,1)S(1)}) custom-call(s32[8]{0:T(128)S(1)} %copy-done.6, f32[8]{0:T(128)S(1)} %copy-done.7, bf16[2,8,3,128,128]{4,3,2,1,0:T(8,128)(2,1)S(1)} %copy-done.8, bf16[2,8,3,128,128]{4,3,2,1,0:T(8,128)(2,1)S(1)} %copy-done, f32[8,128,128]{2,1,0:T(8,128)S(1)} %copy-done.4, ...), custom_call_target="tpu_custom_call" | custom-call | flops 4294967296 | bytes 4194304 | tf_op jit(solution)/shard_map/pallas_call | solution.py:657
  75.3 0.0 collective-permute-done.4.diag_a
  75.3 0.0 collective-permute-done.5.diag_b
  75.3 0.0 copy-done.5
  75.3 2.9 %shard_map.92 = bf16[2,8,3,128,128]{4,3,2,1,0:T(8,128)(2,1)} custom-call(s32[8]{0:T(128)S(1)} %copy-done.6, f32[8]{0:T(128)S(1)} %copy-done.7, bf16[2,8,3,128,128]{4,3,2,1,0:T(8,128)(2,1)S(1)} %copy-done.8, bf16[2,8,3,128,128]{4,3,2,1,0:T(8,128)(2,1)S(1)} %copy-done, f32[8,128,128]{2,1,0:T(8,128)S(1)} %copy-done.5, ...), custom_call_target="tpu_custom_call", output_to_operand_aliasing={{}: (12, {})} | custom-call | flops 4294967296 | bytes 4194304 | tf_op jit(solution)/shard_map/pallas_call | solution.py:666
Async XLA Ops:
  0.6 7.1 %copy-start = (bf16[2,8,3,128,128]{4,3,2,1,0:T(8,128)(2,1)S(1)}, bf16[2,8,3,128,128]{4,3,2,1,0:T(8,128)(2,1)}, u32[]{:S(2)}) copy-start(bf16[2,8,3,128,128]{4,3,2,1,0:T(8,128)(2,1)} %core.11) | copy-start | bytes 4718596
  0.6 7.1 %copy-start.2 = (f32[8,128,128]{2,1,0:T(8,128)S(1)}, f32[8,128,128]{2,1,0:T(8,128)}, u32[]{:S(2)}) copy-start(f32[8,128,128]{2,1,0:T(8,128)} %grid_old.5) | copy-start | bytes 1572868
  0.7 7.1 %copy-start.1 = (bf16[2,8,3,128,128]{4,3,2,1,0:T(8,128)(2,1)S(1)}, bf16[2,8,3,128,128]{4,3,2,1,0:T(8,128)(2,1)}, u32[]{:S(2)}) copy-start(bf16[2,8,3,128,128]{4,3,2,1,0:T(8,128)(2,1)} %dens.5) | copy-start | bytes 4718596
  0.7 0.8 %copy-start.3 = (s32[8,24]{1,0:T(8,128)S(1)}, s32[8,24]{1,0:T(8,128)}, u32[]{:S(2)}) copy-start(s32[8,24]{1,0:T(8,128)} %owners.1) | copy-start | bytes 2308
  1.5 6.3 %copy-start.6 = (s32[8]{0:T(128)S(1)}, s32[8]{0:T(128)}, u32[]{:S(2)}) copy-start(s32[8]{0:T(128)} %leads.7) | copy-start | bytes 100
  1.5 6.3 %copy-start.7 = (f32[8]{0:T(128)S(1)}, f32[8]{0:T(128)}, u32[]{:S(2)}) copy-start(f32[8]{0:T(128)} %absorption.7) | copy-start | bytes 100
  3.2 7.7 %collective-permute-start = (bf16[6,128,128]{2,1,0:T(8,128)(2,1)S(1)}, bf16[6,128,128]{2,1,0:T(8,128)(2,1)S(1)}, u32[]{:S(2)}, u32[]{:S(2)}) collective-permute-start(bf16[6,128,128]{2,1,0:T(8,128)(2,1)S(1)} %get-tuple-element.19), channel_id=1, source_target_pairs={{0,1},{1,0},{2,3},{3,2},{4,5},{5,4},{6,7},{7,6},{8,9},{9,8},{10,11... | collective-permute-start | bytes 589832 | tf_op jit(solution)/shard_map/ppermute | solution.py:552
  3.3 9.0 %collective-permute-start.1 = (bf16[6,128,128]{2,1,0:T(8,128)(2,1)S(1)}, bf16[6,128,128]{2,1,0:T(8,128)(2,1)S(1)}, u32[]{:S(2)}, u32[]{:S(2)}) collective-permute-start(bf16[6,128,128]{2,1,0:T(8,128)(2,1)S(1)} %get-tuple-element.20), channel_id=1, source_target_pairs={{1,2},{2,1},{3,4},{4,3},{5,6},{6,5},{7,8},{8,7},{9,10},{10,9},{11,... | collective-permute-start | bytes 589832 | tf_op jit(solution)/shard_map/ppermute | solution.py:552
  35.8 15.2 %copy-start.10 = (bf16[6,128,128]{2,1,0:T(8,128)(2,1)S(1)}, bf16[6,128,128]{2,1,0:T(8,128)(2,1)}, u32[]{:S(2)}) copy-start(bf16[6,128,128]{2,1,0:T(8,128)(2,1)} %get-tuple-element.28) | copy-start | bytes 589828
  35.8 16.5 %copy-start.9 = (bf16[6,128,128]{2,1,0:T(8,128)(2,1)S(1)}, bf16[6,128,128]{2,1,0:T(8,128)(2,1)}, u32[]{:S(2)}) copy-start(bf16[6,128,128]{2,1,0:T(8,128)(2,1)} %get-tuple-element.29) | copy-start | bytes 589828
  47.0 13.3 %all-to-all-start.1 = ((bf16[8,208,128]{2,1,0:T(8,128)(2,1)}), bf16[8,208,128]{2,1,0:T(8,128)(2,1)S(1)}, u32[]{:S(2)}, u32[]{:S(2)}) async-start(bf16[8,208,128]{2,1,0:T(8,128)(2,1)} %shard_map.89), calls=%async_computation.1 | async-start | bytes 851968 | tf_op jit(solution)/shard_map/all_to_all | solution.py:642
  51.0 18.0 %collective-permute-start.2 = (bf16[6,128,128]{2,1,0:T(8,128)(2,1)S(1)}, bf16[6,128,128]{2,1,0:T(8,128)(2,1)S(1)}, u32[]{:S(2)}, u32[]{:S(2)}) collective-permute-start(bf16[6,128,128]{2,1,0:T(8,128)(2,1)S(1)} %copy-done.10), channel_id=1, source_target_pairs={{0,1},{1,0},{2,3},{3,2},{4,5},{5,4},{6,7},{7,6},{8,9},{9,8},{10,11... | collective-permute-start | bytes 589832 | tf_op jit(solution)/shard_map/ppermute | solution.py:552
  52.3 16.7 %collective-permute-start.3 = (bf16[6,128,128]{2,1,0:T(8,128)(2,1)S(1)}, bf16[6,128,128]{2,1,0:T(8,128)(2,1)S(1)}, u32[]{:S(2)}, u32[]{:S(2)}) collective-permute-start(bf16[6,128,128]{2,1,0:T(8,128)(2,1)S(1)} %copy-done.9), channel_id=1, source_target_pairs={{1,2},{2,1},{3,4},{4,3},{5,6},{6,5},{7,8},{8,7},{9,10},{10,9},{11,... | collective-permute-start | bytes 589832 | tf_op jit(solution)/shard_map/ppermute | solution.py:552
  60.3 8.7 %copy-start.8 = (bf16[2,8,3,128,128]{4,3,2,1,0:T(8,128)(2,1)S(1)}, bf16[2,8,3,128,128]{4,3,2,1,0:T(8,128)(2,1)}, u32[]{:S(2)}) copy-start(bf16[2,8,3,128,128]{4,3,2,1,0:T(8,128)(2,1)} %get-tuple-element.23.half) | copy-start | bytes 4718596
  62.3 13.0 %collective-permute-start.4 = (bf16[1,128,128]{2,1,0:T(8,128)(2,1)S(1)}, bf16[1,128,128]{2,1,0:T(8,128)(2,1)S(1)}, u32[]{:S(2)}, u32[]{:S(2)}) collective-permute-start(bf16[1,128,128]{2,1,0:T(8,128)(2,1)S(1)} %get-tuple-element.30), channel_id=1, source_target_pairs={{0,1},{1,0},{2,3},{3,2},{4,5},{5,4},{6,7},{7,6},{8,9},{9,8},{10,11... | collective-permute-start | bytes 98312 | tf_op jit(solution)/shard_map/ppermute | solution.py:552
  66.4 8.9 %collective-permute-start.5 = (bf16[1,128,128]{2,1,0:T(8,128)(2,1)S(1)}, bf16[1,128,128]{2,1,0:T(8,128)(2,1)S(1)}, u32[]{:S(2)}, u32[]{:S(2)}) collective-permute-start(bf16[1,128,128]{2,1,0:T(8,128)(2,1)S(1)} %get-tuple-element.31), channel_id=1, source_target_pairs={{1,2},{2,1},{3,4},{4,3},{5,6},{6,5},{7,8},{8,7},{9,10},{10,9},{11,... | collective-permute-start | bytes 98312 | tf_op jit(solution)/shard_map/ppermute | solution.py:552
  69.0 1.0 %copy-start.4 = (f32[8,128,128]{2,1,0:T(8,128)S(1)}, f32[8,128,128]{2,1,0:T(8,128)}, u32[]{:S(2)}) copy-start(f32[8,128,128]{2,1,0:T(8,128)} %get-tuple-element.17.grid_term) | copy-start | bytes 1572868
  70.1 5.2 %copy-start.5 = (f32[8,128,128]{2,1,0:T(8,128)S(1)}, f32[8,128,128]{2,1,0:T(8,128)}, u32[]{:S(2)}) copy-start(f32[8,128,128]{2,1,0:T(8,128)} %get-tuple-element.17.grid_term) | copy-start | bytes 1572868

commit v2 on v1

--- a/solution.py
+++ b/solution.py
@@ -86,23 +86,25 @@
             hp_ref[i + 1, j - i + 1] = value.astype(BF16)
 
 
-def propagate(low, high, get_q, get_hp, get_left, get_right, moved_ref, wh_ref, write):
+def propagate(ranges, get_q, get_hp, get_left, get_right, moved_ref, wh_ref, write):
     def get(ref):
         return lambda i, j: ref[i + 1, j - i + 1]
 
-    columns = range(low - 1, high + 2)
-    for j in columns:
-        for i, value in band_column(get_left, get_hp, j, low, high).items():
-            moved = get_q(i, j).astype(F32) - HALF_STEP * times_i(get_hp(i, j).astype(F32)) - SECOND_ORDER * value
-            moved_ref[i + 1, j - i + 1] = moved.astype(BF16)
-    for j in columns:
-        for i, value in band_column(get(moved_ref), get_right, j, low, high).items():
-            wh_ref[i + 1, j - i + 1] = value.astype(BF16)
-    for j in columns:
-        for i, value in band_column(get(wh_ref), get_right, j, low, high).items():
-            moved = moved_ref[i + 1, j - i + 1].astype(F32)
-            wh = wh_ref[i + 1, j - i + 1].astype(F32)
-            write(i, j, (moved + HALF_STEP * times_i(wh) - SECOND_ORDER * value).astype(BF16))
+    def product(left, right):
+        for low, high in ranges:
+            for j in range(low - 1, high + 2):
+                for i, value in band_column(left, right, j, low, high).items():
+                    yield i, j, value
+
+    for i, j, value in product(get_left, get_hp):
+        moved = get_q(i, j).astype(F32) - HALF_STEP * times_i(get_hp(i, j).astype(F32)) - SECOND_ORDER * value
+        moved_ref[i + 1, j - i + 1] = moved.astype(BF16)
+    for i, j, value in product(get(moved_ref), get_right):
+        wh_ref[i + 1, j - i + 1] = value.astype(BF16)
+    for i, j, value in product(get(wh_ref), get_right):
+        moved = moved_ref[i + 1, j - i + 1].astype(F32)
+        wh = wh_ref[i + 1, j - i + 1].astype(F32)
+        write(i, j, (moved + HALF_STEP * times_i(wh) - SECOND_ORDER * value).astype(BF16))
 
 
 def lanes_rows(shape):
@@ -145,7 +147,7 @@
     return 0.5 * (value + value.T)
 
 
-def send_kernel(count, dens, core, grid_old, owners, send_a, send_b, place, sources, slots, bands, grids, sems):
+def send_kernel(count, dens, core, grid_old, send_a, send_b, bands, grids, sems):
     last = count - 1
     places = [(dens, last, 1), (dens, last - 1, 2), (core, last, 1), (core, last, 0),
               (dens, 0, 1), (dens, 1, 0), (core, 0, 1), (core, 0, 2)]
@@ -157,19 +159,6 @@
     ]
     for copy in copies:
         copy.start()
-
-    lane, _ = lanes_rows(owners.shape)
-    source = owners[...] // count // lax.axis_size("col")
-    slot = jnp.zeros(owners.shape, jnp.int32)
-    for t in range(owners.shape[1] - 1):
-        slot += jnp.where((lane > t) & (source == source[:, t : t + 1]), 1, 0)
-    mine = jnp.where(source == lax.axis_index("row"), owners[...] % count, -1)
-    table = jnp.zeros(owners.shape, jnp.int32)
-    for n in range(CAP):
-        table = jnp.where(lane == n, jnp.max(jnp.where(slot == n, mine, -1), axis=1, keepdims=True), table)
-    place[...] = table
-    sources[...] = source
-    slots[...] = slot
     for copy in copies:
         copy.wait()
 
@@ -251,7 +240,7 @@
     set_diagonals(rows, count, leads, absorption, diag_re, diag_im, left_ref, right_ref)
 
 
-def new_diagonals(rows, count, leads, absorption, core, grid_term, left_ref, right_ref, ends=None, ends_re=None):
+def new_diagonals(rows, count, leads, absorption, core, diag_new, left_ref, right_ref, ends=None, ends_re=None):
     width = core.shape[-1]
 
     def diag_re(i):
@@ -259,7 +248,7 @@
             return ends_re[0]
         if i == count:
             return ends_re[1]
-        return (core[0, i, 1].astype(F32) + grid_term[i]).astype(BF16)
+        return diag_new[i]
 
     def diag_im(i):
         return ends[0][:, width:] if i == -1 else ends[1][:, width:] if i == count else core[1, i, 1]
@@ -280,7 +269,29 @@
     return get
 
 
-def first_inner_kernel(count, leads, absorption, dens, core, grid_old, hp_ref, half, moved_ref, wh_ref, left_ref, right_ref):
+def brick_tables(count, owners, place, which):
+    lane, row = lanes_rows(owners.shape)
+    own = lax.axis_index("row")
+    source = owners[...] // count // lax.axis_size("col")
+    slot = jnp.zeros(owners.shape, jnp.int32)
+    for t in range(owners.shape[1] - 1):
+        slot += jnp.where((lane > t) & (source == source[:, t : t + 1]), 1, 0)
+    mine = jnp.where(source == own, owners[...] % count, -1)
+    own_source = jnp.sum(jnp.where(row == own, source, 0), axis=0, keepdims=True)
+    own_slot = jnp.sum(jnp.where(row == own, slot, 0), axis=0, keepdims=True)
+    here = own_source == row
+    places = jnp.zeros(owners.shape, jnp.int32)
+    bricks = jnp.zeros(owners.shape, jnp.int32)
+    for n in range(CAP):
+        places = jnp.where(lane == n, jnp.max(jnp.where(slot == n, mine, -1), axis=1, keepdims=True), places)
+        brick = jnp.max(jnp.where(here & (own_slot == n), lane, 0), axis=1, keepdims=True)
+        bricks = jnp.where(lane == n, brick, bricks)
+    place[...] = places
+    which[...] = bricks
+
+
+def first_inner_kernel(count, leads, absorption, dens, core, grid_old, owners, hp_ref, half, place, which, moved_ref, wh_ref, left_ref, right_ref):
+    brick_tables(count, owners, place, which)
     old_diagonals(range(count), count, leads, absorption, core, grid_old, left_ref, right_ref)
     get_left = band_access(count, core, None, None, None, None, left_ref)
     get_right = band_access(count, core, None, None, None, None, right_ref)
@@ -290,12 +301,12 @@
         return hp_ref[i + 1, j - i + 1]
 
     taylor_first(range(count), 1, count - 2, get_left, get_q, hp_ref)
-    propagate(2, count - 3, get_q, get_hp, get_left, get_right, moved_ref, wh_ref, band_writer(half))
+    propagate([(2, count - 3)], get_q, get_hp, get_left, get_right, moved_ref, wh_ref, band_writer(half))
 
 
 def first_outer_kernel(count, leads, absorption, place, dens, core, grid_old, got_a, got_b, hp_in, half_in,
-                       half_out, outgoing, send_a_out, send_b_out,
-                       hp_ref, moved_ref, wh_ref, left_ref, right_ref, edges, packed, diagonals, half, out_buf, send_a, send_b, sems):
+                       half, send_a, send_b, *rest):
+    outgoing, (hp_ref, moved_ref, wh_ref, left_ref, right_ref, edges, packed, diagonals) = rest[:-8], rest[-8:]
     low, high = halo_reader(got_a, got_b)
     last = count - 1
     edges[0] = dagger(band_at(dens)(0, -1))
@@ -335,10 +346,7 @@
     write = band_writer(half)
     taylor_first(range(-1, 2), -1, 0, get_left, get_q, hp_ref)
     taylor_first(range(last - 1, count + 1), last, count, get_left, get_q, hp_ref)
-    propagate(0, 1, get_q, get_hp, get_left, get_right, moved_ref, wh_ref, write)
-    propagate(last - 1, last, get_q, get_hp, get_left, get_right, moved_ref, wh_ref, write)
-    copies = [pltpu.make_async_copy(half, half_out, sems.at[0])]
-    copies[0].start()
+    propagate([(0, 1), (last - 1, last)], get_q, get_hp, get_left, get_right, moved_ref, wh_ref, write)
 
     right = [(last, 1), (last, 2), (last - 1, 2)]
     left = [(0, 1), (0, 0), (1, 0)]
@@ -359,10 +367,6 @@
     def _():
         send(left, right)
 
-    for source, target, n in ((send_a, send_a_out, 1), (send_b, send_b_out, 2)):
-        copies.append(pltpu.make_async_copy(source, target, sems.at[n]))
-        copies[-1].start()
-
     for i in range(count):
         top, diagonal = pack_symmetric(half[0, i, 1].astype(F32), True)
         packed[i] = top.astype(BF16)
@@ -371,63 +375,44 @@
     height, width = packed.shape[1:]
     _, row = lanes_rows((TILE, width))
 
-    def put(p, carry):
+    for offset, out in enumerate(outgoing):
+        p = lax.axis_index("row") ^ offset
         tail = jnp.zeros((TILE, width), F32)
         for n in range(CAP):
             source = jnp.maximum(place[p, n], 0)
-            out_buf[p, n * height : (n + 1) * height] = packed[source]
+            out[n * height : (n + 1) * height] = packed[source]
             tail = jnp.where(row == n, diagonals[source][:1], tail)
-        out_buf[p, CAP * height :] = tail.astype(BF16)
-        return carry
-
-    lax.fori_loop(0, out_buf.shape[0], put, 0)
-    copies.append(pltpu.make_async_copy(out_buf, outgoing, sems.at[3]))
-    copies[-1].start()
-    for copy in copies:
-        copy.wait()
-
-
-def brick_kernel(chunk, groups, sources, slots, far, incoming, returned, colloc, sems):
-    bricks, points, width = colloc.shape
-    own = lax.axis_index("row")
+        out[CAP * height :] = tail.astype(BF16)
+
+
+def brick_kernel(chunk, offsets, which, colloc, *rest):
+    incoming, returned = rest[: len(offsets)], rest[len(offsets) :]
+    points, width = colloc.shape[1:]
     scale = GRID_FACTOR * width / points
     height = width // 2
-    tail = CAP * height
     _, tail_row = lanes_rows((TILE, width))
-
-    loads = {
-        start: pltpu.make_async_copy(far.at[pl.ds(start, size)], colloc.at[pl.ds(start, size)], sems.at[n])
-        for n, (start, size) in enumerate(groups)
-    }
-    for load in loads.values():
-        load.start()
-    returned[...] = jnp.zeros_like(returned)
-
-    def block(t):
-        start = pl.multiple_of(slots[own, t] * height, height)
-        diagonal = jnp.sum(
-            jnp.where(tail_row == slots[own, t], incoming[sources[own, t], tail : tail + TILE].astype(F32), 0.0),
-            axis=0,
-            keepdims=True,
-        )
-        return unpack_triangle(incoming[sources[own, t], pl.ds(start, height)].astype(F32), diagonal)
-
-    def put(t, result):
-        start = pl.multiple_of(slots[own, t] * height, height)
+    tails = [jnp.zeros((TILE, width), F32) for _ in offsets]
+    jobs = [(m, n, which[lax.axis_index("row") ^ offset, n]) for m, offset in enumerate(offsets) for n in range(CAP)]
+
+    def block(job):
+        m, n, _ = job
+        last = incoming[m][CAP * height :].astype(F32)
+        return unpack_triangle(incoming[m][n * height : (n + 1) * height].astype(F32), last[n : n + 1])
+
+    def put(job, result):
+        m, n, _ = job
         packed, diagonal = pack_symmetric(scale * result, False)
-        returned[sources[own, t], pl.ds(start, height)] = packed.astype(BF16)
-        old = returned[sources[own, t], tail : tail + TILE].astype(F32)
-        returned[sources[own, t], tail : tail + TILE] = jnp.where(tail_row == slots[own, t], diagonal, old).astype(BF16)
-
-    for t in range(0, bricks, 2):
-        q0, q1 = block(t), block(t + 1)
+        returned[m][n * height : (n + 1) * height] = packed.astype(BF16)
+        tails[m] = jnp.where(tail_row == n, diagonal, tails[m])
+
+    for first, second in zip(jobs[::2], jobs[1::2]):
+        c0, c1 = colloc.at[first[2]], colloc.at[second[2]]
+        q0, q1 = block(first), block(second)
         zero = jnp.zeros_like(q0)
         both = jnp.concatenate([joined(q0, zero), joined(zero, q1)], axis=0).astype(BF16)
         columns = []
-        if t in loads:
-            loads[t].wait()
         for g in range(0, points, chunk):
-            turned = jnp.concatenate([colloc[t, g : g + chunk].T, colloc[t + 1, g : g + chunk].T], axis=0)
+            turned = jnp.concatenate([c0[g : g + chunk].T, c1[g : g + chunk].T], axis=0)
             wide = turned.astype(F32)
             projected = jnp.dot(both, turned, preferred_element_type=F32) * wide
             weighted = []
@@ -437,38 +422,35 @@
                 potential = dens * lax.rsqrt(1.0 + dens * dens)
                 weighted.append((potential * wide[rows]).astype(BF16))
             columns.append(jnp.concatenate(weighted, axis=0))
-        result = jnp.dot(
-            jnp.concatenate(columns, axis=1), joined(colloc[t], colloc[t + 1]), preferred_element_type=F32
-        )
-        put(t, result[:width, :width])
-        put(t + 1, result[width:, width:])
-
-
-def collect_kernel(count, place, arriving, core, grid_term, send_a, send_b, total, tails):
-    width = arriving.shape[-1]
+        result = jnp.dot(jnp.concatenate(columns, axis=1), joined(c0[...], c1[...]), preferred_element_type=F32)
+        put(first, result[:width, :width])
+        put(second, result[width:, width:])
+    for out, tail in zip(returned, tails):
+        out[CAP * height :] = tail.astype(BF16)
+
+
+def collect_kernel(count, place, core, *rest):
+    arriving, (grid_term, diag_new, send_a, send_b, total, tails) = rest[:-6], rest[-6:]
+    width = core.shape[-1]
     height = width // 2
     total[...] = jnp.zeros_like(total)
     tails[...] = jnp.zeros_like(tails)
-
-    def add(p, carry):
-        last = arriving[p, CAP * height :].astype(F32)
+    for offset, block in enumerate(arriving):
+        p = lax.axis_index("row") ^ offset
+        last = block[CAP * height :].astype(F32)
         for n in range(CAP):
             at = place[p, n]
-
-            @pl.when(at >= 0)
-            def _():
-                total[at] += arriving[p, n * height : (n + 1) * height].astype(F32)
-                tails[at] += jnp.broadcast_to(last[n : n + 1], tails.shape[1:])
-
-        return carry
-
-    lax.fori_loop(0, arriving.shape[0], add, 0)
+            kept = at >= 0
+            at = jnp.maximum(at, 0)
+            total[at] += jnp.where(kept, block[n * height : (n + 1) * height].astype(F32), 0.0)
+            tails[at] += jnp.where(kept, last[n : n + 1], 0.0)
     lane, row = lanes_rows((width, width))
     for i in range(count):
         triangle = unpack_triangle(total[i], tails[i][:1])
-        grid_term[i] = jnp.where(lane == row, triangle, triangle + triangle.T)
-    right = (core[0, count - 1, 0].astype(F32) + grid_term[count - 1]).astype(BF16)
-    left = (core[0, 0, 0].astype(F32) + grid_term[0]).astype(BF16)
+        term = jnp.where(lane == row, triangle, triangle + triangle.T)
+        grid_term[i] = term
+        diag_new[i] = (core[0, i, 0].astype(F32) + term).astype(BF16)
+    right, left = diag_new[count - 1], diag_new[0]
     even = lax.axis_index("col") % 2 == 0
     send_a[0] = jnp.where(even, right, left)
     send_b[0] = jnp.where(even, left, right)
@@ -489,9 +471,9 @@
     return get_q
 
 
-def second_inner_kernel(count, leads, absorption, half, core, grid_term, half_a, half_b,
+def second_inner_kernel(count, leads, absorption, half, core, diag_new, half_a, half_b,
                         out, hp_ref, moved_ref, wh_ref, left_ref, right_ref):
-    new_diagonals(range(count), count, leads, absorption, core, grid_term, left_ref, right_ref)
+    new_diagonals(range(count), count, leads, absorption, core, diag_new, left_ref, right_ref)
     get_left = band_access(count, core, None, None, None, None, left_ref)
     get_right = band_access(count, core, None, None, None, None, right_ref)
     get_q = half_access(count, half, half_a, half_b)
@@ -500,10 +482,10 @@
         return hp_ref[i + 1, j - i + 1]
 
     taylor_first(range(-1, count + 1), 0, count - 1, get_left, get_q, hp_ref)
-    propagate(1, count - 2, get_q, get_hp, get_left, get_right, moved_ref, wh_ref, band_writer(out))
-
-
-def second_outer_kernel(count, leads, absorption, half, core, grid_term, core_a, core_b, half_a, half_b, diag_a, diag_b,
+    propagate([(1, count - 2)], get_q, get_hp, get_left, get_right, moved_ref, wh_ref, band_writer(out))
+
+
+def second_outer_kernel(count, leads, absorption, half, core, diag_new, core_a, core_b, half_a, half_b, diag_a, diag_b,
                         hp_in, out_in, out, hp_ref, moved_ref, wh_ref, left_ref, right_ref, edges, ready, sems):
     core_low, core_high = halo_reader(core_a, core_b)
     diag_low, diag_high = halo_reader(diag_a, diag_b)
@@ -512,7 +494,7 @@
     edges[1] = dagger(band_at(core)(last, count))
     ends = unpack_hermitian(core_low(3)), unpack_hermitian(core_high(3))
     rows = [-1, 0, 1, count - 2, last, count]
-    new_diagonals(rows, count, leads, absorption, core, grid_term, left_ref, right_ref, ends, (diag_low(0), diag_high(0)))
+    new_diagonals(rows, count, leads, absorption, core, diag_new, left_ref, right_ref, ends, (diag_low(0), diag_high(0)))
     get_q = half_access(count, half, half_a, half_b)
 
     def far_low():
@@ -536,9 +518,9 @@
 
     taylor_first(range(-1, 1), -1, -1, get_left, get_q, hp_ref)
     taylor_first(range(last, count + 1), count, count, get_left, get_q, hp_ref)
+    propagate([(0, 0), (last, last)], get_q, get_hp, get_left, get_right, moved_ref, wh_ref, write)
     copies = []
     for n, i in enumerate((0, last)):
-        propagate(i, i, get_q, get_hp, get_left, get_right, moved_ref, wh_ref, write)
         copies.append(pltpu.make_async_copy(ready.at[:, n], out.at[:, i], sems.at[n]))
         copies[-1].start()
     for copy in copies:
@@ -563,18 +545,18 @@
 
     message = jax.ShapeDtypeStruct((6, width, width), BF16)
     table = jax.ShapeDtypeStruct(brick_block.shape, jnp.int32)
-    send_a, send_b, place, sources, slots = call(
+    send_a, send_b = call(
         functools.partial(send_kernel, count),
-        (message, message, table, table, table),
+        (message, message),
         flops=1 << 20,
         vmem=8,
-        in_specs=[hbm] * 3 + [vmem],
+        in_specs=[hbm] * 3,
         scratch=[
             pltpu.VMEM((8, 2, width, width), BF16),
             pltpu.VMEM((2, width, width), F32),
             pltpu.SemaphoreType.DMA((10,)),
         ],
-    )(*(in_hbm(x) for x in (density, core, grid_old)), brick_block)
+    )(*(in_hbm(x) for x in (density, core, grid_old)))
     got_a, got_b = exchange(send_a, send_b, total)
 
     def band_scratch(rows):
@@ -586,26 +568,26 @@
     hp_shape = jax.ShapeDtypeStruct((count + 2, 3, width, 2 * width), BF16)
     inner_scratch = [band_scratch(count + 2)] * 2 + [sides(count + 2)] * 2
     outer_scratch = [band_scratch(count + 2)] * 3 + [sides(count + 2)] * 2
-    hp, half_inner = call(
+    hp, half_inner, place, which = call(
         functools.partial(first_inner_kernel, count),
-        (hp_shape, jax.ShapeDtypeStruct(density.shape, BF16)),
+        (hp_shape, jax.ShapeDtypeStruct(density.shape, BF16), table, table),
         flops=PROP_FLOPS,
         vmem=16,
         scalars=2,
-        in_specs=[vmem] * 3,
+        in_specs=[vmem] * 4,
         scratch=inner_scratch,
-    )(lead_blocks, absorption, density, core, grid_old)
+    )(lead_blocks, absorption, density, core, grid_old, brick_block)
     packed_rows = CAP * width // 2 + TILE
-    packed_shape = jax.ShapeDtypeStruct((row_size, packed_rows, width), BF16)
-    half_message = pltpu.HBM((6, width, width), BF16)
-    half, outgoing, send_a, send_b = call(
+    packed_shape = jax.ShapeDtypeStruct((packed_rows, width), BF16)
+    half_message = jax.ShapeDtypeStruct((6, width, width), BF16)
+    half, send_a, send_b, *outgoing = call(
         functools.partial(first_outer_kernel, count),
         (
-            pltpu.HBM(density.shape, BF16),
-            pltpu.HBM(packed_shape.shape, BF16),
+            jax.ShapeDtypeStruct(density.shape, BF16),
             half_message,
             half_message,
-        ),
+        )
+        + (packed_shape,) * row_size,
         flops=PROP_FLOPS,
         vmem=20,
         scalars=3,
@@ -615,43 +597,46 @@
             pltpu.VMEM((6, width, 2 * width), BF16),
             pltpu.VMEM((count, width // 2, width), BF16),
             pltpu.VMEM((count, 8, width), F32),
-            pltpu.VMEM(density.shape, BF16),
-            pltpu.VMEM(packed_shape.shape, BF16),
-            pltpu.VMEM(half_message.shape, BF16),
-            pltpu.VMEM(half_message.shape, BF16),
-            pltpu.SemaphoreType.DMA((4,)),
         ],
-        out_specs=(hbm,) * 4,
     )(lead_blocks, absorption, place, density, core, grid_old, got_a, got_b, hp, half_inner)
 
-    incoming = lax.all_to_all(outgoing, "row", split_axis=0, concat_axis=0, tiled=True)
     half_a, half_b = exchange(send_a, send_b, total)
 
+    def across(x, offset):
+        return lax.ppermute(x, "row", [(i, i ^ offset) for i in range(row_size)]) if offset else x
+
+    order = [0] + list(range(row_size // 2, row_size)) + list(range(1, row_size // 2))
+    incoming = {offset: across(outgoing[offset], offset) for offset in order}
     points = collocation.shape[1]
-    ends = [0, bricks // 6, bricks // 2, bricks]
-    groups = [(a, b - a) for a, b in zip(ends, ends[1:])]
-    returned = call(
-        functools.partial(brick_kernel, points // 4, groups),
-        packed_shape,
-        flops=4 * bricks * points * width**2,
-        vmem=20,
-        scalars=2,
-        in_specs=[hbm, vmem],
-        scratch=[pltpu.VMEM(collocation.shape, BF16), pltpu.SemaphoreType.DMA((3,))],
-    )(sources, slots, in_hbm(collocation), incoming)
-    arriving = lax.all_to_all(returned, "row", split_axis=0, concat_axis=0, tiled=True)
+    arriving = {}
+    for offsets in zip(order[::2], order[1::2]):
+        returned = call(
+            functools.partial(brick_kernel, points // 4, offsets),
+            (packed_shape,) * 2,
+            flops=4 * 6 * points * width**2,
+            vmem=8,
+            scalars=1,
+            in_specs=[vmem] * 3,
+        )(which, collocation, *(incoming[offset] for offset in offsets))
+        for offset, x in zip(offsets, returned):
+            arriving[offset] = across(x, offset)
 
     diag_message = jax.ShapeDtypeStruct((1, width, width), BF16)
-    grid_term, send_a, send_b = call(
+    grid_term, diag_new, send_a, send_b = call(
         functools.partial(collect_kernel, count),
-        (jax.ShapeDtypeStruct((count, width, width), F32), diag_message, diag_message),
+        (
+            jax.ShapeDtypeStruct((count, width, width), F32),
+            jax.ShapeDtypeStruct((count, width, width), BF16),
+            diag_message,
+            diag_message,
+        ),
         flops=1 << 20,
         vmem=8,
         scalars=1,
         grid=(1,),
-        in_specs=[vmem, block_spec((1, count, 1, width, width), (0, 0, 1, 0, 0))],
+        in_specs=[block_spec((1, count, 1, width, width), (0, 0, 1, 0, 0))] + [vmem] * row_size,
         scratch=[pltpu.VMEM((count, width // 2, width), F32), pltpu.VMEM((count, 8, width), F32)],
-    )(place, arriving, core)
+    )(place, core, *(arriving[offset] for offset in range(row_size)))
     diag_a, diag_b = exchange(send_a, send_b, total)
 
     inner, hp = call(
@@ -662,7 +647,7 @@
         scalars=2,
         in_specs=[vmem] * 5,
         scratch=inner_scratch,
-    )(lead_blocks, absorption, half, core, grid_term, half_a, half_b)
+    )(lead_blocks, absorption, half, core, diag_new, half_a, half_b)
     density_next = call(
         functools.partial(second_outer_kernel, count),
         pltpu.HBM(density.shape, BF16),
@@ -673,7 +658,7 @@
         out_specs=hbm,
         scratch=outer_scratch + [sides(2), pltpu.VMEM((2, 2, 3, width, width), BF16), pltpu.SemaphoreType.DMA((2,))],
         aliases={12: 0},
-    )(lead_blocks, absorption, half, core, grid_term, got_a, got_b, half_a, half_b, diag_a, diag_b, hp, in_hbm(inner))
+    )(lead_blocks, absorption, half, core, diag_new, got_a, got_b, half_a, half_b, diag_a, diag_b, hp, in_hbm(inner))
     return (density_next, grid_term)
 
 

time: 78.8 us -> 71.1 us (0.902)
  blocking collectives: 19.1 us -> 0 us
  starting transfers between devices: 18.7 us -> 34.2 us
  waiting for transfers between devices: 7.27 us -> 5.66 us
  local copies, waits for them, and re-layouts: 1.9 us -> 0.71 us
  Pallas kernels: 30.4 us -> 29.3 us
    ppermute x0 -> x14, starting transfers between devices: none -> 21.1 us  [across(): lax.ppermute(x, 'row', [(i, i ^ offset) for i in range(row_size)])]
    all_to_all x1 -> x0, blocking collectives: 19.1 us -> none  [shards(): lax.all_to_all(outgoing, 'row', split_axis=0, concat_axis=0, tiled=True)]
    all_to_all x1 -> x0, waiting for transfers between devices: 5.85 us -> none  [shards(): lax.all_to_all(returned, 'row', split_axis=0, concat_axis=0, tiled=True)]
    ppermute x0 -> x14, waiting for transfers between devices: none -> 4.96 us  [across(): lax.ppermute(x, 'row', [(i, i ^ offset) for i in range(row_size)])]
    all_to_all x1 -> x0, starting transfers between devices: 4.02 us -> none  [shards(): lax.all_to_all(returned, 'row', split_axis=0, concat_axis=0, tiled=True)]
    ppermute x3, starting transfers between devices: 5.5 us -> 3.82 us  [exchange(): lax.ppermute(send_a, axes, first)]
    unnamed x22 -> x18, local copies, waits for them, and re-layouts: 1.9 us -> 0.71 us
    pallas_call x3 -> x6, Pallas kernels: 17.2 us -> 16.3 us  [the longest x4 11.3 us: shards(): call(functools.partial(brick_kernel, points // 4, offsets), (packed_shape...]
  transfers between devices with their start and end apart: 7 -> 20, of which waited for: 2 -> 3; matrix products, arithmetic and copies ran while one was open for 0% -> 0% of each run, Pallas kernels for 13% -> 30%
where the time goes in v2:
time: 71.1 us; the launch traced here: 70.9 us
  starting transfers between devices  34.2 us (48%)
  Pallas kernels  29.3 us (41%)
  waiting for transfers between devices  5.66 us (8%)
  between operations  1.02 us (1%)
    ppermute x14, starting transfers between devices, across(): lax.ppermute(x, 'row', [(i, i ^ offset) for i in range(row_size)])  21.1 us
    pallas_call x4, Pallas kernels, shards(): call(functools.partial(brick_kernel, points // 4, offsets), (packed_shape...  11.3 us
    ppermute x3, starting transfers between devices, exchange(): lax.ppermute(send_b, axes, second)  9.3 us
    pallas_call x1, Pallas kernels, shards(): call(functools.partial(second_inner_kernel, count), (jax.ShapeDtypeStruct...  5.32 us
    ppermute x14, waiting for transfers between devices, across(): lax.ppermute(x, 'row', [(i, i ^ offset) for i in range(row_size)])  4.96 us
    ppermute x3, starting transfers between devices, exchange(): lax.ppermute(send_a, axes, first)  3.82 us
    pallas_call x1, Pallas kernels, shards(): call(functools.partial(first_outer_kernel, count), (jax.ShapeDtypeStruct(...  3.46 us
    pallas_call x1, Pallas kernels, shards(): call(functools.partial(first_inner_kernel, count), (hp_shape, jax.ShapeDt...  3.1 us
  transfers between devices with their start and end apart: 20, of which 3 were waited for; matrix products, arithmetic and copies ran while one was open for 0% of the time, Pallas kernels for 30%

profile of v2, /device:TPU:1, one launch (start us, length us, event | category | flops | bytes accessed | tf_op | source)
XLA Modules:
  0.0 70.9 jit_solution(5778936569441118141)
XLA Ops:
  0.6 0.0 copy-start
  0.6 0.0 copy-start.2
  0.7 0.0 copy-start.1
  0.7 0.0 copy-start.5
  0.7 0.0 copy-start.4
  0.7 1.5 %shard_map.87 = (bf16[6,128,128]{2,1,0:T(8,128)(2,1)S(1)}, bf16[6,128,128]{2,1,0:T(8,128)(2,1)S(1)}) custom-call(bf16[2,8,3,128,128]{4,3,2,1,0:T(8,128)(2,1)} %dens.5, bf16[2,8,3,128,128]{4,3,2,1,0:T(8,128)(2,1)} %core.11, f32[8,128,128]{2,1,0:T(8,128)} %grid_old.5), custom_call_target="tpu_custom_call" | custom-call | flops 1048576 | bytes 4194304 | tf_op jit(solution)/shard_map/pallas_call | solution.py:548
  2.2 0.1 collective-permute-start
  2.3 4.5 %collective-permute-start.1 = (bf16[6,128,128]{2,1,0:T(8,128)(2,1)S(1)}, bf16[6,128,128]{2,1,0:T(8,128)(2,1)S(1)}, u32[]{:S(2)}, u32[]{:S(2)}) collective-permute-start(bf16[6,128,128]{2,1,0:T(8,128)(2,1)S(1)} %get-tuple-element.35), channel_id=1, source_target_pairs={{1,2},{2,1},{3,4},{4,3},{5,6},{6,5},{7,8},{8,7},{9,10},{10,9},{11,... | collective-permute-start | bytes 589832 | tf_op jit(solution)/shard_map/ppermute | solution.py:534
  6.8 0.0 copy-done
  6.8 0.0 copy-done.2
  6.8 0.0 copy-done.1
  6.8 0.0 copy-done.5
  6.9 0.0 copy-done.4
  6.9 0.0 copy-start.3
  6.9 0.7 copy-done.3
  7.6 3.1 %shard_map.86 = (bf16[10,3,128,256]{3,2,1,0:T(8,128)(2,1)S(1)}, bf16[2,8,3,128,128]{4,3,2,1,0:T(8,128)(2,1)S(1)}, s32[8,24]{1,0:T(8,128)S(1)}, s32[8,24]{1,0:T(8,128)S(1)}) custom-call(s32[8]{0:T(128)S(1)} %copy-done.4, f32[8]{0:T(128)S(1)} %copy-done.5, bf16[2,8,3,128,128]{4,3,2,1,0:T(8,128)(2,1)S(1)} %copy-done.1, ...), custom_call_target="tpu_custom_call" | custom-call | flops 4294967296 | bytes 4194304 | tf_op jit(solution)/shard_map/pallas_call | solution.py:571
  10.7 0.0 collective-permute-done.got_a.core_a
  10.7 0.7 collective-permute-done.1.got_b.core_b
  11.4 3.5 %shard_map.88 = (bf16[2,8,3,128,128]{4,3,2,1,0:T(8,128)(2,1)S(1)}, bf16[6,128,128]{2,1,0:T(8,128)(2,1)S(1)}, bf16[6,128,128]{2,1,0:T(8,128)(2,1)S(1)}, bf16[208,...) custom-call(s32[8]{0:T(128)S(1)} %copy-done.4, ...), custom_call_target="tpu_custom_call" | custom-call | flops 4294967296 | bytes 4194304 | tf_op jit(solution)/shard_map/pallas_call | solution.py:583
  14.8 3.6 %collective-permute-start.2 = (bf16[208,128]{1,0:T(8,128)(2,1)S(1)}, bf16[208,128]{1,0:T(8,128)(2,1)S(1)}, u32[]{:S(2)}, u32[]{:S(2)}) collective-permute-start(bf16[208,128]{1,0:T(8,128)(2,1)S(1)} %get-tuple-element.41), channel_id=1, source_target_pairs={{0,16},{4,20},{8,24},{12,28},{16,0},{20,4},{24,8},{28,12},{1,17},{... | collective-permute-start | bytes 159752 | tf_op jit(solution)/shard_map/ppermute | solution.py:606
  18.4 2.6 %collective-permute-start.3 = (bf16[208,128]{1,0:T(8,128)(2,1)S(1)}, bf16[208,128]{1,0:T(8,128)(2,1)S(1)}, u32[]{:S(2)}, u32[]{:S(2)}) collective-permute-start(bf16[208,128]{1,0:T(8,128)(2,1)S(1)} %get-tuple-element.43), channel_id=1, source_target_pairs={{0,28},{4,24},{8,20},{12,16},{16,12},{20,8},{24,4},{28,0},{1,29},{... | collective-permute-start | bytes 159752 | tf_op jit(solution)/shard_map/ppermute | solution.py:606
  21.0 0.0 collective-permute-start.4
  21.0 0.5 collective-permute-start.6
  21.5 2.2 %collective-permute-start.7 = (bf16[208,128]{1,0:T(8,128)(2,1)S(1)}, bf16[208,128]{1,0:T(8,128)(2,1)S(1)}, u32[]{:S(2)}, u32[]{:S(2)}) collective-permute-start(bf16[208,128]{1,0:T(8,128)(2,1)S(1)} %get-tuple-element.47), channel_id=1, source_target_pairs={{0,12},{4,8},{8,4},{12,0},{16,28},{20,24},{24,20},{28,16},{1,13},{... | collective-permute-start | bytes 159752 | tf_op jit(solution)/shard_map/ppermute | solution.py:606
  23.6 0.0 collective-permute-done.2.rest_1_
  23.6 1.1 %collective-permute-start.11 = (bf16[208,128]{1,0:T(8,128)(2,1)S(1)}, bf16[208,128]{1,0:T(8,128)(2,1)S(1)}, u32[]{:S(2)}, u32[]{:S(2)}) collective-permute-start(bf16[208,128]{1,0:T(8,128)(2,1)S(1)} %get-tuple-element.51), channel_id=1, source_target_pairs={{0,20},{4,16},{8,28},{12,24},{16,4},{20,0},{24,12},{28,8},{1,21},{... | collective-permute-start | bytes 159752 | tf_op jit(solution)/shard_map/ppermute | solution.py:606
  24.8 0.0 slice-done
  24.8 0.0 slice-done.1
  24.8 2.8 %shard_map.89 = (bf16[208,128]{1,0:T(8,128)(2,1)S(1)}, bf16[208,128]{1,0:T(8,128)(2,1)S(1)}) custom-call(s32[8,24]{1,0:T(8,128)S(1)} %get-tuple-element.39.which, bf16[24,2048,128]{2,1,0:T(8,128)(2,1)S(1)} %bitcast.1, bf16[208,128]{1,0:T(8,128)(2,1)S(1)} %get-tuple-element.40.rest_0_, bf16[208,128]{1,0:T(8,128)(2,1)S(1)} %collective-permute-done.2.rest_1_), custom_call_target="tpu_custom_call" | custom-call | flops 805306368 | bytes 4194304 | tf_op jit(solution)/shard_map/pallas_call | solution.py:613
  27.6 0.0 collective-permute-done.3.rest_0_
  27.6 2.3 %collective-permute-start.12 = (bf16[208,128]{1,0:T(8,128)(2,1)S(1)}, bf16[208,128]{1,0:T(8,128)(2,1)S(1)}, u32[]{:S(2)}, u32[]{:S(2)}) collective-permute-start(bf16[208,128]{1,0:T(8,128)(2,1)S(1)} %get-tuple-element.52), channel_id=1, source_target_pairs={{0,24},{4,28},{8,16},{12,20},{16,8},{20,12},{24,0},{28,4},{1,25},{... | collective-permute-start | bytes 159752 | tf_op jit(solution)/shard_map/ppermute | solution.py:606
  29.9 0.0 collective-permute-done.4.rest_1_
  29.9 1.1 %collective-permute-start.16 = (bf16[6,128,128]{2,1,0:T(8,128)(2,1)S(1)}, bf16[6,128,128]{2,1,0:T(8,128)(2,1)S(1)}, u32[]{:S(2)}, u32[]{:S(2)}) collective-permute-start(bf16[6,128,128]{2,1,0:T(8,128)(2,1)S(1)} %get-tuple-element.57), channel_id=1, source_target_pairs={{0,1},{1,0},{2,3},{3,2},{4,5},{5,4},{6,7},{7,6},{8,9},{9,8},{10,11... | collective-permute-start | bytes 589832 | tf_op jit(solution)/shard_map/ppermute | solution.py:534
  31.1 2.8 %shard_map.90 = (bf16[208,128]{1,0:T(8,128)(2,1)S(1)}, bf16[208,128]{1,0:T(8,128)(2,1)S(1)}) custom-call(s32[8,24]{1,0:T(8,128)S(1)} %get-tuple-element.39.which, bf16[24,2048,128]{2,1,0:T(8,128)(2,1)S(1)} %bitcast.1, bf16[208,128]{1,0:T(8,128)(2,1)S(1)} %collective-permute-done.3.rest_0_, bf16[208,128]{1,0:T(8,128)(2,1)S(1)} %collective-permute-done.4.rest_1_), custom_call_target="tpu_custom_call" | custom-call | flops 805306368 | bytes 4194304 | tf_op jit(solution)/shard_map/pallas_call | solution.py:613
  33.9 0.0 collective-permute-done.6.rest_0_
  33.9 2.3 %collective-permute-start.17 = (bf16[6,128,128]{2,1,0:T(8,128)(2,1)S(1)}, bf16[6,128,128]{2,1,0:T(8,128)(2,1)S(1)}, u32[]{:S(2)}, u32[]{:S(2)}) collective-permute-start(bf16[6,128,128]{2,1,0:T(8,128)(2,1)S(1)} %get-tuple-element.58), channel_id=1, source_target_pairs={{1,2},{2,1},{3,4},{4,3},{5,6},{6,5},{7,8},{8,7},{9,10},{10,9},{11,... | collective-permute-start | bytes 589832 | tf_op jit(solution)/shard_map/ppermute | solution.py:534
  36.2 0.0 collective-permute-done.7.rest_1_
  36.2 2.4 %collective-permute-start.10 = (bf16[208,128]{1,0:T(8,128)(2,1)S(1)}, bf16[208,128]{1,0:T(8,128)(2,1)S(1)}, u32[]{:S(2)}, u32[]{:S(2)}) collective-permute-start(bf16[208,128]{1,0:T(8,128)(2,1)S(1)} %get-tuple-element.50), channel_id=1, source_target_pairs={{0,16},{4,20},{8,24},{12,28},{16,0},{20,4},{24,8},{28,12},{1,17},{... | collective-permute-start | bytes 159752 | tf_op jit(solution)/shard_map/ppermute | solution.py:606
  38.6 2.8 %shard_map.91 = (bf16[208,128]{1,0:T(8,128)(2,1)S(1)}, bf16[208,128]{1,0:T(8,128)(2,1)S(1)}) custom-call(s32[8,24]{1,0:T(8,128)S(1)} %get-tuple-element.39.which, bf16[24,2048,128]{2,1,0:T(8,128)(2,1)S(1)} %bitcast.1, bf16[208,128]{1,0:T(8,128)(2,1)S(1)} %collective-permute-done.6.rest_0_, bf16[208,128]{1,0:T(8,128)(2,1)S(1)} %collective-permute-done.7.rest_1_), custom_call_target="tpu_custom_call" | custom-call | flops 805306368 | bytes 4194304 | tf_op jit(solution)/shard_map/pallas_call | solution.py:613
  41.4 0.0 collective-permute-done.11.rest_0_
  41.4 0.3 collective-permute-start.5
  41.7 0.0 collective-permute-done.12.rest_1_
  41.7 1.7 %collective-permute-start.15 = (bf16[208,128]{1,0:T(8,128)(2,1)S(1)}, bf16[208,128]{1,0:T(8,128)(2,1)S(1)}, u32[]{:S(2)}, u32[]{:S(2)}) collective-permute-start(bf16[208,128]{1,0:T(8,128)(2,1)S(1)} %get-tuple-element.55), channel_id=1, source_target_pairs={{0,28},{4,24},{8,20},{12,16},{16,12},{20,8},{24,4},{28,0},{1,29},{... | collective-permute-start | bytes 159752 | tf_op jit(solution)/shard_map/ppermute | solution.py:606
  43.4 0.0 collective-permute-done.10.rest_4_
  43.4 0.0 collective-permute-start.8
  43.4 2.8 %shard_map.92 = (bf16[208,128]{1,0:T(8,128)(2,1)S(1)}, bf16[208,128]{1,0:T(8,128)(2,1)S(1)}) custom-call(s32[8,24]{1,0:T(8,128)S(1)} %get-tuple-element.39.which, bf16[24,2048,128]{2,1,0:T(8,128)(2,1)S(1)} %bitcast.1, bf16[208,128]{1,0:T(8,128)(2,1)S(1)} %collective-permute-done.11.rest_0_, bf16[208,128]{1,0:T(8,128)(2,1)S(1)} %collective-permute-done.12.rest_1_), custom_call_target="tpu_custom_call" | custom-call | flops 805306368 | bytes 4194304 | tf_op jit(solution)/shard_map/pallas_call | solution.py:613
  46.2 0.0 collective-permute-done.5.rest_1_
  46.2 1.8 %collective-permute-start.9 = (bf16[208,128]{1,0:T(8,128)(2,1)S(1)}, bf16[208,128]{1,0:T(8,128)(2,1)S(1)}, u32[]{:S(2)}, u32[]{:S(2)}) collective-permute-start(bf16[208,128]{1,0:T(8,128)(2,1)S(1)} %get-tuple-element.49), channel_id=1, source_target_pairs={{0,12},{4,8},{8,4},{12,0},{16,28},{20,24},{24,20},{28,16},{1,13},{... | collective-permute-start | bytes 159752 | tf_op jit(solution)/shard_map/ppermute | solution.py:606
  48.0 0.0 collective-permute-done.15.rest_7_
  48.0 2.0 %collective-permute-start.13 = (bf16[208,128]{1,0:T(8,128)(2,1)S(1)}, bf16[208,128]{1,0:T(8,128)(2,1)S(1)}, u32[]{:S(2)}, u32[]{:S(2)}) collective-permute-start(bf16[208,128]{1,0:T(8,128)(2,1)S(1)} %get-tuple-element.53), channel_id=1, source_target_pairs={{0,20},{4,16},{8,28},{12,24},{16,4},{20,0},{24,12},{28,8},{1,21},{... | collective-permute-start | bytes 159752 | tf_op jit(solution)/shard_map/ppermute | solution.py:606
  50.0 0.0 collective-permute-done.8.rest_2_
  50.0 0.7 %collective-permute-start.14 = (bf16[208,128]{1,0:T(8,128)(2,1)S(1)}, bf16[208,128]{1,0:T(8,128)(2,1)S(1)}, u32[]{:S(2)}, u32[]{:S(2)}) collective-permute-start(bf16[208,128]{1,0:T(8,128)(2,1)S(1)} %get-tuple-element.54), channel_id=1, source_target_pairs={{0,24},{4,28},{8,16},{12,20},{16,8},{20,12},{24,0},{28,4},{1,25},{... | collective-permute-start | bytes 159752 | tf_op jit(solution)/shard_map/ppermute | solution.py:606
  50.8 0.0 collective-permute-done.9.rest_3_
  50.8 2.2 %collective-permute-done.13.rest_5_ = bf16[208,128]{1,0:T(8,128)(2,1)S(1)} collective-permute-done((bf16[208,128]{1,0:T(8,128)(2,1)S(1)}, bf16[208,128]{1,0:T(8,128)(2,1)S(1)}, u32[]{:S(2)}, u32[]{:S(2)}) %collective-permute-start.13) | collective-permute-done | bytes 53280 | tf_op jit(solution)/shard_map/ppermute | solution.py:606
  52.9 2.8 %collective-permute-done.14.rest_6_ = bf16[208,128]{1,0:T(8,128)(2,1)S(1)} collective-permute-done((bf16[208,128]{1,0:T(8,128)(2,1)S(1)}, bf16[208,128]{1,0:T(8,128)(2,1)S(1)}, u32[]{:S(2)}, u32[]{:S(2)}) %collective-permute-start.14) | collective-permute-done | bytes 53280 | tf_op jit(solution)/shard_map/ppermute | solution.py:606
  55.7 1.9 %shard_map.93 = (f32[8,128,128]{2,1,0:T(8,128)}, bf16[8,128,128]{2,1,0:T(8,128)(2,1)S(1)}, bf16[1,128,128]{2,1,0:T(8,128)(2,1)S(1)}, bf16[1,128,128]{2,1,0:T(8,128)(2,1)S(1)}) custom-call(s32[8,24]{1,0:T(8,128)S(1)} %get-tuple-element.33.place, bf16[2,8,3,128,128]{4,3,2,1,0:T(8,128)(2,1)S(1)} %copy-done, bf16[208,128]{1,0:T(8,128)(2,1)S(1)} %get-tuple-element.42.rest_0_, ...), custom_call_target="tpu_custom_call" | custom-call | flops 1048576 | bytes 4194304 | tf_op jit(solution)/shard_map/pallas_call | solution.py:625
  57.6 2.6 %collective-permute-start.18 = (bf16[1,128,128]{2,1,0:T(8,128)(2,1)S(1)}, bf16[1,128,128]{2,1,0:T(8,128)(2,1)S(1)}, u32[]{:S(2)}, u32[]{:S(2)}) collective-permute-start(bf16[1,128,128]{2,1,0:T(8,128)(2,1)S(1)} %get-tuple-element.59), channel_id=1, source_target_pairs={{0,1},{1,0},{2,3},{3,2},{4,5},{5,4},{6,7},{7,6},{8,9},{9,8},{10,11... | collective-permute-start | bytes 98312 | tf_op jit(solution)/shard_map/ppermute | solution.py:534
  60.2 2.5 %collective-permute-start.19 = (bf16[1,128,128]{2,1,0:T(8,128)(2,1)S(1)}, bf16[1,128,128]{2,1,0:T(8,128)(2,1)S(1)}, u32[]{:S(2)}, u32[]{:S(2)}) collective-permute-start(bf16[1,128,128]{2,1,0:T(8,128)(2,1)S(1)} %get-tuple-element.60), channel_id=1, source_target_pairs={{1,2},{2,1},{3,4},{4,3},{5,6},{6,5},{7,8},{8,7},{9,10},{10,9},{11,... | collective-permute-start | bytes 98312 | tf_op jit(solution)/shard_map/ppermute | solution.py:534
  62.7 0.0 collective-permute-done.16.half_a
  62.7 0.0 collective-permute-done.17.half_b
  62.7 5.3 %shard_map.94 = (bf16[2,8,3,128,128]{4,3,2,1,0:T(8,128)(2,1)}, bf16[10,3,128,256]{3,2,1,0:T(8,128)(2,1)S(1)}) custom-call(s32[8]{0:T(128)S(1)} %copy-done.4, f32[8]{0:T(128)S(1)} %copy-done.5, bf16[2,8,3,128,128]{4,3,2,1,0:T(8,128)(2,1)S(1)} %get-tuple-element.38.half, bf16[2,8,3,128,128]{4,3,2,1,0:T(8,128)(2,1)S(1)} %copy-done, ...), custom_call_target="tpu_custom_call" | custom-call | flops 4294967296 | bytes 4194304 | tf_op jit(solution)/shard_map/pallas_call | solution.py:642
  68.1 0.0 collective-permute-done.18.diag_a
  68.1 0.0 collective-permute-done.19.diag_b
  68.1 2.6 %shard_map.95 = bf16[2,8,3,128,128]{4,3,2,1,0:T(8,128)(2,1)} custom-call(s32[8]{0:T(128)S(1)} %copy-done.4, f32[8]{0:T(128)S(1)} %copy-done.5, bf16[2,8,3,128,128]{4,3,2,1,0:T(8,128)(2,1)S(1)} %get-tuple-element.38.half, bf16[2,8,3,128,128]{4,3,2,1,0:T(8,128)(2,1)S(1)} %copy-done, ...), custom_call_target="tpu_custom_call", output_to_operand_aliasing={{}: (12, {})} | custom-call | flops 4294967296 | bytes 4194304 | tf_op jit(solution)/shard_map/pallas_call | solution.py:651
  (5 shorter events, 0.0 us)
Async XLA Ops:
  0.6 6.2 %copy-start = (bf16[2,8,3,128,128]{4,3,2,1,0:T(8,128)(2,1)S(1)}, bf16[2,8,3,128,128]{4,3,2,1,0:T(8,128)(2,1)}, u32[]{:S(2)}) copy-start(bf16[2,8,3,128,128]{4,3,2,1,0:T(8,128)(2,1)} %core.11) | copy-start | bytes 4718596
  0.6 6.2 %copy-start.2 = (f32[8,128,128]{2,1,0:T(8,128)S(1)}, f32[8,128,128]{2,1,0:T(8,128)}, u32[]{:S(2)}) copy-start(f32[8,128,128]{2,1,0:T(8,128)} %grid_old.5) | copy-start | bytes 1572868
  0.7 6.2 %copy-start.1 = (bf16[2,8,3,128,128]{4,3,2,1,0:T(8,128)(2,1)S(1)}, bf16[2,8,3,128,128]{4,3,2,1,0:T(8,128)(2,1)}, u32[]{:S(2)}) copy-start(bf16[2,8,3,128,128]{4,3,2,1,0:T(8,128)(2,1)} %dens.5) | copy-start | bytes 4718596
  0.7 6.2 %copy-start.5 = (f32[8]{0:T(128)S(1)}, f32[8]{0:T(128)}, u32[]{:S(2)}) copy-start(f32[8]{0:T(128)} %absorption.7) | copy-start | bytes 100
  0.7 6.2 %copy-start.4 = (s32[8]{0:T(128)S(1)}, s32[8]{0:T(128)}, u32[]{:S(2)}) copy-start(s32[8]{0:T(128)} %leads.7) | copy-start | bytes 100
  2.2 8.4 %collective-permute-start = (bf16[6,128,128]{2,1,0:T(8,128)(2,1)S(1)}, bf16[6,128,128]{2,1,0:T(8,128)(2,1)S(1)}, u32[]{:S(2)}, u32[]{:S(2)}) collective-permute-start(bf16[6,128,128]{2,1,0:T(8,128)(2,1)S(1)} %get-tuple-element.34), channel_id=1, source_target_pairs={{0,1},{1,0},{2,3},{3,2},{4,5},{5,4},{6,7},{7,6},{8,9},{9,8},{10,11... | collective-permute-start | bytes 589832 | tf_op jit(solution)/shard_map/ppermute | solution.py:534
  2.3 9.0 %collective-permute-start.1 = (bf16[6,128,128]{2,1,0:T(8,128)(2,1)S(1)}, bf16[6,128,128]{2,1,0:T(8,128)(2,1)S(1)}, u32[]{:S(2)}, u32[]{:S(2)}) collective-permute-start(bf16[6,128,128]{2,1,0:T(8,128)(2,1)S(1)} %get-tuple-element.35), channel_id=1, source_target_pairs={{1,2},{2,1},{3,4},{4,3},{5,6},{6,5},{7,8},{8,7},{9,10},{10,9},{11,... | collective-permute-start | bytes 589832 | tf_op jit(solution)/shard_map/ppermute | solution.py:534
  6.9 0.7 copy-start.3
  7.6 17.2 %slice-start = ((s8[12582912]{0:T(1024)(128)(4,1)}), s8[4194304]{0:T(1024)(128)(4,1)S(1)}, s32[]{:S(2)}) async-start(s8[12582912]{0:T(1024)(128)(4,1)} %bitcast), calls=%async_computation | async-start | bytes 8388608
  7.6 17.2 %slice-start.1 = ((s8[12582912]{0:T(1024)(128)(4,1)}), s8[4194304]{0:T(1024)(128)(4,1)S(1)}, s32[]{:S(2)}) async-start(s8[12582912]{0:T(1024)(128)(4,1)} %bitcast), calls=%async_computation.1 | async-start | bytes 8388608
  11.4 13.4 %slice-start.2 = ((s8[12582912]{0:T(1024)(128)(4,1)}), s8[4194304]{0:T(1024)(128)(4,1)S(1)}, s32[]{:S(2)}) async-start(s8[12582912]{0:T(1024)(128)(4,1)} %bitcast), calls=%async_computation.2 | async-start | bytes 8388608
  14.8 8.8 %collective-permute-start.2 = (bf16[208,128]{1,0:T(8,128)(2,1)S(1)}, bf16[208,128]{1,0:T(8,128)(2,1)S(1)}, u32[]{:S(2)}, u32[]{:S(2)}) collective-permute-start(bf16[208,128]{1,0:T(8,128)(2,1)S(1)} %get-tuple-element.41), channel_id=1, source_target_pairs={{0,16},{4,20},{8,24},{12,28},{16,0},{20,4},{24,8},{28,12},{1,17},{... | collective-permute-start | bytes 159752 | tf_op jit(solution)/shard_map/ppermute | solution.py:606
  18.4 9.2 %collective-permute-start.3 = (bf16[208,128]{1,0:T(8,128)(2,1)S(1)}, bf16[208,128]{1,0:T(8,128)(2,1)S(1)}, u32[]{:S(2)}, u32[]{:S(2)}) collective-permute-start(bf16[208,128]{1,0:T(8,128)(2,1)S(1)} %get-tuple-element.43), channel_id=1, source_target_pairs={{0,28},{4,24},{8,20},{12,16},{16,12},{20,8},{24,4},{28,0},{1,29},{... | collective-permute-start | bytes 159752 | tf_op jit(solution)/shard_map/ppermute | solution.py:606
  21.0 8.9 %collective-permute-start.4 = (bf16[208,128]{1,0:T(8,128)(2,1)S(1)}, bf16[208,128]{1,0:T(8,128)(2,1)S(1)}, u32[]{:S(2)}, u32[]{:S(2)}) collective-permute-start(bf16[208,128]{1,0:T(8,128)(2,1)S(1)} %get-tuple-element.44), channel_id=1, source_target_pairs={{0,4},{4,0},{8,12},{12,8},{16,20},{20,16},{24,28},{28,24},{1,5},{5... | collective-permute-start | bytes 159752 | tf_op jit(solution)/shard_map/ppermute | solution.py:606
  21.0 12.9 %collective-permute-start.6 = (bf16[208,128]{1,0:T(8,128)(2,1)S(1)}, bf16[208,128]{1,0:T(8,128)(2,1)S(1)}, u32[]{:S(2)}, u32[]{:S(2)}) collective-permute-start(bf16[208,128]{1,0:T(8,128)(2,1)S(1)} %get-tuple-element.46), channel_id=1, source_target_pairs={{0,8},{4,12},{8,0},{12,4},{16,24},{20,28},{24,16},{28,20},{1,9},{5... | collective-permute-start | bytes 159752 | tf_op jit(solution)/shard_map/ppermute | solution.py:606
  21.5 14.7 %collective-permute-start.7 = (bf16[208,128]{1,0:T(8,128)(2,1)S(1)}, bf16[208,128]{1,0:T(8,128)(2,1)S(1)}, u32[]{:S(2)}, u32[]{:S(2)}) collective-permute-start(bf16[208,128]{1,0:T(8,128)(2,1)S(1)} %get-tuple-element.47), channel_id=1, source_target_pairs={{0,12},{4,8},{8,4},{12,0},{16,28},{20,24},{24,20},{28,16},{1,13},{... | collective-permute-start | bytes 159752 | tf_op jit(solution)/shard_map/ppermute | solution.py:606
  23.6 17.8 %collective-permute-start.11 = (bf16[208,128]{1,0:T(8,128)(2,1)S(1)}, bf16[208,128]{1,0:T(8,128)(2,1)S(1)}, u32[]{:S(2)}, u32[]{:S(2)}) collective-permute-start(bf16[208,128]{1,0:T(8,128)(2,1)S(1)} %get-tuple-element.51), channel_id=1, source_target_pairs={{0,20},{4,16},{8,28},{12,24},{16,4},{20,0},{24,12},{28,8},{1,21},{... | collective-permute-start | bytes 159752 | tf_op jit(solution)/shard_map/ppermute | solution.py:606
  27.6 14.1 %collective-permute-start.12 = (bf16[208,128]{1,0:T(8,128)(2,1)S(1)}, bf16[208,128]{1,0:T(8,128)(2,1)S(1)}, u32[]{:S(2)}, u32[]{:S(2)}) collective-permute-start(bf16[208,128]{1,0:T(8,128)(2,1)S(1)} %get-tuple-element.52), channel_id=1, source_target_pairs={{0,24},{4,28},{8,16},{12,20},{16,8},{20,12},{24,0},{28,4},{1,25},{... | collective-permute-start | bytes 159752 | tf_op jit(solution)/shard_map/ppermute | solution.py:606
  29.9 32.8 %collective-permute-start.16 = (bf16[6,128,128]{2,1,0:T(8,128)(2,1)S(1)}, bf16[6,128,128]{2,1,0:T(8,128)(2,1)S(1)}, u32[]{:S(2)}, u32[]{:S(2)}) collective-permute-start(bf16[6,128,128]{2,1,0:T(8,128)(2,1)S(1)} %get-tuple-element.57), channel_id=1, source_target_pairs={{0,1},{1,0},{2,3},{3,2},{4,5},{5,4},{6,7},{7,6},{8,9},{9,8},{10,11... | collective-permute-start | bytes 589832 | tf_op jit(solution)/shard_map/ppermute | solution.py:534
  33.9 28.8 %collective-permute-start.17 = (bf16[6,128,128]{2,1,0:T(8,128)(2,1)S(1)}, bf16[6,128,128]{2,1,0:T(8,128)(2,1)S(1)}, u32[]{:S(2)}, u32[]{:S(2)}) collective-permute-start(bf16[6,128,128]{2,1,0:T(8,128)(2,1)S(1)} %get-tuple-element.58), channel_id=1, source_target_pairs={{1,2},{2,1},{3,4},{4,3},{5,6},{6,5},{7,8},{8,7},{9,10},{10,9},{11,... | collective-permute-start | bytes 589832 | tf_op jit(solution)/shard_map/ppermute | solution.py:534
  36.2 7.2 %collective-permute-start.10 = (bf16[208,128]{1,0:T(8,128)(2,1)S(1)}, bf16[208,128]{1,0:T(8,128)(2,1)S(1)}, u32[]{:S(2)}, u32[]{:S(2)}) collective-permute-start(bf16[208,128]{1,0:T(8,128)(2,1)S(1)} %get-tuple-element.50), channel_id=1, source_target_pairs={{0,16},{4,20},{8,24},{12,28},{16,0},{20,4},{24,8},{28,12},{1,17},{... | collective-permute-start | bytes 159752 | tf_op jit(solution)/shard_map/ppermute | solution.py:606
  41.4 4.8 %collective-permute-start.5 = (bf16[208,128]{1,0:T(8,128)(2,1)S(1)}, bf16[208,128]{1,0:T(8,128)(2,1)S(1)}, u32[]{:S(2)}, u32[]{:S(2)}) collective-permute-start(bf16[208,128]{1,0:T(8,128)(2,1)S(1)} %get-tuple-element.45), channel_id=1, source_target_pairs={{0,4},{4,0},{8,12},{12,8},{16,20},{20,16},{24,28},{28,24},{1,5},{5... | collective-permute-start | bytes 159752 | tf_op jit(solution)/shard_map/ppermute | solution.py:606
  41.7 6.4 %collective-permute-start.15 = (bf16[208,128]{1,0:T(8,128)(2,1)S(1)}, bf16[208,128]{1,0:T(8,128)(2,1)S(1)}, u32[]{:S(2)}, u32[]{:S(2)}) collective-permute-start(bf16[208,128]{1,0:T(8,128)(2,1)S(1)} %get-tuple-element.55), channel_id=1, source_target_pairs={{0,28},{4,24},{8,20},{12,16},{16,12},{20,8},{24,4},{28,0},{1,29},{... | collective-permute-start | bytes 159752 | tf_op jit(solution)/shard_map/ppermute | solution.py:606
  43.4 6.6 %collective-permute-start.8 = (bf16[208,128]{1,0:T(8,128)(2,1)S(1)}, bf16[208,128]{1,0:T(8,128)(2,1)S(1)}, u32[]{:S(2)}, u32[]{:S(2)}) collective-permute-start(bf16[208,128]{1,0:T(8,128)(2,1)S(1)} %get-tuple-element.48), channel_id=1, source_target_pairs={{0,8},{4,12},{8,0},{12,4},{16,24},{20,28},{24,16},{28,20},{1,9},{5... | collective-permute-start | bytes 159752 | tf_op jit(solution)/shard_map/ppermute | solution.py:606
  46.2 4.5 %collective-permute-start.9 = (bf16[208,128]{1,0:T(8,128)(2,1)S(1)}, bf16[208,128]{1,0:T(8,128)(2,1)S(1)}, u32[]{:S(2)}, u32[]{:S(2)}) collective-permute-start(bf16[208,128]{1,0:T(8,128)(2,1)S(1)} %get-tuple-element.49), channel_id=1, source_target_pairs={{0,12},{4,8},{8,4},{12,0},{16,28},{20,24},{24,20},{28,16},{1,13},{... | collective-permute-start | bytes 159752 | tf_op jit(solution)/shard_map/ppermute | solution.py:606
  48.0 4.9 %collective-permute-start.13 = (bf16[208,128]{1,0:T(8,128)(2,1)S(1)}, bf16[208,128]{1,0:T(8,128)(2,1)S(1)}, u32[]{:S(2)}, u32[]{:S(2)}) collective-permute-start(bf16[208,128]{1,0:T(8,128)(2,1)S(1)} %get-tuple-element.53), channel_id=1, source_target_pairs={{0,20},{4,16},{8,28},{12,24},{16,4},{20,0},{24,12},{28,8},{1,21},{... | collective-permute-start | bytes 159752 | tf_op jit(solution)/shard_map/ppermute | solution.py:606
  50.0 5.6 %collective-permute-start.14 = (bf16[208,128]{1,0:T(8,128)(2,1)S(1)}, bf16[208,128]{1,0:T(8,128)(2,1)S(1)}, u32[]{:S(2)}, u32[]{:S(2)}) collective-permute-start(bf16[208,128]{1,0:T(8,128)(2,1)S(1)} %get-tuple-element.54), channel_id=1, source_target_pairs={{0,24},{4,28},{8,16},{12,20},{16,8},{20,12},{24,0},{28,4},{1,25},{... | collective-permute-start | bytes 159752 | tf_op jit(solution)/shard_map/ppermute | solution.py:606
  57.6 10.5 %collective-permute-start.18 = (bf16[1,128,128]{2,1,0:T(8,128)(2,1)S(1)}, bf16[1,128,128]{2,1,0:T(8,128)(2,1)S(1)}, u32[]{:S(2)}, u32[]{:S(2)}) collective-permute-start(bf16[1,128,128]{2,1,0:T(8,128)(2,1)S(1)} %get-tuple-element.59), channel_id=1, source_target_pairs={{0,1},{1,0},{2,3},{3,2},{4,5},{5,4},{6,7},{7,6},{8,9},{9,8},{10,11... | collective-permute-start | bytes 98312 | tf_op jit(solution)/shard_map/ppermute | solution.py:534
  60.2 7.9 %collective-permute-start.19 = (bf16[1,128,128]{2,1,0:T(8,128)(2,1)S(1)}, bf16[1,128,128]{2,1,0:T(8,128)(2,1)S(1)}, u32[]{:S(2)}, u32[]{:S(2)}) collective-permute-start(bf16[1,128,128]{2,1,0:T(8,128)(2,1)S(1)} %get-tuple-element.60), channel_id=1, source_target_pairs={{1,2},{2,1},{3,4},{4,3},{5,6},{6,5},{7,8},{8,7},{9,10},{10,9},{11,... | collective-permute-start | bytes 98312 | tf_op jit(solution)/shard_map/ppermute | solution.py:534

commit v3 on v2

--- a/solution.py
+++ b/solution.py
@@ -18,7 +18,7 @@
 TILE = 16
 
 
-def call(kernel, out_shape, flops, vmem, scalars=0, grid=(), in_specs=None, out_specs=None, scratch=(), aliases={}):
+def call(kernel, out_shape, flops, vmem, scalars=0, grid=(), in_specs=None, out_specs=None, scratch=()):
     whole = pl.BlockSpec(memory_space=pltpu.VMEM)
     return pl.pallas_call(
         kernel,
@@ -30,7 +30,6 @@
             out_specs=jax.tree.map(lambda _: whole, out_shape) if out_specs is None else out_specs,
             scratch_shapes=scratch,
         ),
-        input_output_aliases=aliases,
         compiler_params=pltpu.CompilerParams(vmem_limit_bytes=vmem * MIB),
         cost_estimate=pl.CostEstimate(flops=flops, bytes_accessed=4 << 20, transcendentals=0),
     )
@@ -184,6 +183,12 @@
             send_b[n] = x
 
 
+def partner(orders, n):
+    even, odd = orders[0][n], orders[1][n]
+    offset = even if even == odd else jnp.where(lax.axis_index("col") % 2 == 0, even, odd)
+    return lax.axis_index("row") ^ offset
+
+
 def halo_reader(got_a, got_b):
     even = lax.axis_index("col") % 2 == 0
 
@@ -215,11 +220,11 @@
     return lambda i, j: joined(ref[0, i, j - i + 1], ref[1, i, j - i + 1])
 
 
-def band_writer(ref):
+def band_writer(ref, first=0):
     def write(i, j, value):
         width = value.shape[0]
-        ref[0, i, j - i + 1] = value[:, :width]
-        ref[1, i, j - i + 1] = value[:, width:]
+        ref[0, i - first, j - i + 1] = value[:, :width]
+        ref[1, i - first, j - i + 1] = value[:, width:]
 
     return write
 
@@ -267,6 +272,14 @@
         return joined(core[0, i, j - i + 1], core[1, i, j - i + 1])
 
     return get
+
+
+def put_half(count, half, target, start, right):
+    last = count - 1
+    blocks = [(last, 1), (last, 2), (last - 1, 2)] if right else [(0, 1), (0, 0), (1, 0)]
+    for n, (i, k) in enumerate(blocks):
+        for part in range(2):
+            target[start + 2 * n + part] = half[part, i, k]
 
 
 def brick_tables(count, owners, place, which):
@@ -304,8 +317,8 @@
     propagate([(2, count - 3)], get_q, get_hp, get_left, get_right, moved_ref, wh_ref, band_writer(half))
 
 
-def first_outer_kernel(count, leads, absorption, place, dens, core, grid_old, got_a, got_b, hp_in, half_in,
-                       half, send_a, send_b, *rest):
+def first_outer_kernel(count, orders, leads, absorption, place, dens, core, grid_old, got_a, got_b, hp_in, half_in,
+                       half, send_b, *rest):
     outgoing, (hp_ref, moved_ref, wh_ref, left_ref, right_ref, edges, packed, diagonals) = rest[:-8], rest[-8:]
     low, high = halo_reader(got_a, got_b)
     last = count - 1
@@ -348,24 +361,15 @@
     taylor_first(range(last - 1, count + 1), last, count, get_left, get_q, hp_ref)
     propagate([(0, 1), (last - 1, last)], get_q, get_hp, get_left, get_right, moved_ref, wh_ref, write)
 
-    right = [(last, 1), (last, 2), (last - 1, 2)]
-    left = [(0, 1), (0, 0), (1, 0)]
-
-    def send(to_a, to_b):
-        for n in range(3):
-            for part in range(2):
-                send_a[2 * n + part] = half[part, to_a[n][0], to_a[n][1]]
-                send_b[2 * n + part] = half[part, to_b[n][0], to_b[n][1]]
-
     even = lax.axis_index("col") % 2 == 0
 
     @pl.when(even)
     def _():
-        send(right, left)
+        put_half(count, half, send_b, 0, False)
 
     @pl.when(jnp.logical_not(even))
     def _():
-        send(left, right)
+        put_half(count, half, send_b, 0, True)
 
     for i in range(count):
         top, diagonal = pack_symmetric(half[0, i, 1].astype(F32), True)
@@ -375,8 +379,8 @@
     height, width = packed.shape[1:]
     _, row = lanes_rows((TILE, width))
 
-    for offset, out in enumerate(outgoing):
-        p = lax.axis_index("row") ^ offset
+    for number, out in enumerate(outgoing):
+        p = partner(orders, number)
         tail = jnp.zeros((TILE, width), F32)
         for n in range(CAP):
             source = jnp.maximum(place[p, n], 0)
@@ -385,14 +389,14 @@
         out[CAP * height :] = tail.astype(BF16)
 
 
-def brick_kernel(chunk, offsets, which, colloc, *rest):
-    incoming, returned = rest[: len(offsets)], rest[len(offsets) :]
+def brick_kernel(chunk, orders, numbers, which, colloc, unread, *rest):
+    incoming, returned = rest[: len(numbers)], rest[len(numbers) :]
     points, width = colloc.shape[1:]
     scale = GRID_FACTOR * width / points
     height = width // 2
     _, tail_row = lanes_rows((TILE, width))
-    tails = [jnp.zeros((TILE, width), F32) for _ in offsets]
-    jobs = [(m, n, which[lax.axis_index("row") ^ offset, n]) for m, offset in enumerate(offsets) for n in range(CAP)]
+    tails = [jnp.zeros((TILE, width), F32) for _ in numbers]
+    jobs = [(m, n, which[partner(orders, number), n]) for m, number in enumerate(numbers) for n in range(CAP)]
 
     def block(job):
         m, n, _ = job
@@ -429,14 +433,14 @@
         out[CAP * height :] = tail.astype(BF16)
 
 
-def collect_kernel(count, place, core, *rest):
-    arriving, (grid_term, diag_new, send_a, send_b, total, tails) = rest[:-6], rest[-6:]
+def collect_kernel(count, orders, place, core, half, *rest):
+    arriving, (term, diag_new, send_a, send_b, total, tails) = rest[:-6], rest[-6:]
     width = core.shape[-1]
     height = width // 2
     total[...] = jnp.zeros_like(total)
     tails[...] = jnp.zeros_like(tails)
-    for offset, block in enumerate(arriving):
-        p = lax.axis_index("row") ^ offset
+    for number, block in enumerate(arriving):
+        p = partner(orders, number)
         last = block[CAP * height :].astype(F32)
         for n in range(CAP):
             at = place[p, n]
@@ -447,55 +451,69 @@
     lane, row = lanes_rows((width, width))
     for i in range(count):
         triangle = unpack_triangle(total[i], tails[i][:1])
-        term = jnp.where(lane == row, triangle, triangle + triangle.T)
-        grid_term[i] = term
-        diag_new[i] = (core[0, i, 0].astype(F32) + term).astype(BF16)
-    right, left = diag_new[count - 1], diag_new[0]
+        whole = jnp.where(lane == row, triangle, triangle + triangle.T)
+        term[i] = whole
+        diag_new[i] = (core[0, i, 0].astype(F32) + whole).astype(BF16)
+
     even = lax.axis_index("col") % 2 == 0
-    send_a[0] = jnp.where(even, right, left)
-    send_b[0] = jnp.where(even, left, right)
-
-
-def half_access(count, half, half_a, half_b):
-    low, high = halo_reader(half_a, half_b)
-
-    def get_q(i, j):
-        if i < 0:
-            n = 0 if i == -1 and j == -1 else 2 if i == -1 else 4
-            return joined(low(n), low(n + 1))
-        if i >= count:
-            n = 0 if i == count and j == count else 2 if i == count else 4
-            return joined(high(n), high(n + 1))
-        return band_at(half)(i, j)
-
-    return get_q
-
-
-def second_inner_kernel(count, leads, absorption, half, core, diag_new, half_a, half_b,
-                        out, hp_ref, moved_ref, wh_ref, left_ref, right_ref):
+    last = count - 1
+
+    @pl.when(even)
+    def _():
+        send_a[0] = diag_new[last]
+        send_b[0] = diag_new[0]
+        put_half(count, half, send_a, 1, True)
+
+    @pl.when(jnp.logical_not(even))
+    def _():
+        send_a[0] = diag_new[0]
+        send_b[0] = diag_new[last]
+        put_half(count, half, send_a, 1, False)
+
+
+def second_inner_kernel(count, leads, absorption, half, core, diag_new, term, out, hp_ref, grid_term,
+                        moved_ref, wh_ref, left_ref, right_ref, sem):
+    copy = pltpu.make_async_copy(term, grid_term, sem.at[0])
+    copy.start()
     new_diagonals(range(count), count, leads, absorption, core, diag_new, left_ref, right_ref)
     get_left = band_access(count, core, None, None, None, None, left_ref)
     get_right = band_access(count, core, None, None, None, None, right_ref)
-    get_q = half_access(count, half, half_a, half_b)
+    get_q = band_at(half)
 
     def get_hp(i, j):
         return hp_ref[i + 1, j - i + 1]
 
-    taylor_first(range(-1, count + 1), 0, count - 1, get_left, get_q, hp_ref)
-    propagate([(1, count - 2)], get_q, get_hp, get_left, get_right, moved_ref, wh_ref, band_writer(out))
-
-
-def second_outer_kernel(count, leads, absorption, half, core, diag_new, core_a, core_b, half_a, half_b, diag_a, diag_b,
-                        hp_in, out_in, out, hp_ref, moved_ref, wh_ref, left_ref, right_ref, edges, ready, sems):
+    taylor_first(range(count), 1, count - 2, get_left, get_q, hp_ref)
+    propagate([(2, count - 3)], get_q, get_hp, get_left, get_right, moved_ref, wh_ref, band_writer(out, 2))
+    copy.wait()
+
+
+def second_outer_kernel(count, leads, absorption, half, core, diag_new, core_a, core_b, got_a, got_b, half_b,
+                        hp_in, inner, out, hp_ref, moved_ref, wh_ref, left_ref, right_ref, edges, ready, sems):
+    copies = [pltpu.make_async_copy(inner, out.at[:, pl.ds(2, count - 4)], sems.at[2])]
+    copies[0].start()
     core_low, core_high = halo_reader(core_a, core_b)
-    diag_low, diag_high = halo_reader(diag_a, diag_b)
+    even = lax.axis_index("col") % 2 == 0
+
+    def low(n):
+        return jnp.where(even, got_b[0] if n == 0 else half_b[n - 1], got_a[n])
+
+    def high(n):
+        return jnp.where(even, got_a[n], got_b[0] if n == 0 else half_b[n - 1])
+
     last = count - 1
     edges[0] = dagger(band_at(core)(0, -1))
     edges[1] = dagger(band_at(core)(last, count))
     ends = unpack_hermitian(core_low(3)), unpack_hermitian(core_high(3))
-    rows = [-1, 0, 1, count - 2, last, count]
-    new_diagonals(rows, count, leads, absorption, core, diag_new, left_ref, right_ref, ends, (diag_low(0), diag_high(0)))
-    get_q = half_access(count, half, half_a, half_b)
+    rows = [-1, 0, 1, 2, count - 3, count - 2, last, count]
+    new_diagonals(rows, count, leads, absorption, core, diag_new, left_ref, right_ref, ends, (low(0), high(0)))
+
+    def get_q(i, j):
+        if 0 <= i < count:
+            return band_at(half)(i, j)
+        n = 1 if i == j else 3 if i in (-1, count) else 5
+        side = low if i < 0 else high
+        return joined(side(n), side(n + 1))
 
     def far_low():
         return joined(core_low(4), core_low(5))
@@ -507,38 +525,41 @@
     get_right = band_access(count, core, far_low, far_high, edges.at[0], edges.at[1], right_ref)
 
     def get_hp(i, j):
-        ref = hp_in if 0 <= i < count else hp_ref
+        ref = hp_in if 1 <= i <= count - 2 else hp_ref
         return ref[i + 1, j - i + 1]
 
     def write(i, j, value):
         width = value.shape[0]
-        n = 0 if i == 0 else 1
+        n = i if i < 2 else i - count + 4
         ready[0, n, j - i + 1] = value[:, :width]
         ready[1, n, j - i + 1] = value[:, width:]
 
-    taylor_first(range(-1, 1), -1, -1, get_left, get_q, hp_ref)
-    taylor_first(range(last, count + 1), count, count, get_left, get_q, hp_ref)
-    propagate([(0, 0), (last, last)], get_q, get_hp, get_left, get_right, moved_ref, wh_ref, write)
-    copies = []
-    for n, i in enumerate((0, last)):
-        copies.append(pltpu.make_async_copy(ready.at[:, n], out.at[:, i], sems.at[n]))
+    taylor_first(range(-1, 2), -1, 0, get_left, get_q, hp_ref)
+    taylor_first(range(last - 1, count + 1), last, count, get_left, get_q, hp_ref)
+    propagate([(0, 1), (last - 1, last)], get_q, get_hp, get_left, get_right, moved_ref, wh_ref, write)
+    for n, i in enumerate((0, last - 1)):
+        copies.append(pltpu.make_async_copy(ready.at[:, pl.ds(2 * n, 2)], out.at[:, pl.ds(i, 2)], sems.at[n]))
         copies[-1].start()
     for copy in copies:
         copy.wait()
 
 
-def exchange(send_a, send_b, total):
-    first = [(i, i ^ 1) for i in range(total)]
-    second = [(i, i + 1) if i % 2 else (i, i - 1) for i in range(1, total - 1)]
-    axes = ("row", "col")
-    return lax.ppermute(send_a, axes, first), lax.ppermute(send_b, axes, second)
+def exchange_a(x, total):
+    return lax.ppermute(x, ("row", "col"), [(i, i ^ 1) for i in range(total)])
+
+
+def exchange_b(x, total):
+    return lax.ppermute(x, ("row", "col"), [(i, i + 1) if i % 2 else (i, i - 1) for i in range(1, total - 1)])
 
 
 def shards(density, core, grid_old, lead_blocks, absorption, collocation, brick_block):
     count = density.shape[1]
     width = density.shape[-1]
     row_size = lax.axis_size("row")
-    total = row_size * lax.axis_size("col")
+    col_size = lax.axis_size("col")
+    total = row_size * col_size
+    near, far = list(range(1, row_size // 2)), list(range(row_size // 2, row_size))
+    orders = [[0] + far + near, [0] + far + near]
     bricks = brick_block.shape[1]
     vmem = pl.BlockSpec(memory_space=pltpu.VMEM)
     hbm = pl.BlockSpec(memory_space=pltpu.HBM)
@@ -557,7 +578,7 @@
             pltpu.SemaphoreType.DMA((10,)),
         ],
     )(*(in_hbm(x) for x in (density, core, grid_old)))
-    got_a, got_b = exchange(send_a, send_b, total)
+    got_a, got_b = exchange_a(send_a, total), exchange_b(send_b, total)
 
     def band_scratch(rows):
         return pltpu.VMEM((rows, 3, width, 2 * width), BF16)
@@ -580,11 +601,10 @@
     packed_rows = CAP * width // 2 + TILE
     packed_shape = jax.ShapeDtypeStruct((packed_rows, width), BF16)
     half_message = jax.ShapeDtypeStruct((6, width, width), BF16)
-    half, send_a, send_b, *outgoing = call(
-        functools.partial(first_outer_kernel, count),
+    half, send_b, *outgoing = call(
+        functools.partial(first_outer_kernel, count, orders),
         (
             jax.ShapeDtypeStruct(density.shape, BF16),
-            half_message,
             half_message,
         )
         + (packed_shape,) * row_size,
@@ -600,65 +620,74 @@
         ],
     )(lead_blocks, absorption, place, density, core, grid_old, got_a, got_b, hp, half_inner)
 
-    half_a, half_b = exchange(send_a, send_b, total)
-
-    def across(x, offset):
-        return lax.ppermute(x, "row", [(i, i ^ offset) for i in range(row_size)]) if offset else x
-
-    order = [0] + list(range(row_size // 2, row_size)) + list(range(1, row_size // 2))
-    incoming = {offset: across(outgoing[offset], offset) for offset in order}
+
+    def across(x, number):
+        if number == 0:
+            return x
+        pairs = []
+        for row in range(row_size):
+            for col in range(col_size):
+                pairs.append((row * col_size + col, (row ^ orders[col % 2][number]) * col_size + col))
+        return lax.ppermute(x, ("row", "col"), pairs)
+
+    half_b = exchange_b(send_b, total)
+    incoming = [across(x, number) for number, x in enumerate(outgoing)]
     points = collocation.shape[1]
-    arriving = {}
-    for offsets in zip(order[::2], order[1::2]):
+    arriving = []
+    before = which
+    for numbers in zip(range(0, row_size, 2), range(1, row_size, 2)):
         returned = call(
-            functools.partial(brick_kernel, points // 4, offsets),
+            functools.partial(brick_kernel, points // 4, orders, numbers),
             (packed_shape,) * 2,
             flops=4 * 6 * points * width**2,
             vmem=8,
             scalars=1,
-            in_specs=[vmem] * 3,
-        )(which, collocation, *(incoming[offset] for offset in offsets))
-        for offset, x in zip(offsets, returned):
-            arriving[offset] = across(x, offset)
-
-    diag_message = jax.ShapeDtypeStruct((1, width, width), BF16)
-    grid_term, diag_new, send_a, send_b = call(
-        functools.partial(collect_kernel, count),
+            in_specs=[vmem, pl.BlockSpec(memory_space=pl.ANY), vmem, vmem],
+        )(which, collocation, before, *(incoming[number] for number in numbers))
+        arriving += [across(x, number) for number, x in zip(numbers, returned)]
+        before = returned[0]
+
+    term, diag_new, send_a, send_b = call(
+        functools.partial(collect_kernel, count, orders),
         (
             jax.ShapeDtypeStruct((count, width, width), F32),
             jax.ShapeDtypeStruct((count, width, width), BF16),
-            diag_message,
-            diag_message,
+            jax.ShapeDtypeStruct((7, width, width), BF16),
+            jax.ShapeDtypeStruct((1, width, width), BF16),
         ),
         flops=1 << 20,
         vmem=8,
         scalars=1,
         grid=(1,),
-        in_specs=[block_spec((1, count, 1, width, width), (0, 0, 1, 0, 0))] + [vmem] * row_size,
+        in_specs=[block_spec((1, count, 1, width, width), (0, 0, 1, 0, 0))] + [vmem] * (row_size + 1),
         scratch=[pltpu.VMEM((count, width // 2, width), F32), pltpu.VMEM((count, 8, width), F32)],
-    )(place, core, *(arriving[offset] for offset in range(row_size)))
-    diag_a, diag_b = exchange(send_a, send_b, total)
-
-    inner, hp = call(
+    )(place, core, half, *arriving)
+    half_a, diag_b = exchange_a(send_a, total), exchange_b(send_b, total)
+
+    inner, hp, grid_term = call(
         functools.partial(second_inner_kernel, count),
-        (jax.ShapeDtypeStruct(density.shape, BF16), hp_shape),
+        (
+            jax.ShapeDtypeStruct((2, count - 4, 3, width, width), BF16),
+            hp_shape,
+            pltpu.HBM((count, width, width), F32),
+        ),
         flops=PROP_FLOPS,
         vmem=16,
         scalars=2,
-        in_specs=[vmem] * 5,
-        scratch=inner_scratch,
-    )(lead_blocks, absorption, half, core, diag_new, half_a, half_b)
+        in_specs=[vmem] * 4,
+        out_specs=(vmem, vmem, hbm),
+        scratch=inner_scratch + [pltpu.SemaphoreType.DMA((1,))],
+    )(lead_blocks, absorption, half, core, diag_new, term)
     density_next = call(
         functools.partial(second_outer_kernel, count),
         pltpu.HBM(density.shape, BF16),
         flops=PROP_FLOPS,
         vmem=16,
         scalars=2,
-        in_specs=[vmem] * 10 + [hbm],
+        in_specs=[vmem] * 10,
         out_specs=hbm,
-        scratch=outer_scratch + [sides(2), pltpu.VMEM((2, 2, 3, width, width), BF16), pltpu.SemaphoreType.DMA((2,))],
-        aliases={12: 0},
-    )(lead_blocks, absorption, half, core, diag_new, got_a, got_b, half_a, half_b, diag_a, diag_b, hp, in_hbm(inner))
+        scratch=outer_scratch + [sides(2), pltpu.VMEM((2, 4, 3, width, width), BF16), pltpu.SemaphoreType.DMA((3,))],
+    )(lead_blocks, absorption, half, core, diag_new, got_a, got_b, half_a, diag_b, half_b, hp, inner)
     return (density_next, grid_term)
 
 

time: 71.1 us -> 66.3 us (0.932); the launches traced: 70.9 us -> 65.2 us
  waiting for transfers between devices: 5.66 us -> 0.73 us
  Pallas kernels: 29.3 us -> 27.7 us
    ppermute x20 -> x19, waiting for transfers between devices: 5.66 us -> 0.73 us  [the longest x3 0.69 us: exchange_b(): lax.ppermute(x, ('row', 'col'), [(i, i + 1) if i % 2 else (i, i - 1) for...]
    pallas_call x1, Pallas kernels: 5.32 us -> 3.17 us  [shards(): call(functools.partial(second_inner_kernel, count), (jax.ShapeDtypeStruct...]
    pallas_call x1, Pallas kernels: 2.64 us -> 3.84 us  [shards(): call(functools.partial(second_outer_kernel, count), pltpu.HBM(density.sha...]
    ppermute x20 -> x19, starting transfers between devices: 34.2 us -> 34.9 us  [the longest x14 21.2 us: across(): return lax.ppermute(x, ('row', 'col'), pairs)]
  transfers between devices with their start and end apart: 20 -> 19, of which waited for: 3 -> 1; matrix products, arithmetic and copies ran while one was open for 0% -> 0% of each run, Pallas kernels for 30% -> 29%
where the time goes in v3:
time: 66.3 us; the launch traced here: 65.2 us
  starting transfers between devices  34.9 us (53%)
  Pallas kernels  27.7 us (42%)
  between operations  1.11 us (2%)
  waiting for transfers between devices  0.73 us (1%)
  local copies, waits for them, and re-layouts  0.71 us (1%)
    ppermute x14, starting transfers between devices, across(): return lax.ppermute(x, ('row', 'col'), pairs)  21.2 us
    ppermute x3, starting transfers between devices, exchange_b(): lax.ppermute(x, ('row', 'col'), [(i, i + 1) if i % 2 else (i, i - 1) for...  13.6 us
    pallas_call x4, Pallas kernels, shards(): call(functools.partial(brick_kernel, points // 4, orders, numbers), (pack...  11.3 us
    pallas_call x1, Pallas kernels, shards(): call(functools.partial(second_outer_kernel, count), pltpu.HBM(density.sha...  3.84 us
    pallas_call x1, Pallas kernels, shards(): call(functools.partial(first_outer_kernel, count, orders), (jax.ShapeDtyp...  3.64 us
    pallas_call x1, Pallas kernels, shards(): call(functools.partial(second_inner_kernel, count), (jax.ShapeDtypeStruct...  3.17 us
    pallas_call x1, Pallas kernels, shards(): call(functools.partial(first_inner_kernel, count), (hp_shape, jax.ShapeDt...  3.11 us
    pallas_call x1, Pallas kernels, shards(): call(functools.partial(send_kernel, count), (message, message), flops=1 <...  1.54 us
  transfers between devices with their start and end apart: 19, of which 1 were waited for; matrix products, arithmetic and copies ran while one was open for 0% of the time, Pallas kernels for 29%

profile of v3, /device:TPU:1, one launch (start us, length us, event | category | flops | bytes accessed | tf_op | source)
XLA Modules:
  0.0 65.2 jit_solution(12570309422414172824)
XLA Ops:
  0.6 0.0 copy-start
  0.6 0.0 copy-start.2
  0.7 0.0 copy-start.1
  0.7 0.0 copy-start.5
  0.7 0.0 copy-start.4
  0.7 1.5 %shard_map.87 = (bf16[6,128,128]{2,1,0:T(8,128)(2,1)S(1)}, bf16[6,128,128]{2,1,0:T(8,128)(2,1)S(1)}) custom-call(bf16[2,8,3,128,128]{4,3,2,1,0:T(8,128)(2,1)} %dens.5, bf16[2,8,3,128,128]{4,3,2,1,0:T(8,128)(2,1)} %core.11, f32[8,128,128]{2,1,0:T(8,128)} %grid_old.5), custom_call_target="tpu_custom_call" | custom-call | flops 1048576 | bytes 4194304 | tf_op jit(solution)/shard_map/pallas_call | solution.py:569
  2.2 0.1 collective-permute-start
  2.3 4.5 %collective-permute-start.1 = (bf16[6,128,128]{2,1,0:T(8,128)(2,1)S(1)}, bf16[6,128,128]{2,1,0:T(8,128)(2,1)S(1)}, u32[]{:S(2)}, u32[]{:S(2)}) collective-permute-start(bf16[6,128,128]{2,1,0:T(8,128)(2,1)S(1)} %get-tuple-element.35), channel_id=1, source_target_pairs={{1,2},{2,1},{3,4},{4,3},{5,6},{6,5},{7,8},{8,7},{9,10},{10,9},{11,... | collective-permute-start | bytes 589832 | tf_op jit(solution)/shard_map/ppermute | solution.py:552
  6.8 0.0 copy-done
  6.8 0.0 copy-done.2
  6.8 0.0 copy-done.1
  6.8 0.0 copy-done.5
  6.9 0.0 copy-done.4
  6.9 0.0 copy-start.3
  6.9 0.7 %copy-done.3 = s32[8,24]{1,0:T(8,128)S(1)} copy-done((s32[8,24]{1,0:T(8,128)S(1)}, s32[8,24]{1,0:T(8,128)}, u32[]{:S(2)}) %copy-start.3) | copy-done | bytes 792
  7.6 0.0 slice-start
  7.6 3.1 %shard_map.86 = (bf16[10,3,128,256]{3,2,1,0:T(8,128)(2,1)S(1)}, bf16[2,8,3,128,128]{4,3,2,1,0:T(8,128)(2,1)S(1)}, s32[8,24]{1,0:T(8,128)S(1)}, s32[8,24]{1,0:T(8,128)S(1)}) custom-call(s32[8]{0:T(128)S(1)} %copy-done.4, f32[8]{0:T(128)S(1)} %copy-done.5, bf16[2,8,3,128,128]{4,3,2,1,0:T(8,128)(2,1)S(1)} %copy-done.1, ...), custom_call_target="tpu_custom_call" | custom-call | flops 4294967296 | bytes 4194304 | tf_op jit(solution)/shard_map/pallas_call | solution.py:592
  10.7 0.0 collective-permute-done.got_a.core_a
  10.7 0.7 %collective-permute-done.1.got_b.core_b = bf16[6,128,128]{2,1,0:T(8,128)(2,1)S(1)} collective-permute-done((bf16[6,128,128]{2,1,0:T(8,128)(2,1)S(1)}, bf16[6,128,128]{2,1,0:T(8,128)(2,1)S(1)}, u32[]{:S(2)}, u32[]{:S(2)}) %collective-permute-start.1) | collective-permute-done | bytes 196640 | tf_op jit(solution)/shard_map/ppermute | solution.py:552
  11.4 3.6 %shard_map.88 = (bf16[2,8,3,128,128]{4,3,2,1,0:T(8,128)(2,1)S(1)}, bf16[6,128,128]{2,1,0:T(8,128)(2,1)S(1)}, bf16[208,128]{1,0:T(8,128)(2,1)S(1)}, bf16[208,128]...) custom-call(s32[8]{0:T(128)S(1)} %copy-done.4, ...), custom_call_target="tpu_custom_call" | custom-call | flops 4294967296 | bytes 4194304 | tf_op jit(solution)/shard_map/pallas_call | solution.py:604
  15.0 3.6 %collective-permute-start.2 = (bf16[208,128]{1,0:T(8,128)(2,1)S(1)}, bf16[208,128]{1,0:T(8,128)(2,1)S(1)}, u32[]{:S(2)}, u32[]{:S(2)}) collective-permute-start(bf16[208,128]{1,0:T(8,128)(2,1)S(1)} %get-tuple-element.41), channel_id=1, source_target_pairs={{0,16},{1,17},{2,18},{3,19},{4,20},{5,21},{6,22},{7,23},{8,24},{9,... | collective-permute-start | bytes 159752 | tf_op jit(solution)/shard_map/ppermute | solution.py:631
  18.6 1.5 %collective-permute-start.4 = (bf16[208,128]{1,0:T(8,128)(2,1)S(1)}, bf16[208,128]{1,0:T(8,128)(2,1)S(1)}, u32[]{:S(2)}, u32[]{:S(2)}) collective-permute-start(bf16[208,128]{1,0:T(8,128)(2,1)S(1)} %get-tuple-element.44), channel_id=1, source_target_pairs={{0,20},{1,21},{2,22},{3,23},{4,16},{5,17},{6,18},{7,19},{8,28},{9,... | collective-permute-start | bytes 159752 | tf_op jit(solution)/shard_map/ppermute | solution.py:631
  20.2 3.3 %collective-permute-start.5 = (bf16[208,128]{1,0:T(8,128)(2,1)S(1)}, bf16[208,128]{1,0:T(8,128)(2,1)S(1)}, u32[]{:S(2)}, u32[]{:S(2)}) collective-permute-start(bf16[208,128]{1,0:T(8,128)(2,1)S(1)} %get-tuple-element.45), channel_id=1, source_target_pairs={{0,24},{1,25},{2,26},{3,27},{4,28},{5,29},{6,30},{7,31},{8,16},{9,... | collective-permute-start | bytes 159752 | tf_op jit(solution)/shard_map/ppermute | solution.py:631
  23.5 0.0 collective-permute-start.8
  23.5 1.2 %collective-permute-start.9 = (bf16[208,128]{1,0:T(8,128)(2,1)S(1)}, bf16[208,128]{1,0:T(8,128)(2,1)S(1)}, u32[]{:S(2)}, u32[]{:S(2)}) collective-permute-start(bf16[208,128]{1,0:T(8,128)(2,1)S(1)} %get-tuple-element.49), channel_id=1, source_target_pairs={{0,4},{1,5},{2,6},{3,7},{4,0},{5,1},{6,2},{7,3},{8,12},{9,13},{10,... | collective-permute-start | bytes 159752 | tf_op jit(solution)/shard_map/ppermute | solution.py:631
  24.7 0.0 collective-permute-done.2.rest_1_
  24.7 0.0 collective-permute-start.12
  24.7 0.0 slice-done
  24.7 0.0 slice-done.1
  24.7 0.0 slice-done.2
  24.7 2.8 %shard_map.89 = (bf16[208,128]{1,0:T(8,128)(2,1)S(1)}, bf16[208,128]{1,0:T(8,128)(2,1)S(1)}) custom-call(s32[8,24]{1,0:T(8,128)S(1)} %get-tuple-element.39.which.unread, bf16[24,2048,128]{2,1,0:T(8,128)(2,1)S(1)} %bitcast.1, s32[8,24]{1,0:T(8,128)S(1)} %get-tuple-element.39.which.unread, bf16[208,128]{1,0:T(8,128)(2,1)S(1)} %get-tuple-element.40.rest_0_, ...), custom_call_target="tpu_custom_call" | custom-call | flops 805306368 | bytes 4194304 | tf_op jit(solution)/shard_map/pallas_call | solution.py:639
  27.5 0.0 collective-permute-done.4.rest_0_
  27.5 1.5 %collective-permute-start.13 = (bf16[208,128]{1,0:T(8,128)(2,1)S(1)}, bf16[208,128]{1,0:T(8,128)(2,1)S(1)}, u32[]{:S(2)}, u32[]{:S(2)}) collective-permute-start(bf16[208,128]{1,0:T(8,128)(2,1)S(1)} %get-tuple-element.53), channel_id=1, source_target_pairs={{0,12},{1,13},{2,14},{3,15},{4,8},{5,9},{6,10},{7,11},{8,4},{9,5},... | collective-permute-start | bytes 159752 | tf_op jit(solution)/shard_map/ppermute | solution.py:631
  29.0 0.0 collective-permute-done.5.rest_1_
  29.1 2.7 %collective-permute-start.3 = (bf16[208,128]{1,0:T(8,128)(2,1)S(1)}, bf16[208,128]{1,0:T(8,128)(2,1)S(1)}, u32[]{:S(2)}, u32[]{:S(2)}) collective-permute-start(bf16[208,128]{1,0:T(8,128)(2,1)S(1)} %get-tuple-element.43), channel_id=1, source_target_pairs={{0,16},{1,17},{2,18},{3,19},{4,20},{5,21},{6,22},{7,23},{8,24},{9,... | collective-permute-start | bytes 159752 | tf_op jit(solution)/shard_map/ppermute | solution.py:631
  31.7 2.8 %shard_map.90 = (bf16[208,128]{1,0:T(8,128)(2,1)S(1)}, bf16[208,128]{1,0:T(8,128)(2,1)S(1)}) custom-call(s32[8,24]{1,0:T(8,128)S(1)} %get-tuple-element.39.which.unread, bf16[24,2048,128]{2,1,0:T(8,128)(2,1)S(1)} %bitcast.1, bf16[208,128]{1,0:T(8,128)(2,1)S(1)} %get-tuple-element.42.unread.rest_0_, bf16[208,128]{1,0:T(8,128)(2,1)S(1)} %collective-permute-done.4.rest_0_, ...), custom_call_target="tpu_custom_call" | custom-call | flops 805306368 | bytes 4194304 | tf_op jit(solution)/shard_map/pallas_call | solution.py:639
  34.6 0.0 collective-permute-done.8.rest_0_
  34.6 1.2 %collective-permute-start.7 = (bf16[208,128]{1,0:T(8,128)(2,1)S(1)}, bf16[208,128]{1,0:T(8,128)(2,1)S(1)}, u32[]{:S(2)}, u32[]{:S(2)}) collective-permute-start(bf16[208,128]{1,0:T(8,128)(2,1)S(1)} %get-tuple-element.47), channel_id=1, source_target_pairs={{0,24},{1,25},{2,26},{3,27},{4,28},{5,29},{6,30},{7,31},{8,16},{9,... | collective-permute-start | bytes 159752 | tf_op jit(solution)/shard_map/ppermute | solution.py:631
  35.8 0.0 collective-permute-done.9.rest_1_
  35.8 1.8 %collective-permute-start.6 = (bf16[208,128]{1,0:T(8,128)(2,1)S(1)}, bf16[208,128]{1,0:T(8,128)(2,1)S(1)}, u32[]{:S(2)}, u32[]{:S(2)}) collective-permute-start(bf16[208,128]{1,0:T(8,128)(2,1)S(1)} %get-tuple-element.46.unread), channel_id=1, source_target_pairs={{0,20},{1,21},{2,22},{3,23},{4,16},{5,17},{6,18},{7,19},{8,28},{9,... | collective-permute-start | bytes 159752 | tf_op jit(solution)/shard_map/ppermute | solution.py:631
  37.6 2.8 %shard_map.91 = (bf16[208,128]{1,0:T(8,128)(2,1)S(1)}, bf16[208,128]{1,0:T(8,128)(2,1)S(1)}) custom-call(s32[8,24]{1,0:T(8,128)S(1)} %get-tuple-element.39.which.unread, bf16[24,2048,128]{2,1,0:T(8,128)(2,1)S(1)} %bitcast.1, bf16[208,128]{1,0:T(8,128)(2,1)S(1)} %get-tuple-element.46.unread, bf16[208,128]{1,0:T(8,128)(2,1)S(1)} %collective-permute-done.8.rest_0_, ...), custom_call_target="tpu_custom_call" | custom-call | flops 805306368 | bytes 4194304 | tf_op jit(solution)/shard_map/pallas_call | solution.py:639
  40.4 0.0 collective-permute-done.12.rest_0_
  40.4 0.9 %collective-permute-start.11 = (bf16[208,128]{1,0:T(8,128)(2,1)S(1)}, bf16[208,128]{1,0:T(8,128)(2,1)S(1)}, u32[]{:S(2)}, u32[]{:S(2)}) collective-permute-start(bf16[208,128]{1,0:T(8,128)(2,1)S(1)} %get-tuple-element.51), channel_id=1, source_target_pairs={{0,4},{1,5},{2,6},{3,7},{4,0},{5,1},{6,2},{7,3},{8,12},{9,13},{10,... | collective-permute-start | bytes 159752 | tf_op jit(solution)/shard_map/ppermute | solution.py:631
  41.4 0.0 collective-permute-done.13.rest_1_
  41.4 1.3 %collective-permute-start.10 = (bf16[208,128]{1,0:T(8,128)(2,1)S(1)}, bf16[208,128]{1,0:T(8,128)(2,1)S(1)}, u32[]{:S(2)}, u32[]{:S(2)}) collective-permute-start(bf16[208,128]{1,0:T(8,128)(2,1)S(1)} %get-tuple-element.50.unread), channel_id=1, source_target_pairs={{0,28},{1,29},{2,30},{3,31},{4,24},{5,25},{6,26},{7,27},{8,20},{9,... | collective-permute-start | bytes 159752 | tf_op jit(solution)/shard_map/ppermute | solution.py:631
  42.7 2.8 %shard_map.92 = (bf16[208,128]{1,0:T(8,128)(2,1)S(1)}, bf16[208,128]{1,0:T(8,128)(2,1)S(1)}) custom-call(s32[8,24]{1,0:T(8,128)S(1)} %get-tuple-element.39.which.unread, bf16[24,2048,128]{2,1,0:T(8,128)(2,1)S(1)} %bitcast.1, bf16[208,128]{1,0:T(8,128)(2,1)S(1)} %get-tuple-element.50.unread, bf16[208,128]{1,0:T(8,128)(2,1)S(1)} %collective-permute-done.12.rest_0_, ...), custom_call_target="tpu_custom_call" | custom-call | flops 805306368 | bytes 4194304 | tf_op jit(solution)/shard_map/pallas_call | solution.py:639
  45.5 0.0 collective-permute-done.3.rest_1_
  45.5 0.3 collective-permute-start.14
  45.8 0.0 collective-permute-done.7.rest_3_
  45.8 1.8 %collective-permute-start.15 = (bf16[208,128]{1,0:T(8,128)(2,1)S(1)}, bf16[208,128]{1,0:T(8,128)(2,1)S(1)}, u32[]{:S(2)}, u32[]{:S(2)}) collective-permute-start(bf16[208,128]{1,0:T(8,128)(2,1)S(1)} %get-tuple-element.55), channel_id=1, source_target_pairs={{0,12},{1,13},{2,14},{3,15},{4,8},{5,9},{6,10},{7,11},{8,4},{9,5},... | collective-permute-start | bytes 159752 | tf_op jit(solution)/shard_map/ppermute | solution.py:631
  47.6 0.0 collective-permute-done.6.rest_2_
  47.6 6.3 %collective-permute-start.18 = (bf16[6,128,128]{2,1,0:T(8,128)(2,1)S(1)}, bf16[6,128,128]{2,1,0:T(8,128)(2,1)S(1)}, u32[]{:S(2)}, u32[]{:S(2)}) collective-permute-start(bf16[6,128,128]{2,1,0:T(8,128)(2,1)S(1)} %get-tuple-element.59), channel_id=1, source_target_pairs={{1,2},{2,1},{3,4},{4,3},{5,6},{6,5},{7,8},{8,7},{9,10},{10,9},{11,... | collective-permute-start | bytes 589832 | tf_op jit(solution)/shard_map/ppermute | solution.py:552
  53.9 0.0 collective-permute-done.11.rest_5_
  53.9 0.0 collective-permute-done.10.rest_4_
  53.9 0.0 collective-permute-done.14.rest_6_
  53.9 0.0 collective-permute-done.15.rest_7_
  54.0 1.1 %shard_map.93 = (f32[8,128,128]{2,1,0:T(8,128)S(1)}, bf16[8,128,128]{2,1,0:T(8,128)(2,1)S(1)}, bf16[7,128,128]{2,1,0:T(8,128)(2,1)S(1)}, bf16[1,128,128]{2,1,0:T(8,128)(2,1)S(1)}) custom-call(s32[8,24]{1,0:T(8,128)S(1)} %get-tuple-element.33.place, bf16[2,8,3,128,128]{4,3,2,1,0:T(8,128)(2,1)S(1)} %copy-done, ...), custom_call_target="tpu_custom_call" | custom-call | flops 1048576 | bytes 4194304 | tf_op jit(solution)/shard_map/pallas_call | solution.py:650
  55.1 2.8 %collective-permute-start.17 = (bf16[1,128,128]{2,1,0:T(8,128)(2,1)S(1)}, bf16[1,128,128]{2,1,0:T(8,128)(2,1)S(1)}, u32[]{:S(2)}, u32[]{:S(2)}) collective-permute-start(bf16[1,128,128]{2,1,0:T(8,128)(2,1)S(1)} %get-tuple-element.58), channel_id=1, source_target_pairs={{1,2},{2,1},{3,4},{4,3},{5,6},{6,5},{7,8},{8,7},{9,10},{10,9},{11,... | collective-permute-start | bytes 98312 | tf_op jit(solution)/shard_map/ppermute | solution.py:552
  57.9 0.1 collective-permute-start.16
  58.0 3.2 %shard_map.94 = (bf16[2,4,3,128,128]{4,3,2,1,0:T(8,128)(2,1)S(1)}, bf16[10,3,128,256]{3,2,1,0:T(8,128)(2,1)S(1)}, f32[8,128,128]{2,1,0:T(8,128)}) custom-call(s32[8]{0:T(128)S(1)} %copy-done.4, f32[8]{0:T(128)S(1)} %copy-done.5, bf16[2,8,3,128,128]{4,3,2,1,0:T(8,128)(2,1)S(1)} %get-tuple-element.38.half, bf16[2,8,3,128,128]{4,3,2,1,0:T(8,128)(2,1)S(1)} %copy-done, ...), custom_call_target="tpu_custom_call" | custom-call | flops 4294967296 | bytes 4194304 | tf_op jit(solution)/shard_map/pallas_call | solution.py:667
  61.2 0.0 collective-permute-done.17.got_b
  61.2 0.0 collective-permute-done.18.half_b
  61.2 0.0 collective-permute-done.16.got_a
  61.2 3.8 %shard_map.95 = bf16[2,8,3,128,128]{4,3,2,1,0:T(8,128)(2,1)} custom-call(s32[8]{0:T(128)S(1)} %copy-done.4, f32[8]{0:T(128)S(1)} %copy-done.5, bf16[2,8,3,128,128]{4,3,2,1,0:T(8,128)(2,1)S(1)} %get-tuple-element.38.half, bf16[2,8,3,128,128]{4,3,2,1,0:T(8,128)(2,1)S(1)} %copy-done, bf16[8,128,128]{2,1,0:T(8,128)(2,1)S(1)} %get-tuple-element.56.diag_new, ...), custom_call_target="tpu_custom_call" | custom-call | flops 4294967296 | bytes 4194304 | tf_op jit(solution)/shard_map/pallas_call | solution.py:681
  (3 shorter events, 0.0 us)
Async XLA Ops:
  0.6 6.2 %copy-start = (bf16[2,8,3,128,128]{4,3,2,1,0:T(8,128)(2,1)S(1)}, bf16[2,8,3,128,128]{4,3,2,1,0:T(8,128)(2,1)}, u32[]{:S(2)}) copy-start(bf16[2,8,3,128,128]{4,3,2,1,0:T(8,128)(2,1)} %core.11) | copy-start | bytes 4718596
  0.6 6.2 %copy-start.2 = (f32[8,128,128]{2,1,0:T(8,128)S(1)}, f32[8,128,128]{2,1,0:T(8,128)}, u32[]{:S(2)}) copy-start(f32[8,128,128]{2,1,0:T(8,128)} %grid_old.5) | copy-start | bytes 1572868
  0.7 6.2 %copy-start.1 = (bf16[2,8,3,128,128]{4,3,2,1,0:T(8,128)(2,1)S(1)}, bf16[2,8,3,128,128]{4,3,2,1,0:T(8,128)(2,1)}, u32[]{:S(2)}) copy-start(bf16[2,8,3,128,128]{4,3,2,1,0:T(8,128)(2,1)} %dens.5) | copy-start | bytes 4718596
  0.7 6.2 %copy-start.5 = (f32[8]{0:T(128)S(1)}, f32[8]{0:T(128)}, u32[]{:S(2)}) copy-start(f32[8]{0:T(128)} %absorption.7) | copy-start | bytes 100
  0.7 6.2 %copy-start.4 = (s32[8]{0:T(128)S(1)}, s32[8]{0:T(128)}, u32[]{:S(2)}) copy-start(s32[8]{0:T(128)} %leads.7) | copy-start | bytes 100
  2.2 8.4 %collective-permute-start = (bf16[6,128,128]{2,1,0:T(8,128)(2,1)S(1)}, bf16[6,128,128]{2,1,0:T(8,128)(2,1)S(1)}, u32[]{:S(2)}, u32[]{:S(2)}) collective-permute-start(bf16[6,128,128]{2,1,0:T(8,128)(2,1)S(1)} %get-tuple-element.34), channel_id=1, source_target_pairs={{0,1},{1,0},{2,3},{3,2},{4,5},{5,4},{6,7},{7,6},{8,9},{9,8},{10,11... | collective-permute-start | bytes 589832 | tf_op jit(solution)/shard_map/ppermute | solution.py:548
  2.3 9.0 %collective-permute-start.1 = (bf16[6,128,128]{2,1,0:T(8,128)(2,1)S(1)}, bf16[6,128,128]{2,1,0:T(8,128)(2,1)S(1)}, u32[]{:S(2)}, u32[]{:S(2)}) collective-permute-start(bf16[6,128,128]{2,1,0:T(8,128)(2,1)S(1)} %get-tuple-element.35), channel_id=1, source_target_pairs={{1,2},{2,1},{3,4},{4,3},{5,6},{6,5},{7,8},{8,7},{9,10},{10,9},{11,... | collective-permute-start | bytes 589832 | tf_op jit(solution)/shard_map/ppermute | solution.py:552
  6.9 0.7 %copy-start.3 = (s32[8,24]{1,0:T(8,128)S(1)}, s32[8,24]{1,0:T(8,128)}, u32[]{:S(2)}) copy-start(s32[8,24]{1,0:T(8,128)} %owners.1) | copy-start | bytes 2308
  7.6 17.1 %slice-start = ((s8[12582912]{0:T(1024)(128)(4,1)}), s8[4194304]{0:T(1024)(128)(4,1)S(1)}, s32[]{:S(2)}) async-start(s8[12582912]{0:T(1024)(128)(4,1)} %bitcast), calls=%async_computation | async-start | bytes 8388608
  7.6 17.1 %slice-start.1 = ((s8[12582912]{0:T(1024)(128)(4,1)}), s8[4194304]{0:T(1024)(128)(4,1)S(1)}, s32[]{:S(2)}) async-start(s8[12582912]{0:T(1024)(128)(4,1)} %bitcast), calls=%async_computation.1 | async-start | bytes 8388608
  11.4 13.3 %slice-start.2 = ((s8[12582912]{0:T(1024)(128)(4,1)}), s8[4194304]{0:T(1024)(128)(4,1)S(1)}, s32[]{:S(2)}) async-start(s8[12582912]{0:T(1024)(128)(4,1)} %bitcast), calls=%async_computation.2 | async-start | bytes 8388608
  15.0 9.6 %collective-permute-start.2 = (bf16[208,128]{1,0:T(8,128)(2,1)S(1)}, bf16[208,128]{1,0:T(8,128)(2,1)S(1)}, u32[]{:S(2)}, u32[]{:S(2)}) collective-permute-start(bf16[208,128]{1,0:T(8,128)(2,1)S(1)} %get-tuple-element.41), channel_id=1, source_target_pairs={{0,16},{1,17},{2,18},{3,19},{4,20},{5,21},{6,22},{7,23},{8,24},{9,... | collective-permute-start | bytes 159752 | tf_op jit(solution)/shard_map/ppermute | solution.py:631
  18.6 8.9 %collective-permute-start.4 = (bf16[208,128]{1,0:T(8,128)(2,1)S(1)}, bf16[208,128]{1,0:T(8,128)(2,1)S(1)}, u32[]{:S(2)}, u32[]{:S(2)}) collective-permute-start(bf16[208,128]{1,0:T(8,128)(2,1)S(1)} %get-tuple-element.44), channel_id=1, source_target_pairs={{0,20},{1,21},{2,22},{3,23},{4,16},{5,17},{6,18},{7,19},{8,28},{9,... | collective-permute-start | bytes 159752 | tf_op jit(solution)/shard_map/ppermute | solution.py:631
  20.2 8.9 %collective-permute-start.5 = (bf16[208,128]{1,0:T(8,128)(2,1)S(1)}, bf16[208,128]{1,0:T(8,128)(2,1)S(1)}, u32[]{:S(2)}, u32[]{:S(2)}) collective-permute-start(bf16[208,128]{1,0:T(8,128)(2,1)S(1)} %get-tuple-element.45), channel_id=1, source_target_pairs={{0,24},{1,25},{2,26},{3,27},{4,28},{5,29},{6,30},{7,31},{8,16},{9,... | collective-permute-start | bytes 159752 | tf_op jit(solution)/shard_map/ppermute | solution.py:631
  23.5 11.1 %collective-permute-start.8 = (bf16[208,128]{1,0:T(8,128)(2,1)S(1)}, bf16[208,128]{1,0:T(8,128)(2,1)S(1)}, u32[]{:S(2)}, u32[]{:S(2)}) collective-permute-start(bf16[208,128]{1,0:T(8,128)(2,1)S(1)} %get-tuple-element.48), channel_id=1, source_target_pairs={{0,28},{1,29},{2,30},{3,31},{4,24},{5,25},{6,26},{7,27},{8,20},{9,... | collective-permute-start | bytes 159752 | tf_op jit(solution)/shard_map/ppermute | solution.py:631
  23.5 12.3 %collective-permute-start.9 = (bf16[208,128]{1,0:T(8,128)(2,1)S(1)}, bf16[208,128]{1,0:T(8,128)(2,1)S(1)}, u32[]{:S(2)}, u32[]{:S(2)}) collective-permute-start(bf16[208,128]{1,0:T(8,128)(2,1)S(1)} %get-tuple-element.49), channel_id=1, source_target_pairs={{0,4},{1,5},{2,6},{3,7},{4,0},{5,1},{6,2},{7,3},{8,12},{9,13},{10,... | collective-permute-start | bytes 159752 | tf_op jit(solution)/shard_map/ppermute | solution.py:631
  24.7 15.8 %collective-permute-start.12 = (bf16[208,128]{1,0:T(8,128)(2,1)S(1)}, bf16[208,128]{1,0:T(8,128)(2,1)S(1)}, u32[]{:S(2)}, u32[]{:S(2)}) collective-permute-start(bf16[208,128]{1,0:T(8,128)(2,1)S(1)} %get-tuple-element.52), channel_id=1, source_target_pairs={{0,8},{1,9},{2,10},{3,11},{4,12},{5,13},{6,14},{7,15},{8,0},{9,1},... | collective-permute-start | bytes 159752 | tf_op jit(solution)/shard_map/ppermute | solution.py:631
  27.5 13.8 %collective-permute-start.13 = (bf16[208,128]{1,0:T(8,128)(2,1)S(1)}, bf16[208,128]{1,0:T(8,128)(2,1)S(1)}, u32[]{:S(2)}, u32[]{:S(2)}) collective-permute-start(bf16[208,128]{1,0:T(8,128)(2,1)S(1)} %get-tuple-element.53), channel_id=1, source_target_pairs={{0,12},{1,13},{2,14},{3,15},{4,8},{5,9},{6,10},{7,11},{8,4},{9,5},... | collective-permute-start | bytes 159752 | tf_op jit(solution)/shard_map/ppermute | solution.py:631
  29.1 16.4 %collective-permute-start.3 = (bf16[208,128]{1,0:T(8,128)(2,1)S(1)}, bf16[208,128]{1,0:T(8,128)(2,1)S(1)}, u32[]{:S(2)}, u32[]{:S(2)}) collective-permute-start(bf16[208,128]{1,0:T(8,128)(2,1)S(1)} %get-tuple-element.43), channel_id=1, source_target_pairs={{0,16},{1,17},{2,18},{3,19},{4,20},{5,21},{6,22},{7,23},{8,24},{9,... | collective-permute-start | bytes 159752 | tf_op jit(solution)/shard_map/ppermute | solution.py:631
  34.6 11.2 %collective-permute-start.7 = (bf16[208,128]{1,0:T(8,128)(2,1)S(1)}, bf16[208,128]{1,0:T(8,128)(2,1)S(1)}, u32[]{:S(2)}, u32[]{:S(2)}) collective-permute-start(bf16[208,128]{1,0:T(8,128)(2,1)S(1)} %get-tuple-element.47), channel_id=1, source_target_pairs={{0,24},{1,25},{2,26},{3,27},{4,28},{5,29},{6,30},{7,31},{8,16},{9,... | collective-permute-start | bytes 159752 | tf_op jit(solution)/shard_map/ppermute | solution.py:631
  35.8 11.8 %collective-permute-start.6 = (bf16[208,128]{1,0:T(8,128)(2,1)S(1)}, bf16[208,128]{1,0:T(8,128)(2,1)S(1)}, u32[]{:S(2)}, u32[]{:S(2)}) collective-permute-start(bf16[208,128]{1,0:T(8,128)(2,1)S(1)} %get-tuple-element.46.unread), channel_id=1, source_target_pairs={{0,20},{1,21},{2,22},{3,23},{4,16},{5,17},{6,18},{7,19},{8,28},{9,... | collective-permute-start | bytes 159752 | tf_op jit(solution)/shard_map/ppermute | solution.py:631
  40.4 13.5 %collective-permute-start.11 = (bf16[208,128]{1,0:T(8,128)(2,1)S(1)}, bf16[208,128]{1,0:T(8,128)(2,1)S(1)}, u32[]{:S(2)}, u32[]{:S(2)}) collective-permute-start(bf16[208,128]{1,0:T(8,128)(2,1)S(1)} %get-tuple-element.51), channel_id=1, source_target_pairs={{0,4},{1,5},{2,6},{3,7},{4,0},{5,1},{6,2},{7,3},{8,12},{9,13},{10,... | collective-permute-start | bytes 159752 | tf_op jit(solution)/shard_map/ppermute | solution.py:631
  41.4 12.6 %collective-permute-start.10 = (bf16[208,128]{1,0:T(8,128)(2,1)S(1)}, bf16[208,128]{1,0:T(8,128)(2,1)S(1)}, u32[]{:S(2)}, u32[]{:S(2)}) collective-permute-start(bf16[208,128]{1,0:T(8,128)(2,1)S(1)} %get-tuple-element.50.unread), channel_id=1, source_target_pairs={{0,28},{1,29},{2,30},{3,31},{4,24},{5,25},{6,26},{7,27},{8,20},{9,... | collective-permute-start | bytes 159752 | tf_op jit(solution)/shard_map/ppermute | solution.py:631
  45.5 8.4 %collective-permute-start.14 = (bf16[208,128]{1,0:T(8,128)(2,1)S(1)}, bf16[208,128]{1,0:T(8,128)(2,1)S(1)}, u32[]{:S(2)}, u32[]{:S(2)}) collective-permute-start(bf16[208,128]{1,0:T(8,128)(2,1)S(1)} %get-tuple-element.54), channel_id=1, source_target_pairs={{0,8},{1,9},{2,10},{3,11},{4,12},{5,13},{6,14},{7,15},{8,0},{9,1},... | collective-permute-start | bytes 159752 | tf_op jit(solution)/shard_map/ppermute | solution.py:631
  45.8 8.2 %collective-permute-start.15 = (bf16[208,128]{1,0:T(8,128)(2,1)S(1)}, bf16[208,128]{1,0:T(8,128)(2,1)S(1)}, u32[]{:S(2)}, u32[]{:S(2)}) collective-permute-start(bf16[208,128]{1,0:T(8,128)(2,1)S(1)} %get-tuple-element.55), channel_id=1, source_target_pairs={{0,12},{1,13},{2,14},{3,15},{4,8},{5,9},{6,10},{7,11},{8,4},{9,5},... | collective-permute-start | bytes 159752 | tf_op jit(solution)/shard_map/ppermute | solution.py:631
  47.6 13.5 %collective-permute-start.18 = (bf16[6,128,128]{2,1,0:T(8,128)(2,1)S(1)}, bf16[6,128,128]{2,1,0:T(8,128)(2,1)S(1)}, u32[]{:S(2)}, u32[]{:S(2)}) collective-permute-start(bf16[6,128,128]{2,1,0:T(8,128)(2,1)S(1)} %get-tuple-element.59), channel_id=1, source_target_pairs={{1,2},{2,1},{3,4},{4,3},{5,6},{6,5},{7,8},{8,7},{9,10},{10,9},{11,... | collective-permute-start | bytes 589832 | tf_op jit(solution)/shard_map/ppermute | solution.py:552
  55.1 6.1 %collective-permute-start.17 = (bf16[1,128,128]{2,1,0:T(8,128)(2,1)S(1)}, bf16[1,128,128]{2,1,0:T(8,128)(2,1)S(1)}, u32[]{:S(2)}, u32[]{:S(2)}) collective-permute-start(bf16[1,128,128]{2,1,0:T(8,128)(2,1)S(1)} %get-tuple-element.58), channel_id=1, source_target_pairs={{1,2},{2,1},{3,4},{4,3},{5,6},{6,5},{7,8},{8,7},{9,10},{10,9},{11,... | collective-permute-start | bytes 98312 | tf_op jit(solution)/shard_map/ppermute | solution.py:552
  57.9 3.3 %collective-permute-start.16 = (bf16[7,128,128]{2,1,0:T(8,128)(2,1)S(1)}, bf16[7,128,128]{2,1,0:T(8,128)(2,1)S(1)}, u32[]{:S(2)}, u32[]{:S(2)}) collective-permute-start(bf16[7,128,128]{2,1,0:T(8,128)(2,1)S(1)} %get-tuple-element.57), channel_id=1, source_target_pairs={{0,1},{1,0},{2,3},{3,2},{4,5},{5,4},{6,7},{7,6},{8,9},{9,8},{10,11... | collective-permute-start | bytes 688136 | tf_op jit(solution)/shard_map/ppermute | solution.py:548

commit v4 on v3

--- a/solution.py
+++ b/solution.py
@@ -491,6 +491,8 @@
 def second_outer_kernel(count, leads, absorption, half, core, diag_new, core_a, core_b, got_a, got_b, half_b,
                         hp_in, inner, out, hp_ref, moved_ref, wh_ref, left_ref, right_ref, edges, ready, sems):
     copies = [pltpu.make_async_copy(inner, out.at[:, pl.ds(2, count - 4)], sems.at[2])]
+    for n, i in enumerate((0, count - 2)):
+        copies.append(pltpu.make_async_copy(ready.at[:, pl.ds(2 * n, 2)], out.at[:, pl.ds(i, 2)], sems.at[n]))
     copies[0].start()
     core_low, core_high = halo_reader(core_a, core_b)
     even = lax.axis_index("col") % 2 == 0
@@ -533,13 +535,14 @@
         n = i if i < 2 else i - count + 4
         ready[0, n, j - i + 1] = value[:, :width]
         ready[1, n, j - i + 1] = value[:, width:]
+        if (i, j) == (1, 2):
+            copies[1].start()
+        if (i, j) == (last, count):
+            copies[2].start()
 
     taylor_first(range(-1, 2), -1, 0, get_left, get_q, hp_ref)
     taylor_first(range(last - 1, count + 1), last, count, get_left, get_q, hp_ref)
     propagate([(0, 1), (last - 1, last)], get_q, get_hp, get_left, get_right, moved_ref, wh_ref, write)
-    for n, i in enumerate((0, last - 1)):
-        copies.append(pltpu.make_async_copy(ready.at[:, pl.ds(2 * n, 2)], out.at[:, pl.ds(i, 2)], sems.at[n]))
-        copies[-1].start()
     for copy in copies:
         copy.wait()
 
@@ -635,14 +638,15 @@
     points = collocation.shape[1]
     arriving = []
     before = which
-    for numbers in zip(range(0, row_size, 2), range(1, row_size, 2)):
+    ends = list(range(2, row_size - 3, 2)) + [row_size]
+    for numbers in [range(a, b) for a, b in zip([0] + ends, ends)]:
         returned = call(
             functools.partial(brick_kernel, points // 4, orders, numbers),
-            (packed_shape,) * 2,
-            flops=4 * 6 * points * width**2,
+            (packed_shape,) * len(numbers),
+            flops=4 * CAP * len(numbers) * points * width**2,
             vmem=8,
             scalars=1,
-            in_specs=[vmem, pl.BlockSpec(memory_space=pl.ANY), vmem, vmem],
+            in_specs=[vmem, pl.BlockSpec(memory_space=pl.ANY)] + [vmem] * len(numbers),
         )(which, collocation, before, *(incoming[number] for number in numbers))
         arriving += [across(x, number) for number, x in zip(numbers, returned)]
         before = returned[0]

time: 66.3 us -> 65 us (0.980)
  Pallas kernels: 27.7 us -> 26.6 us
    pallas_call x4 -> x3, Pallas kernels: 11.3 us -> 10.3 us  [shards(): call(functools.partial(brick_kernel, points // 4, orders, numbers), (pack...]
  transfers between devices with their start and end apart: 19 -> 19, of which waited for: 1 -> 1; matrix products, arithmetic and copies ran while one was open for 0% -> 0% of each run, Pallas kernels for 29% -> 28%
where the time goes in v4:
time: 65 us; the launch traced here: 64 us
  starting transfers between devices  34.9 us (54%)
  Pallas kernels  26.6 us (41%)
  between operations  1.1 us (2%)
  waiting for transfers between devices  0.74 us (1%)
  local copies, waits for them, and re-layouts  0.71 us (1%)
    ppermute x14, starting transfers between devices, across(): return lax.ppermute(x, ('row', 'col'), pairs)  21.1 us
    ppermute x3, starting transfers between devices, exchange_b(): lax.ppermute(x, ('row', 'col'), [(i, i + 1) if i % 2 else (i, i - 1) for...  13.6 us
    pallas_call x3, Pallas kernels, shards(): call(functools.partial(brick_kernel, points // 4, orders, numbers), (pack...  10.3 us
    pallas_call x1, Pallas kernels, shards(): call(functools.partial(second_outer_kernel, count), pltpu.HBM(density.sha...  3.73 us
    pallas_call x1, Pallas kernels, shards(): call(functools.partial(first_outer_kernel, count, orders), (jax.ShapeDtyp...  3.63 us
    pallas_call x1, Pallas kernels, shards(): call(functools.partial(second_inner_kernel, count), (jax.ShapeDtypeStruct...  3.17 us
    pallas_call x1, Pallas kernels, shards(): call(functools.partial(first_inner_kernel, count), (hp_shape, jax.ShapeDt...  3.1 us
    pallas_call x1, Pallas kernels, shards(): call(functools.partial(send_kernel, count), (message, message), flops=1 <...  1.54 us
  transfers between devices with their start and end apart: 19, of which 1 were waited for; matrix products, arithmetic and copies ran while one was open for 0% of the time, Pallas kernels for 28%

profile of v4, /device:TPU:1, one launch (start us, length us, event | category | flops | bytes accessed | tf_op | source)
XLA Modules:
  0.0 64.0 jit_solution(17740742247121373451)
XLA Ops:
  0.6 0.0 copy-start
  0.6 0.0 copy-start.2
  0.7 0.0 copy-start.1
  0.7 0.0 copy-start.5
  0.7 0.0 copy-start.4
  0.7 1.5 %shard_map.87 = (bf16[6,128,128]{2,1,0:T(8,128)(2,1)S(1)}, bf16[6,128,128]{2,1,0:T(8,128)(2,1)S(1)}) custom-call(bf16[2,8,3,128,128]{4,3,2,1,0:T(8,128)(2,1)} %dens.5, bf16[2,8,3,128,128]{4,3,2,1,0:T(8,128)(2,1)} %core.11, f32[8,128,128]{2,1,0:T(8,128)} %grid_old.5), custom_call_target="tpu_custom_call" | custom-call | flops 1048576 | bytes 4194304 | tf_op jit(solution)/shard_map/pallas_call | solution.py:572
  2.2 0.1 collective-permute-start
  2.3 4.5 %collective-permute-start.1 = (bf16[6,128,128]{2,1,0:T(8,128)(2,1)S(1)}, bf16[6,128,128]{2,1,0:T(8,128)(2,1)S(1)}, u32[]{:S(2)}, u32[]{:S(2)}) collective-permute-start(bf16[6,128,128]{2,1,0:T(8,128)(2,1)S(1)} %get-tuple-element.35), channel_id=1, source_target_pairs={{1,2},{2,1},{3,4},{4,3},{5,6},{6,5},{7,8},{8,7},{9,10},{10,9},{11,... | collective-permute-start | bytes 589832 | tf_op jit(solution)/shard_map/ppermute | solution.py:555
  6.8 0.0 copy-done
  6.8 0.0 copy-done.2
  6.8 0.0 copy-done.1
  6.8 0.0 copy-done.5
  6.9 0.0 copy-done.4
  6.9 0.0 copy-start.3
  6.9 0.7 %copy-done.3 = s32[8,24]{1,0:T(8,128)S(1)} copy-done((s32[8,24]{1,0:T(8,128)S(1)}, s32[8,24]{1,0:T(8,128)}, u32[]{:S(2)}) %copy-start.3) | copy-done | bytes 792
  7.6 0.0 slice-start
  7.6 0.0 slice-start.1
  7.6 3.1 %shard_map.86 = (bf16[10,3,128,256]{3,2,1,0:T(8,128)(2,1)S(1)}, bf16[2,8,3,128,128]{4,3,2,1,0:T(8,128)(2,1)S(1)}, s32[8,24]{1,0:T(8,128)S(1)}, s32[8,24]{1,0:T(8,128)S(1)}) custom-call(s32[8]{0:T(128)S(1)} %copy-done.4, f32[8]{0:T(128)S(1)} %copy-done.5, bf16[2,8,3,128,128]{4,3,2,1,0:T(8,128)(2,1)S(1)} %copy-done.1, ...), custom_call_target="tpu_custom_call" | custom-call | flops 4294967296 | bytes 4194304 | tf_op jit(solution)/shard_map/pallas_call | solution.py:595
  10.7 0.0 collective-permute-done.got_a.core_a
  10.7 0.7 %collective-permute-done.1.got_b.core_b = bf16[6,128,128]{2,1,0:T(8,128)(2,1)S(1)} collective-permute-done((bf16[6,128,128]{2,1,0:T(8,128)(2,1)S(1)}, bf16[6,128,128]{2,1,0:T(8,128)(2,1)S(1)}, u32[]{:S(2)}, u32[]{:S(2)}) %collective-permute-start.1) | collective-permute-done | bytes 196640 | tf_op jit(solution)/shard_map/ppermute | solution.py:555
  11.4 3.6 %shard_map.88 = (bf16[2,8,3,128,128]{4,3,2,1,0:T(8,128)(2,1)S(1)}, bf16[6,128,128]{2,1,0:T(8,128)(2,1)S(1)}, bf16[208,128]{1,0:T(8,128)(2,1)S(1)}, bf16[208,128]...) custom-call(s32[8]{0:T(128)S(1)} %copy-done.4, ...), custom_call_target="tpu_custom_call" | custom-call | flops 4294967296 | bytes 4194304 | tf_op jit(solution)/shard_map/pallas_call | solution.py:607
  15.0 3.6 %collective-permute-start.2 = (bf16[208,128]{1,0:T(8,128)(2,1)S(1)}, bf16[208,128]{1,0:T(8,128)(2,1)S(1)}, u32[]{:S(2)}, u32[]{:S(2)}) collective-permute-start(bf16[208,128]{1,0:T(8,128)(2,1)S(1)} %get-tuple-element.41), channel_id=1, source_target_pairs={{0,16},{1,17},{2,18},{3,19},{4,20},{5,21},{6,22},{7,23},{8,24},{9,... | collective-permute-start | bytes 159752 | tf_op jit(solution)/shard_map/ppermute | solution.py:634
  18.6 1.5 %collective-permute-start.4 = (bf16[208,128]{1,0:T(8,128)(2,1)S(1)}, bf16[208,128]{1,0:T(8,128)(2,1)S(1)}, u32[]{:S(2)}, u32[]{:S(2)}) collective-permute-start(bf16[208,128]{1,0:T(8,128)(2,1)S(1)} %get-tuple-element.44), channel_id=1, source_target_pairs={{0,20},{1,21},{2,22},{3,23},{4,16},{5,17},{6,18},{7,19},{8,28},{9,... | collective-permute-start | bytes 159752 | tf_op jit(solution)/shard_map/ppermute | solution.py:634
  20.1 3.3 %collective-permute-start.5 = (bf16[208,128]{1,0:T(8,128)(2,1)S(1)}, bf16[208,128]{1,0:T(8,128)(2,1)S(1)}, u32[]{:S(2)}, u32[]{:S(2)}) collective-permute-start(bf16[208,128]{1,0:T(8,128)(2,1)S(1)} %get-tuple-element.45), channel_id=1, source_target_pairs={{0,24},{1,25},{2,26},{3,27},{4,28},{5,29},{6,30},{7,31},{8,16},{9,... | collective-permute-start | bytes 159752 | tf_op jit(solution)/shard_map/ppermute | solution.py:634
  23.4 0.0 collective-permute-start.8
  23.5 1.2 %collective-permute-start.9 = (bf16[208,128]{1,0:T(8,128)(2,1)S(1)}, bf16[208,128]{1,0:T(8,128)(2,1)S(1)}, u32[]{:S(2)}, u32[]{:S(2)}) collective-permute-start(bf16[208,128]{1,0:T(8,128)(2,1)S(1)} %get-tuple-element.49), channel_id=1, source_target_pairs={{0,4},{1,5},{2,6},{3,7},{4,0},{5,1},{6,2},{7,3},{8,12},{9,13},{10,... | collective-permute-start | bytes 159752 | tf_op jit(solution)/shard_map/ppermute | solution.py:634
  24.6 0.0 collective-permute-done.2.rest_1_
  24.6 0.0 collective-permute-start.10
  24.6 0.0 slice-done
  24.6 0.0 slice-done.1
  24.7 0.0 slice-done.2
  24.7 2.8 %shard_map.89 = (bf16[208,128]{1,0:T(8,128)(2,1)S(1)}, bf16[208,128]{1,0:T(8,128)(2,1)S(1)}) custom-call(s32[8,24]{1,0:T(8,128)S(1)} %get-tuple-element.39.which.unread, bf16[24,2048,128]{2,1,0:T(8,128)(2,1)S(1)} %bitcast.1, s32[8,24]{1,0:T(8,128)S(1)} %get-tuple-element.39.which.unread, bf16[208,128]{1,0:T(8,128)(2,1)S(1)} %get-tuple-element.40.rest_0_, ...), custom_call_target="tpu_custom_call" | custom-call | flops 805306368 | bytes 4194304 | tf_op jit(solution)/shard_map/pallas_call | solution.py:643
  27.5 0.0 collective-permute-done.4.rest_0_
  27.5 1.5 %collective-permute-start.11 = (bf16[208,128]{1,0:T(8,128)(2,1)S(1)}, bf16[208,128]{1,0:T(8,128)(2,1)S(1)}, u32[]{:S(2)}, u32[]{:S(2)}) collective-permute-start(bf16[208,128]{1,0:T(8,128)(2,1)S(1)} %get-tuple-element.51), channel_id=1, source_target_pairs={{0,12},{1,13},{2,14},{3,15},{4,8},{5,9},{6,10},{7,11},{8,4},{9,5},... | collective-permute-start | bytes 159752 | tf_op jit(solution)/shard_map/ppermute | solution.py:634
  29.0 0.0 collective-permute-done.5.rest_1_
  29.0 2.7 %collective-permute-start.3 = (bf16[208,128]{1,0:T(8,128)(2,1)S(1)}, bf16[208,128]{1,0:T(8,128)(2,1)S(1)}, u32[]{:S(2)}, u32[]{:S(2)}) collective-permute-start(bf16[208,128]{1,0:T(8,128)(2,1)S(1)} %get-tuple-element.43), channel_id=1, source_target_pairs={{0,16},{1,17},{2,18},{3,19},{4,20},{5,21},{6,22},{7,23},{8,24},{9,... | collective-permute-start | bytes 159752 | tf_op jit(solution)/shard_map/ppermute | solution.py:634
  31.7 2.8 %shard_map.90 = (bf16[208,128]{1,0:T(8,128)(2,1)S(1)}, bf16[208,128]{1,0:T(8,128)(2,1)S(1)}) custom-call(s32[8,24]{1,0:T(8,128)S(1)} %get-tuple-element.39.which.unread, bf16[24,2048,128]{2,1,0:T(8,128)(2,1)S(1)} %bitcast.1, bf16[208,128]{1,0:T(8,128)(2,1)S(1)} %get-tuple-element.42.unread.rest_0_, bf16[208,128]{1,0:T(8,128)(2,1)S(1)} %collective-permute-done.4.rest_0_, ...), custom_call_target="tpu_custom_call" | custom-call | flops 805306368 | bytes 4194304 | tf_op jit(solution)/shard_map/pallas_call | solution.py:643
  34.5 0.0 collective-permute-done.8.rest_0_
  34.6 1.2 %collective-permute-start.7 = (bf16[208,128]{1,0:T(8,128)(2,1)S(1)}, bf16[208,128]{1,0:T(8,128)(2,1)S(1)}, u32[]{:S(2)}, u32[]{:S(2)}) collective-permute-start(bf16[208,128]{1,0:T(8,128)(2,1)S(1)} %get-tuple-element.47), channel_id=1, source_target_pairs={{0,24},{1,25},{2,26},{3,27},{4,28},{5,29},{6,30},{7,31},{8,16},{9,... | collective-permute-start | bytes 159752 | tf_op jit(solution)/shard_map/ppermute | solution.py:634
  35.8 0.0 collective-permute-done.9.rest_1_
  35.8 1.8 %collective-permute-start.6 = (bf16[208,128]{1,0:T(8,128)(2,1)S(1)}, bf16[208,128]{1,0:T(8,128)(2,1)S(1)}, u32[]{:S(2)}, u32[]{:S(2)}) collective-permute-start(bf16[208,128]{1,0:T(8,128)(2,1)S(1)} %get-tuple-element.46.unread), channel_id=1, source_target_pairs={{0,20},{1,21},{2,22},{3,23},{4,16},{5,17},{6,18},{7,19},{8,28},{9,... | collective-permute-start | bytes 159752 | tf_op jit(solution)/shard_map/ppermute | solution.py:634
  37.6 0.0 collective-permute-done.10.rest_2_
  37.6 0.0 collective-permute-done.11.rest_3_
  37.6 4.6 %shard_map.91 = (bf16[208,128]{1,0:T(8,128)(2,1)S(1)}, bf16[208,128]{1,0:T(8,128)(2,1)S(1)}, bf16[208,128]{1,0:T(8,128)(2,1)S(1)}, bf16[208,128]{1,0:T(8,128)(2,1)S(1)}) custom-call(s32[8,24]{1,0:T(8,128)S(1)} %get-tuple-element.39.which.unread, bf16[24,2048,128]{2,1,0:T(8,128)(2,1)S(1)} %bitcast.1, bf16[208,128]{1,0:T(8,128)(2,1)S(1)} %get-tuple-element.46.unread, ...), custom_call_target="tpu_custom_call" | custom-call | flops 1610612736 | bytes 4194304 | tf_op jit(solution)/shard_map/pallas_call | solution.py:643
  42.2 1.6 %collective-permute-start.12 = (bf16[208,128]{1,0:T(8,128)(2,1)S(1)}, bf16[208,128]{1,0:T(8,128)(2,1)S(1)}, u32[]{:S(2)}, u32[]{:S(2)}) collective-permute-start(bf16[208,128]{1,0:T(8,128)(2,1)S(1)} %get-tuple-element.52), channel_id=1, source_target_pairs={{0,28},{1,29},{2,30},{3,31},{4,24},{5,25},{6,26},{7,27},{8,20},{9,... | collective-permute-start | bytes 159752 | tf_op jit(solution)/shard_map/ppermute | solution.py:634
  43.8 0.6 collective-permute-start.13
  44.4 0.0 collective-permute-done.3.rest_1_
  44.4 0.2 collective-permute-start.14
  44.6 0.0 collective-permute-done.7.rest_3_
  44.6 1.9 %collective-permute-start.15 = (bf16[208,128]{1,0:T(8,128)(2,1)S(1)}, bf16[208,128]{1,0:T(8,128)(2,1)S(1)}, u32[]{:S(2)}, u32[]{:S(2)}) collective-permute-start(bf16[208,128]{1,0:T(8,128)(2,1)S(1)} %get-tuple-element.55), channel_id=1, source_target_pairs={{0,12},{1,13},{2,14},{3,15},{4,8},{5,9},{6,10},{7,11},{8,4},{9,5},... | collective-permute-start | bytes 159752 | tf_op jit(solution)/shard_map/ppermute | solution.py:634
  46.5 0.0 collective-permute-done.6.rest_2_
  46.5 6.3 %collective-permute-start.18 = (bf16[6,128,128]{2,1,0:T(8,128)(2,1)S(1)}, bf16[6,128,128]{2,1,0:T(8,128)(2,1)S(1)}, u32[]{:S(2)}, u32[]{:S(2)}) collective-permute-start(bf16[6,128,128]{2,1,0:T(8,128)(2,1)S(1)} %get-tuple-element.59), channel_id=1, source_target_pairs={{1,2},{2,1},{3,4},{4,3},{5,6},{6,5},{7,8},{8,7},{9,10},{10,9},{11,... | collective-permute-start | bytes 589832 | tf_op jit(solution)/shard_map/ppermute | solution.py:555
  52.8 0.0 collective-permute-done.12.rest_4_
  52.8 0.0 collective-permute-done.13.rest_5_
  52.8 0.0 collective-permute-done.14.rest_6_
  52.8 0.0 collective-permute-done.15.rest_7_
  52.8 1.1 %shard_map.92 = (f32[8,128,128]{2,1,0:T(8,128)S(1)}, bf16[8,128,128]{2,1,0:T(8,128)(2,1)S(1)}, bf16[7,128,128]{2,1,0:T(8,128)(2,1)S(1)}, bf16[1,128,128]{2,1,0:T(8,128)(2,1)S(1)}) custom-call(s32[8,24]{1,0:T(8,128)S(1)} %get-tuple-element.33.place, bf16[2,8,3,128,128]{4,3,2,1,0:T(8,128)(2,1)S(1)} %copy-done, ...), custom_call_target="tpu_custom_call" | custom-call | flops 1048576 | bytes 4194304 | tf_op jit(solution)/shard_map/pallas_call | solution.py:654
  53.9 2.8 %collective-permute-start.17 = (bf16[1,128,128]{2,1,0:T(8,128)(2,1)S(1)}, bf16[1,128,128]{2,1,0:T(8,128)(2,1)S(1)}, u32[]{:S(2)}, u32[]{:S(2)}) collective-permute-start(bf16[1,128,128]{2,1,0:T(8,128)(2,1)S(1)} %get-tuple-element.58), channel_id=1, source_target_pairs={{1,2},{2,1},{3,4},{4,3},{5,6},{6,5},{7,8},{8,7},{9,10},{10,9},{11,... | collective-permute-start | bytes 98312 | tf_op jit(solution)/shard_map/ppermute | solution.py:555
  56.8 0.1 collective-permute-start.16
  56.9 3.2 %shard_map.93 = (bf16[2,4,3,128,128]{4,3,2,1,0:T(8,128)(2,1)S(1)}, bf16[10,3,128,256]{3,2,1,0:T(8,128)(2,1)S(1)}, f32[8,128,128]{2,1,0:T(8,128)}) custom-call(s32[8]{0:T(128)S(1)} %copy-done.4, f32[8]{0:T(128)S(1)} %copy-done.5, bf16[2,8,3,128,128]{4,3,2,1,0:T(8,128)(2,1)S(1)} %get-tuple-element.38.half, bf16[2,8,3,128,128]{4,3,2,1,0:T(8,128)(2,1)S(1)} %copy-done, ...), custom_call_target="tpu_custom_call" | custom-call | flops 4294967296 | bytes 4194304 | tf_op jit(solution)/shard_map/pallas_call | solution.py:671
  60.0 0.0 collective-permute-done.17.got_b
  60.0 0.0 collective-permute-done.18.half_b
  60.1 0.0 collective-permute-done.16.got_a
  60.1 3.7 %shard_map.94 = bf16[2,8,3,128,128]{4,3,2,1,0:T(8,128)(2,1)} custom-call(s32[8]{0:T(128)S(1)} %copy-done.4, f32[8]{0:T(128)S(1)} %copy-done.5, bf16[2,8,3,128,128]{4,3,2,1,0:T(8,128)(2,1)S(1)} %get-tuple-element.38.half, bf16[2,8,3,128,128]{4,3,2,1,0:T(8,128)(2,1)S(1)} %copy-done, bf16[8,128,128]{2,1,0:T(8,128)(2,1)S(1)} %get-tuple-element.56.diag_new, ...), custom_call_target="tpu_custom_call" | custom-call | flops 4294967296 | bytes 4194304 | tf_op jit(solution)/shard_map/pallas_call | solution.py:685
  (2 shorter events, 0.0 us)
Async XLA Ops:
  0.6 6.2 %copy-start = (bf16[2,8,3,128,128]{4,3,2,1,0:T(8,128)(2,1)S(1)}, bf16[2,8,3,128,128]{4,3,2,1,0:T(8,128)(2,1)}, u32[]{:S(2)}) copy-start(bf16[2,8,3,128,128]{4,3,2,1,0:T(8,128)(2,1)} %core.11) | copy-start | bytes 4718596
  0.6 6.2 %copy-start.2 = (f32[8,128,128]{2,1,0:T(8,128)S(1)}, f32[8,128,128]{2,1,0:T(8,128)}, u32[]{:S(2)}) copy-start(f32[8,128,128]{2,1,0:T(8,128)} %grid_old.5) | copy-start | bytes 1572868
  0.7 6.2 %copy-start.1 = (bf16[2,8,3,128,128]{4,3,2,1,0:T(8,128)(2,1)S(1)}, bf16[2,8,3,128,128]{4,3,2,1,0:T(8,128)(2,1)}, u32[]{:S(2)}) copy-start(bf16[2,8,3,128,128]{4,3,2,1,0:T(8,128)(2,1)} %dens.5) | copy-start | bytes 4718596
  0.7 6.2 %copy-start.5 = (f32[8]{0:T(128)S(1)}, f32[8]{0:T(128)}, u32[]{:S(2)}) copy-start(f32[8]{0:T(128)} %absorption.7) | copy-start | bytes 100
  0.7 6.2 %copy-start.4 = (s32[8]{0:T(128)S(1)}, s32[8]{0:T(128)}, u32[]{:S(2)}) copy-start(s32[8]{0:T(128)} %leads.7) | copy-start | bytes 100
  2.2 8.4 %collective-permute-start = (bf16[6,128,128]{2,1,0:T(8,128)(2,1)S(1)}, bf16[6,128,128]{2,1,0:T(8,128)(2,1)S(1)}, u32[]{:S(2)}, u32[]{:S(2)}) collective-permute-start(bf16[6,128,128]{2,1,0:T(8,128)(2,1)S(1)} %get-tuple-element.34), channel_id=1, source_target_pairs={{0,1},{1,0},{2,3},{3,2},{4,5},{5,4},{6,7},{7,6},{8,9},{9,8},{10,11... | collective-permute-start | bytes 589832 | tf_op jit(solution)/shard_map/ppermute | solution.py:551
  2.3 9.0 %collective-permute-start.1 = (bf16[6,128,128]{2,1,0:T(8,128)(2,1)S(1)}, bf16[6,128,128]{2,1,0:T(8,128)(2,1)S(1)}, u32[]{:S(2)}, u32[]{:S(2)}) collective-permute-start(bf16[6,128,128]{2,1,0:T(8,128)(2,1)S(1)} %get-tuple-element.35), channel_id=1, source_target_pairs={{1,2},{2,1},{3,4},{4,3},{5,6},{6,5},{7,8},{8,7},{9,10},{10,9},{11,... | collective-permute-start | bytes 589832 | tf_op jit(solution)/shard_map/ppermute | solution.py:555
  6.9 0.7 %copy-start.3 = (s32[8,24]{1,0:T(8,128)S(1)}, s32[8,24]{1,0:T(8,128)}, u32[]{:S(2)}) copy-start(s32[8,24]{1,0:T(8,128)} %owners.1) | copy-start | bytes 2308
  7.6 17.1 %slice-start = ((s8[12582912]{0:T(1024)(128)(4,1)}), s8[4194304]{0:T(1024)(128)(4,1)S(1)}, s32[]{:S(2)}) async-start(s8[12582912]{0:T(1024)(128)(4,1)} %bitcast), calls=%async_computation | async-start | bytes 8388608
  7.6 17.1 %slice-start.1 = ((s8[12582912]{0:T(1024)(128)(4,1)}), s8[4194304]{0:T(1024)(128)(4,1)S(1)}, s32[]{:S(2)}) async-start(s8[12582912]{0:T(1024)(128)(4,1)} %bitcast), calls=%async_computation.1 | async-start | bytes 8388608
  11.4 13.3 %slice-start.2 = ((s8[12582912]{0:T(1024)(128)(4,1)}), s8[4194304]{0:T(1024)(128)(4,1)S(1)}, s32[]{:S(2)}) async-start(s8[12582912]{0:T(1024)(128)(4,1)} %bitcast), calls=%async_computation.2 | async-start | bytes 8388608
  15.0 9.6 %collective-permute-start.2 = (bf16[208,128]{1,0:T(8,128)(2,1)S(1)}, bf16[208,128]{1,0:T(8,128)(2,1)S(1)}, u32[]{:S(2)}, u32[]{:S(2)}) collective-permute-start(bf16[208,128]{1,0:T(8,128)(2,1)S(1)} %get-tuple-element.41), channel_id=1, source_target_pairs={{0,16},{1,17},{2,18},{3,19},{4,20},{5,21},{6,22},{7,23},{8,24},{9,... | collective-permute-start | bytes 159752 | tf_op jit(solution)/shard_map/ppermute | solution.py:634
  18.6 8.9 %collective-permute-start.4 = (bf16[208,128]{1,0:T(8,128)(2,1)S(1)}, bf16[208,128]{1,0:T(8,128)(2,1)S(1)}, u32[]{:S(2)}, u32[]{:S(2)}) collective-permute-start(bf16[208,128]{1,0:T(8,128)(2,1)S(1)} %get-tuple-element.44), channel_id=1, source_target_pairs={{0,20},{1,21},{2,22},{3,23},{4,16},{5,17},{6,18},{7,19},{8,28},{9,... | collective-permute-start | bytes 159752 | tf_op jit(solution)/shard_map/ppermute | solution.py:634
  20.1 8.9 %collective-permute-start.5 = (bf16[208,128]{1,0:T(8,128)(2,1)S(1)}, bf16[208,128]{1,0:T(8,128)(2,1)S(1)}, u32[]{:S(2)}, u32[]{:S(2)}) collective-permute-start(bf16[208,128]{1,0:T(8,128)(2,1)S(1)} %get-tuple-element.45), channel_id=1, source_target_pairs={{0,24},{1,25},{2,26},{3,27},{4,28},{5,29},{6,30},{7,31},{8,16},{9,... | collective-permute-start | bytes 159752 | tf_op jit(solution)/shard_map/ppermute | solution.py:634
  23.4 11.1 %collective-permute-start.8 = (bf16[208,128]{1,0:T(8,128)(2,1)S(1)}, bf16[208,128]{1,0:T(8,128)(2,1)S(1)}, u32[]{:S(2)}, u32[]{:S(2)}) collective-permute-start(bf16[208,128]{1,0:T(8,128)(2,1)S(1)} %get-tuple-element.48), channel_id=1, source_target_pairs={{0,28},{1,29},{2,30},{3,31},{4,24},{5,25},{6,26},{7,27},{8,20},{9,... | collective-permute-start | bytes 159752 | tf_op jit(solution)/shard_map/ppermute | solution.py:634
  23.5 12.3 %collective-permute-start.9 = (bf16[208,128]{1,0:T(8,128)(2,1)S(1)}, bf16[208,128]{1,0:T(8,128)(2,1)S(1)}, u32[]{:S(2)}, u32[]{:S(2)}) collective-permute-start(bf16[208,128]{1,0:T(8,128)(2,1)S(1)} %get-tuple-element.49), channel_id=1, source_target_pairs={{0,4},{1,5},{2,6},{3,7},{4,0},{5,1},{6,2},{7,3},{8,12},{9,13},{10,... | collective-permute-start | bytes 159752 | tf_op jit(solution)/shard_map/ppermute | solution.py:634
  24.6 12.9 %collective-permute-start.10 = (bf16[208,128]{1,0:T(8,128)(2,1)S(1)}, bf16[208,128]{1,0:T(8,128)(2,1)S(1)}, u32[]{:S(2)}, u32[]{:S(2)}) collective-permute-start(bf16[208,128]{1,0:T(8,128)(2,1)S(1)} %get-tuple-element.50), channel_id=1, source_target_pairs={{0,8},{1,9},{2,10},{3,11},{4,12},{5,13},{6,14},{7,15},{8,0},{9,1},... | collective-permute-start | bytes 159752 | tf_op jit(solution)/shard_map/ppermute | solution.py:634
  27.5 10.1 %collective-permute-start.11 = (bf16[208,128]{1,0:T(8,128)(2,1)S(1)}, bf16[208,128]{1,0:T(8,128)(2,1)S(1)}, u32[]{:S(2)}, u32[]{:S(2)}) collective-permute-start(bf16[208,128]{1,0:T(8,128)(2,1)S(1)} %get-tuple-element.51), channel_id=1, source_target_pairs={{0,12},{1,13},{2,14},{3,15},{4,8},{5,9},{6,10},{7,11},{8,4},{9,5},... | collective-permute-start | bytes 159752 | tf_op jit(solution)/shard_map/ppermute | solution.py:634
  29.0 15.4 %collective-permute-start.3 = (bf16[208,128]{1,0:T(8,128)(2,1)S(1)}, bf16[208,128]{1,0:T(8,128)(2,1)S(1)}, u32[]{:S(2)}, u32[]{:S(2)}) collective-permute-start(bf16[208,128]{1,0:T(8,128)(2,1)S(1)} %get-tuple-element.43), channel_id=1, source_target_pairs={{0,16},{1,17},{2,18},{3,19},{4,20},{5,21},{6,22},{7,23},{8,24},{9,... | collective-permute-start | bytes 159752 | tf_op jit(solution)/shard_map/ppermute | solution.py:634
  34.6 10.1 %collective-permute-start.7 = (bf16[208,128]{1,0:T(8,128)(2,1)S(1)}, bf16[208,128]{1,0:T(8,128)(2,1)S(1)}, u32[]{:S(2)}, u32[]{:S(2)}) collective-permute-start(bf16[208,128]{1,0:T(8,128)(2,1)S(1)} %get-tuple-element.47), channel_id=1, source_target_pairs={{0,24},{1,25},{2,26},{3,27},{4,28},{5,29},{6,30},{7,31},{8,16},{9,... | collective-permute-start | bytes 159752 | tf_op jit(solution)/shard_map/ppermute | solution.py:634
  35.8 10.7 %collective-permute-start.6 = (bf16[208,128]{1,0:T(8,128)(2,1)S(1)}, bf16[208,128]{1,0:T(8,128)(2,1)S(1)}, u32[]{:S(2)}, u32[]{:S(2)}) collective-permute-start(bf16[208,128]{1,0:T(8,128)(2,1)S(1)} %get-tuple-element.46.unread), channel_id=1, source_target_pairs={{0,20},{1,21},{2,22},{3,23},{4,16},{5,17},{6,18},{7,19},{8,28},{9,... | collective-permute-start | bytes 159752 | tf_op jit(solution)/shard_map/ppermute | solution.py:634
  42.2 10.6 %collective-permute-start.12 = (bf16[208,128]{1,0:T(8,128)(2,1)S(1)}, bf16[208,128]{1,0:T(8,128)(2,1)S(1)}, u32[]{:S(2)}, u32[]{:S(2)}) collective-permute-start(bf16[208,128]{1,0:T(8,128)(2,1)S(1)} %get-tuple-element.52), channel_id=1, source_target_pairs={{0,28},{1,29},{2,30},{3,31},{4,24},{5,25},{6,26},{7,27},{8,20},{9,... | collective-permute-start | bytes 159752 | tf_op jit(solution)/shard_map/ppermute | solution.py:634
  43.8 8.9 %collective-permute-start.13 = (bf16[208,128]{1,0:T(8,128)(2,1)S(1)}, bf16[208,128]{1,0:T(8,128)(2,1)S(1)}, u32[]{:S(2)}, u32[]{:S(2)}) collective-permute-start(bf16[208,128]{1,0:T(8,128)(2,1)S(1)} %get-tuple-element.53), channel_id=1, source_target_pairs={{0,4},{1,5},{2,6},{3,7},{4,0},{5,1},{6,2},{7,3},{8,12},{9,13},{10,... | collective-permute-start | bytes 159752 | tf_op jit(solution)/shard_map/ppermute | solution.py:634
  44.4 8.4 %collective-permute-start.14 = (bf16[208,128]{1,0:T(8,128)(2,1)S(1)}, bf16[208,128]{1,0:T(8,128)(2,1)S(1)}, u32[]{:S(2)}, u32[]{:S(2)}) collective-permute-start(bf16[208,128]{1,0:T(8,128)(2,1)S(1)} %get-tuple-element.54), channel_id=1, source_target_pairs={{0,8},{1,9},{2,10},{3,11},{4,12},{5,13},{6,14},{7,15},{8,0},{9,1},... | collective-permute-start | bytes 159752 | tf_op jit(solution)/shard_map/ppermute | solution.py:634
  44.6 8.2 %collective-permute-start.15 = (bf16[208,128]{1,0:T(8,128)(2,1)S(1)}, bf16[208,128]{1,0:T(8,128)(2,1)S(1)}, u32[]{:S(2)}, u32[]{:S(2)}) collective-permute-start(bf16[208,128]{1,0:T(8,128)(2,1)S(1)} %get-tuple-element.55), channel_id=1, source_target_pairs={{0,12},{1,13},{2,14},{3,15},{4,8},{5,9},{6,10},{7,11},{8,4},{9,5},... | collective-permute-start | bytes 159752 | tf_op jit(solution)/shard_map/ppermute | solution.py:634
  46.5 13.5 %collective-permute-start.18 = (bf16[6,128,128]{2,1,0:T(8,128)(2,1)S(1)}, bf16[6,128,128]{2,1,0:T(8,128)(2,1)S(1)}, u32[]{:S(2)}, u32[]{:S(2)}) collective-permute-start(bf16[6,128,128]{2,1,0:T(8,128)(2,1)S(1)} %get-tuple-element.59), channel_id=1, source_target_pairs={{1,2},{2,1},{3,4},{4,3},{5,6},{6,5},{7,8},{8,7},{9,10},{10,9},{11,... | collective-permute-start | bytes 589832 | tf_op jit(solution)/shard_map/ppermute | solution.py:555
  53.9 6.1 %collective-permute-start.17 = (bf16[1,128,128]{2,1,0:T(8,128)(2,1)S(1)}, bf16[1,128,128]{2,1,0:T(8,128)(2,1)S(1)}, u32[]{:S(2)}, u32[]{:S(2)}) collective-permute-start(bf16[1,128,128]{2,1,0:T(8,128)(2,1)S(1)} %get-tuple-element.58), channel_id=1, source_target_pairs={{1,2},{2,1},{3,4},{4,3},{5,6},{6,5},{7,8},{8,7},{9,10},{10,9},{11,... | collective-permute-start | bytes 98312 | tf_op jit(solution)/shard_map/ppermute | solution.py:555
  56.8 3.3 %collective-permute-start.16 = (bf16[7,128,128]{2,1,0:T(8,128)(2,1)S(1)}, bf16[7,128,128]{2,1,0:T(8,128)(2,1)S(1)}, u32[]{:S(2)}, u32[]{:S(2)}) collective-permute-start(bf16[7,128,128]{2,1,0:T(8,128)(2,1)S(1)} %get-tuple-element.57), channel_id=1, source_target_pairs={{0,1},{1,0},{2,3},{3,2},{4,5},{5,4},{6,7},{7,6},{8,9},{9,8},{10,11... | collective-permute-start | bytes 688136 | tf_op jit(solution)/shard_map/ppermute | solution.py:551

commit v5 on v4

--- a/solution.py
+++ b/solution.py
@@ -146,41 +146,29 @@
     return 0.5 * (value + value.T)
 
 
-def send_kernel(count, dens, core, grid_old, send_a, send_b, bands, grids, sems):
+def halo_message(q, q_far, h, h_far, grid):
+    h_re = (h[0].astype(F32) + symmetric(grid)).astype(BF16)
+    return [pack_hermitian(*q), *q_far, pack_hermitian(h_re, h[1]), *h_far]
+
+
+def send_kernel(count, dens, core, grid_old, send_b, bands, grid, sems):
+    even = lax.axis_index("col") % 2 == 0
     last = count - 1
-    places = [(dens, last, 1), (dens, last - 1, 2), (core, last, 1), (core, last, 0),
-              (dens, 0, 1), (dens, 1, 0), (core, 0, 1), (core, 0, 2)]
+    edge = jnp.where(even, 0, last)
+    next_edge = jnp.where(even, 1, last - 1)
+    places = [(dens, edge, 1), (dens, next_edge, jnp.where(even, 0, 2)),
+              (core, edge, 1), (core, edge, jnp.where(even, 2, 0))]
     copies = [
         pltpu.make_async_copy(ref.at[:, i, k], bands.at[n], sems.at[n]) for n, (ref, i, k) in enumerate(places)
     ]
-    copies += [
-        pltpu.make_async_copy(grid_old.at[i], grids.at[n], sems.at[8 + n]) for n, i in enumerate((last, 0))
-    ]
+    copies.append(pltpu.make_async_copy(grid_old.at[edge], grid, sems.at[4]))
     for copy in copies:
         copy.start()
     for copy in copies:
         copy.wait()
-
-    def message(first, grid):
-        h_re = (bands[first + 2, 0].astype(F32) + symmetric(grids[grid])).astype(BF16)
-        return [pack_hermitian(bands[first, 0], bands[first, 1]), bands[first + 1, 0], bands[first + 1, 1],
-                pack_hermitian(h_re, bands[first + 2, 1]), bands[first + 3, 0], bands[first + 3, 1]]
-
-    right = message(0, 0)
-    left = message(4, 1)
-    even = lax.axis_index("col") % 2 == 0
-
-    @pl.when(even)
-    def _():
-        for n, (x, y) in enumerate(zip(right, left)):
-            send_a[n] = x
-            send_b[n] = y
-
-    @pl.when(jnp.logical_not(even))
-    def _():
-        for n, (x, y) in enumerate(zip(right, left)):
-            send_a[n] = y
-            send_b[n] = x
+    pairs = [(bands[n, 0], bands[n, 1]) for n in range(4)]
+    for n, x in enumerate(halo_message(*pairs, grid[...])):
+        send_b[n] = x
 
 
 def partner(orders, n):
@@ -303,8 +291,25 @@
     which[...] = bricks
 
 
-def first_inner_kernel(count, leads, absorption, dens, core, grid_old, owners, hp_ref, half, place, which, moved_ref, wh_ref, left_ref, right_ref):
+def first_inner_kernel(count, leads, absorption, dens, core, grid_old, owners, hp_ref, half, place, which, send_a, moved_ref, wh_ref, left_ref, right_ref):
     brick_tables(count, owners, place, which)
+    even = lax.axis_index("col") % 2 == 0
+    last = count - 1
+
+    def put_message(edge, next_edge, near, far):
+        places = [(dens, edge, 1), (dens, next_edge, near), (core, edge, 1), (core, edge, far)]
+        pairs = [(ref[0, i, k], ref[1, i, k]) for ref, i, k in places]
+        for n, x in enumerate(halo_message(*pairs, grid_old[edge])):
+            send_a[n] = x
+
+    @pl.when(even)
+    def _():
+        put_message(last, last - 1, 2, 0)
+
+    @pl.when(jnp.logical_not(even))
+    def _():
+        put_message(0, 1, 0, 2)
+
     old_diagonals(range(count), count, leads, absorption, core, grid_old, left_ref, right_ref)
     get_left = band_access(count, core, None, None, None, None, left_ref)
     get_right = band_access(count, core, None, None, None, None, right_ref)
@@ -569,19 +574,19 @@
 
     message = jax.ShapeDtypeStruct((6, width, width), BF16)
     table = jax.ShapeDtypeStruct(brick_block.shape, jnp.int32)
-    send_a, send_b = call(
+    send_b = call(
         functools.partial(send_kernel, count),
-        (message, message),
+        message,
         flops=1 << 20,
         vmem=8,
         in_specs=[hbm] * 3,
         scratch=[
-            pltpu.VMEM((8, 2, width, width), BF16),
-            pltpu.VMEM((2, width, width), F32),
-            pltpu.SemaphoreType.DMA((10,)),
+            pltpu.VMEM((4, 2, width, width), BF16),
+            pltpu.VMEM((width, width), F32),
+            pltpu.SemaphoreType.DMA((5,)),
         ],
     )(*(in_hbm(x) for x in (density, core, grid_old)))
-    got_a, got_b = exchange_a(send_a, total), exchange_b(send_b, total)
+    got_b = exchange_b(send_b, total)
 
     def band_scratch(rows):
         return pltpu.VMEM((rows, 3, width, 2 * width), BF16)
@@ -592,15 +597,16 @@
     hp_shape = jax.ShapeDtypeStruct((count + 2, 3, width, 2 * width), BF16)
     inner_scratch = [band_scratch(count + 2)] * 2 + [sides(count + 2)] * 2
     outer_scratch = [band_scratch(count + 2)] * 3 + [sides(count + 2)] * 2
-    hp, half_inner, place, which = call(
+    hp, half_inner, place, which, send_a = call(
         functools.partial(first_inner_kernel, count),
-        (hp_shape, jax.ShapeDtypeStruct(density.shape, BF16), table, table),
+        (hp_shape, jax.ShapeDtypeStruct(density.shape, BF16), table, table, message),
         flops=PROP_FLOPS,
         vmem=16,
         scalars=2,
         in_specs=[vmem] * 4,
         scratch=inner_scratch,
     )(lead_blocks, absorption, density, core, grid_old, brick_block)
+    got_a = exchange_a(send_a, total)
     packed_rows = CAP * width // 2 + TILE
     packed_shape = jax.ShapeDtypeStruct((packed_rows, width), BF16)
     half_message = jax.ShapeDtypeStruct((6, width, width), BF16)

time: 65 us -> 64.6 us (level)
  waiting for transfers between devices: 0.74 us -> 1.47 us
  local copies, waits for them, and re-layouts: 0.71 us -> 0.04 us
    ppermute x14, starting transfers between devices: 21.1 us -> 20 us  [across(): return lax.ppermute(x, ('row', 'col'), pairs)]
    ppermute x3, starting transfers between devices: 13.6 us -> 14.5 us  [exchange_b(): lax.ppermute(x, ('row', 'col'), [(i, i + 1) if i % 2 else (i, i - 1) for...]
    unnamed x18, local copies, waits for them, and re-layouts: 0.71 us -> 0.04 us
  transfers between devices with their start and end apart: 19 -> 19, of which waited for: 1 -> 2; matrix products, arithmetic and copies ran while one was open for 0% -> 0% of each run, Pallas kernels for 28% -> 28%
where the time goes in v5:
time: 64.6 us; the launch traced here: 64 us
  starting transfers between devices  34.6 us (54%)
  Pallas kernels  26.7 us (41%)
  waiting for transfers between devices  1.47 us (2%)
  between operations  1.12 us (2%)
    ppermute x14, starting transfers between devices, across(): return lax.ppermute(x, ('row', 'col'), pairs)  20 us
    ppermute x3, starting transfers between devices, exchange_b(): lax.ppermute(x, ('row', 'col'), [(i, i + 1) if i % 2 else (i, i - 1) for...  14.5 us
    pallas_call x3, Pallas kernels, shards(): call(functools.partial(brick_kernel, points // 4, orders, numbers), (pack...  10.3 us
    pallas_call x1, Pallas kernels, shards(): call(functools.partial(second_outer_kernel, count), pltpu.HBM(density.sha...  3.72 us
    pallas_call x1, Pallas kernels, shards(): call(functools.partial(first_outer_kernel, count, orders), (jax.ShapeDtyp...  3.63 us
    pallas_call x1, Pallas kernels, shards(): call(functools.partial(first_inner_kernel, count), (hp_shape, jax.ShapeDt...  3.51 us
    pallas_call x1, Pallas kernels, shards(): call(functools.partial(second_inner_kernel, count), (jax.ShapeDtypeStruct...  3.17 us
  transfers between devices with their start and end apart: 19, of which 2 were waited for; matrix products, arithmetic and copies ran while one was open for 0% of the time, Pallas kernels for 28%

profile of v5, /device:TPU:1, one launch (start us, length us, event | category | flops | bytes accessed | tf_op | source)
XLA Modules:
  0.0 64.0 jit_solution(10984947520738596770)
XLA Ops:
  0.6 0.0 copy-start
  0.6 0.0 copy-start.2
  0.7 0.0 copy-start.1
  0.7 0.0 copy-start.5
  0.7 0.0 copy-start.4
  0.7 0.0 copy-start.3
  0.7 1.3 %shard_map.87 = bf16[6,128,128]{2,1,0:T(8,128)(2,1)S(1)} custom-call(bf16[2,8,3,128,128]{4,3,2,1,0:T(8,128)(2,1)} %dens.5, bf16[2,8,3,128,128]{4,3,2,1,0:T(8,128)(2,1)} %core.11, f32[8,128,128]{2,1,0:T(8,128)} %grid_old.5), custom_call_target="tpu_custom_call" | custom-call | flops 1048576 | bytes 4194304 | tf_op jit(solution)/shard_map/pallas_call | solution.py:577
  2.0 4.5 %collective-permute-start.1 = (bf16[6,128,128]{2,1,0:T(8,128)(2,1)S(1)}, bf16[6,128,128]{2,1,0:T(8,128)(2,1)S(1)}, u32[]{:S(2)}, u32[]{:S(2)}) collective-permute-start(bf16[6,128,128]{2,1,0:T(8,128)(2,1)S(1)} %shard_map.87), channel_id=1, source_target_pairs={{1,2},{2,1},{3,4},{4,3},{5,6},{6,5},{7,8},{8,7},{9,10},{10,9},{11,... | collective-permute-start | bytes 589832 | tf_op jit(solution)/shard_map/ppermute | solution.py:560
  6.5 0.0 copy-done
  6.5 0.0 copy-done.2
  6.5 0.0 copy-done.1
  6.5 0.0 copy-done.5
  6.5 0.0 copy-done.4
  6.6 0.0 copy-done.3
  6.6 0.0 slice-start
  6.6 0.0 slice-start.1
  6.6 3.5 %shard_map.86 = (bf16[10,3,128,256]{3,2,1,0:T(8,128)(2,1)S(1)}, bf16[2,8,3,128,128]{4,3,2,1,0:T(8,128)(2,1)S(1)}, s32[8,24]{1,0:T(8,128)S(1)}, s32[8,24]{1,0:T(8,128)S(1)}, bf16[6,128,128]{2,1,0:T(8,128)(2,1)S(1)}) custom-call(s32[8]{0:T(128)S(1)} %copy-done.4, f32[8]{0:T(128)S(1)} %copy-done.5, bf16[2,8,3,128,128]{4,3,2,1,0:T(8,128)(2,1)S(1)} %copy-done.1, ...), custom_call_target="tpu_custom_call" | custom-call | flops 4294967296 | bytes 4194304 | tf_op jit(solution)/shard_map/pallas_call | solution.py:600
  10.1 0.1 collective-permute-start
  10.2 0.9 %collective-permute-done.1.got_b.core_b = bf16[6,128,128]{2,1,0:T(8,128)(2,1)S(1)} collective-permute-done((bf16[6,128,128]{2,1,0:T(8,128)(2,1)S(1)}, bf16[6,128,128]{2,1,0:T(8,128)(2,1)S(1)}, u32[]{:S(2)}, u32[]{:S(2)}) %collective-permute-start.1) | collective-permute-done | bytes 196640 | tf_op jit(solution)/shard_map/ppermute | solution.py:560
  11.1 0.6 collective-permute-done.got_a.core_a
  11.6 3.6 %shard_map.88 = (bf16[2,8,3,128,128]{4,3,2,1,0:T(8,128)(2,1)S(1)}, bf16[6,128,128]{2,1,0:T(8,128)(2,1)S(1)}, bf16[208,128]{1,0:T(8,128)(2,1)S(1)}, bf16[208,128]...) custom-call(s32[8]{0:T(128)S(1)} %copy-done.4, ...), custom_call_target="tpu_custom_call" | custom-call | flops 4294967296 | bytes 4194304 | tf_op jit(solution)/shard_map/pallas_call | solution.py:613
  15.3 2.7 %collective-permute-start.2 = (bf16[208,128]{1,0:T(8,128)(2,1)S(1)}, bf16[208,128]{1,0:T(8,128)(2,1)S(1)}, u32[]{:S(2)}, u32[]{:S(2)}) collective-permute-start(bf16[208,128]{1,0:T(8,128)(2,1)S(1)} %get-tuple-element.39), channel_id=1, source_target_pairs={{0,16},{1,17},{2,18},{3,19},{4,20},{5,21},{6,22},{7,23},{8,24},{9,... | collective-permute-start | bytes 159752 | tf_op jit(solution)/shard_map/ppermute | solution.py:640
  17.9 1.3 %collective-permute-start.4 = (bf16[208,128]{1,0:T(8,128)(2,1)S(1)}, bf16[208,128]{1,0:T(8,128)(2,1)S(1)}, u32[]{:S(2)}, u32[]{:S(2)}) collective-permute-start(bf16[208,128]{1,0:T(8,128)(2,1)S(1)} %get-tuple-element.42), channel_id=1, source_target_pairs={{0,20},{1,21},{2,22},{3,23},{4,16},{5,17},{6,18},{7,19},{8,28},{9,... | collective-permute-start | bytes 159752 | tf_op jit(solution)/shard_map/ppermute | solution.py:640
  19.2 3.3 %collective-permute-start.5 = (bf16[208,128]{1,0:T(8,128)(2,1)S(1)}, bf16[208,128]{1,0:T(8,128)(2,1)S(1)}, u32[]{:S(2)}, u32[]{:S(2)}) collective-permute-start(bf16[208,128]{1,0:T(8,128)(2,1)S(1)} %get-tuple-element.43), channel_id=1, source_target_pairs={{0,24},{1,25},{2,26},{3,27},{4,28},{5,29},{6,30},{7,31},{8,16},{9,... | collective-permute-start | bytes 159752 | tf_op jit(solution)/shard_map/ppermute | solution.py:640
  22.5 0.0 collective-permute-start.8
  22.5 1.2 %collective-permute-start.9 = (bf16[208,128]{1,0:T(8,128)(2,1)S(1)}, bf16[208,128]{1,0:T(8,128)(2,1)S(1)}, u32[]{:S(2)}, u32[]{:S(2)}) collective-permute-start(bf16[208,128]{1,0:T(8,128)(2,1)S(1)} %get-tuple-element.47), channel_id=1, source_target_pairs={{0,4},{1,5},{2,6},{3,7},{4,0},{5,1},{6,2},{7,3},{8,12},{9,13},{10,... | collective-permute-start | bytes 159752 | tf_op jit(solution)/shard_map/ppermute | solution.py:640
  23.7 0.0 collective-permute-done.2.rest_1_
  23.7 0.0 collective-permute-start.10
  23.7 0.0 slice-done
  23.7 0.0 slice-done.1
  23.8 0.0 slice-done.2
  23.8 2.8 %shard_map.89 = (bf16[208,128]{1,0:T(8,128)(2,1)S(1)}, bf16[208,128]{1,0:T(8,128)(2,1)S(1)}) custom-call(s32[8,24]{1,0:T(8,128)S(1)} %get-tuple-element.37.which.unread, bf16[24,2048,128]{2,1,0:T(8,128)(2,1)S(1)} %bitcast.1, s32[8,24]{1,0:T(8,128)S(1)} %get-tuple-element.37.which.unread, bf16[208,128]{1,0:T(8,128)(2,1)S(1)} %get-tuple-element.38.rest_0_, ...), custom_call_target="tpu_custom_call" | custom-call | flops 805306368 | bytes 4194304 | tf_op jit(solution)/shard_map/pallas_call | solution.py:649
  26.6 0.0 collective-permute-done.4.rest_0_
  26.6 1.5 %collective-permute-start.11 = (bf16[208,128]{1,0:T(8,128)(2,1)S(1)}, bf16[208,128]{1,0:T(8,128)(2,1)S(1)}, u32[]{:S(2)}, u32[]{:S(2)}) collective-permute-start(bf16[208,128]{1,0:T(8,128)(2,1)S(1)} %get-tuple-element.49), channel_id=1, source_target_pairs={{0,12},{1,13},{2,14},{3,15},{4,8},{5,9},{6,10},{7,11},{8,4},{9,5},... | collective-permute-start | bytes 159752 | tf_op jit(solution)/shard_map/ppermute | solution.py:640
  28.1 0.0 collective-permute-done.5.rest_1_
  28.1 2.7 %collective-permute-start.3 = (bf16[208,128]{1,0:T(8,128)(2,1)S(1)}, bf16[208,128]{1,0:T(8,128)(2,1)S(1)}, u32[]{:S(2)}, u32[]{:S(2)}) collective-permute-start(bf16[208,128]{1,0:T(8,128)(2,1)S(1)} %get-tuple-element.41), channel_id=1, source_target_pairs={{0,16},{1,17},{2,18},{3,19},{4,20},{5,21},{6,22},{7,23},{8,24},{9,... | collective-permute-start | bytes 159752 | tf_op jit(solution)/shard_map/ppermute | solution.py:640
  30.8 2.8 %shard_map.90 = (bf16[208,128]{1,0:T(8,128)(2,1)S(1)}, bf16[208,128]{1,0:T(8,128)(2,1)S(1)}) custom-call(s32[8,24]{1,0:T(8,128)S(1)} %get-tuple-element.37.which.unread, bf16[24,2048,128]{2,1,0:T(8,128)(2,1)S(1)} %bitcast.1, bf16[208,128]{1,0:T(8,128)(2,1)S(1)} %get-tuple-element.40.unread.rest_0_, bf16[208,128]{1,0:T(8,128)(2,1)S(1)} %collective-permute-done.4.rest_0_, ...), custom_call_target="tpu_custom_call" | custom-call | flops 805306368 | bytes 4194304 | tf_op jit(solution)/shard_map/pallas_call | solution.py:649
  33.6 0.0 collective-permute-done.8.rest_0_
  33.7 1.2 %collective-permute-start.7 = (bf16[208,128]{1,0:T(8,128)(2,1)S(1)}, bf16[208,128]{1,0:T(8,128)(2,1)S(1)}, u32[]{:S(2)}, u32[]{:S(2)}) collective-permute-start(bf16[208,128]{1,0:T(8,128)(2,1)S(1)} %get-tuple-element.45), channel_id=1, source_target_pairs={{0,24},{1,25},{2,26},{3,27},{4,28},{5,29},{6,30},{7,31},{8,16},{9,... | collective-permute-start | bytes 159752 | tf_op jit(solution)/shard_map/ppermute | solution.py:640
  34.9 0.0 collective-permute-done.9.rest_1_
  34.9 1.8 %collective-permute-start.6 = (bf16[208,128]{1,0:T(8,128)(2,1)S(1)}, bf16[208,128]{1,0:T(8,128)(2,1)S(1)}, u32[]{:S(2)}, u32[]{:S(2)}) collective-permute-start(bf16[208,128]{1,0:T(8,128)(2,1)S(1)} %get-tuple-element.44.unread), channel_id=1, source_target_pairs={{0,20},{1,21},{2,22},{3,23},{4,16},{5,17},{6,18},{7,19},{8,28},{9,... | collective-permute-start | bytes 159752 | tf_op jit(solution)/shard_map/ppermute | solution.py:640
  36.7 0.0 collective-permute-done.10.rest_2_
  36.7 0.0 collective-permute-done.11.rest_3_
  36.7 4.6 %shard_map.91 = (bf16[208,128]{1,0:T(8,128)(2,1)S(1)}, bf16[208,128]{1,0:T(8,128)(2,1)S(1)}, bf16[208,128]{1,0:T(8,128)(2,1)S(1)}, bf16[208,128]{1,0:T(8,128)(2,1)S(1)}) custom-call(s32[8,24]{1,0:T(8,128)S(1)} %get-tuple-element.37.which.unread, bf16[24,2048,128]{2,1,0:T(8,128)(2,1)S(1)} %bitcast.1, bf16[208,128]{1,0:T(8,128)(2,1)S(1)} %get-tuple-element.44.unread, ...), custom_call_target="tpu_custom_call" | custom-call | flops 1610612736 | bytes 4194304 | tf_op jit(solution)/shard_map/pallas_call | solution.py:649
  41.3 1.6 %collective-permute-start.12 = (bf16[208,128]{1,0:T(8,128)(2,1)S(1)}, bf16[208,128]{1,0:T(8,128)(2,1)S(1)}, u32[]{:S(2)}, u32[]{:S(2)}) collective-permute-start(bf16[208,128]{1,0:T(8,128)(2,1)S(1)} %get-tuple-element.50), channel_id=1, source_target_pairs={{0,28},{1,29},{2,30},{3,31},{4,24},{5,25},{6,26},{7,27},{8,20},{9,... | collective-permute-start | bytes 159752 | tf_op jit(solution)/shard_map/ppermute | solution.py:640
  42.9 0.6 collective-permute-start.13
  43.5 0.0 collective-permute-done.3.rest_1_
  43.5 0.2 collective-permute-start.14
  43.7 0.0 collective-permute-done.7.rest_3_
  43.7 1.9 %collective-permute-start.15 = (bf16[208,128]{1,0:T(8,128)(2,1)S(1)}, bf16[208,128]{1,0:T(8,128)(2,1)S(1)}, u32[]{:S(2)}, u32[]{:S(2)}) collective-permute-start(bf16[208,128]{1,0:T(8,128)(2,1)S(1)} %get-tuple-element.53), channel_id=1, source_target_pairs={{0,12},{1,13},{2,14},{3,15},{4,8},{5,9},{6,10},{7,11},{8,4},{9,5},... | collective-permute-start | bytes 159752 | tf_op jit(solution)/shard_map/ppermute | solution.py:640
  45.6 0.0 collective-permute-done.6.rest_2_
  45.6 5.8 %collective-permute-start.18 = (bf16[6,128,128]{2,1,0:T(8,128)(2,1)S(1)}, bf16[6,128,128]{2,1,0:T(8,128)(2,1)S(1)}, u32[]{:S(2)}, u32[]{:S(2)}) collective-permute-start(bf16[6,128,128]{2,1,0:T(8,128)(2,1)S(1)} %get-tuple-element.57), channel_id=1, source_target_pairs={{1,2},{2,1},{3,4},{4,3},{5,6},{6,5},{7,8},{8,7},{9,10},{10,9},{11,... | collective-permute-start | bytes 589832 | tf_op jit(solution)/shard_map/ppermute | solution.py:560
  51.4 0.0 collective-permute-done.12.rest_4_
  51.4 0.0 collective-permute-done.13.rest_5_
  51.5 0.0 collective-permute-done.14.rest_6_
  51.5 0.0 collective-permute-done.15.rest_7_
  51.5 1.1 %shard_map.92 = (f32[8,128,128]{2,1,0:T(8,128)S(1)}, bf16[8,128,128]{2,1,0:T(8,128)(2,1)S(1)}, bf16[7,128,128]{2,1,0:T(8,128)(2,1)S(1)}, bf16[1,128,128]{2,1,0:T(8,128)(2,1)S(1)}) custom-call(s32[8,24]{1,0:T(8,128)S(1)} %get-tuple-element.32.place, bf16[2,8,3,128,128]{4,3,2,1,0:T(8,128)(2,1)S(1)} %copy-done, ...), custom_call_target="tpu_custom_call" | custom-call | flops 1048576 | bytes 4194304 | tf_op jit(solution)/shard_map/pallas_call | solution.py:660
  52.6 4.2 %collective-permute-start.17 = (bf16[1,128,128]{2,1,0:T(8,128)(2,1)S(1)}, bf16[1,128,128]{2,1,0:T(8,128)(2,1)S(1)}, u32[]{:S(2)}, u32[]{:S(2)}) collective-permute-start(bf16[1,128,128]{2,1,0:T(8,128)(2,1)S(1)} %get-tuple-element.56), channel_id=1, source_target_pairs={{1,2},{2,1},{3,4},{4,3},{5,6},{6,5},{7,8},{8,7},{9,10},{10,9},{11,... | collective-permute-start | bytes 98312 | tf_op jit(solution)/shard_map/ppermute | solution.py:560
  56.8 0.1 collective-permute-start.16
  56.9 3.2 %shard_map.93 = (bf16[2,4,3,128,128]{4,3,2,1,0:T(8,128)(2,1)S(1)}, bf16[10,3,128,256]{3,2,1,0:T(8,128)(2,1)S(1)}, f32[8,128,128]{2,1,0:T(8,128)}) custom-call(s32[8]{0:T(128)S(1)} %copy-done.4, f32[8]{0:T(128)S(1)} %copy-done.5, bf16[2,8,3,128,128]{4,3,2,1,0:T(8,128)(2,1)S(1)} %get-tuple-element.36.half, bf16[2,8,3,128,128]{4,3,2,1,0:T(8,128)(2,1)S(1)} %copy-done, ...), custom_call_target="tpu_custom_call" | custom-call | flops 4294967296 | bytes 4194304 | tf_op jit(solution)/shard_map/pallas_call | solution.py:677
  60.1 0.0 collective-permute-done.17.got_b
  60.1 0.0 collective-permute-done.18.half_b
  60.1 0.0 collective-permute-done.16.got_a
  60.1 3.7 %shard_map.94 = bf16[2,8,3,128,128]{4,3,2,1,0:T(8,128)(2,1)} custom-call(s32[8]{0:T(128)S(1)} %copy-done.4, f32[8]{0:T(128)S(1)} %copy-done.5, bf16[2,8,3,128,128]{4,3,2,1,0:T(8,128)(2,1)S(1)} %get-tuple-element.36.half, bf16[2,8,3,128,128]{4,3,2,1,0:T(8,128)(2,1)S(1)} %copy-done, bf16[8,128,128]{2,1,0:T(8,128)(2,1)S(1)} %get-tuple-element.54.diag_new, ...), custom_call_target="tpu_custom_call" | custom-call | flops 4294967296 | bytes 4194304 | tf_op jit(solution)/shard_map/pallas_call | solution.py:691
  (2 shorter events, 0.0 us)
Async XLA Ops:
  0.6 5.9 %copy-start = (bf16[2,8,3,128,128]{4,3,2,1,0:T(8,128)(2,1)S(1)}, bf16[2,8,3,128,128]{4,3,2,1,0:T(8,128)(2,1)}, u32[]{:S(2)}) copy-start(bf16[2,8,3,128,128]{4,3,2,1,0:T(8,128)(2,1)} %core.11) | copy-start | bytes 4718596
  0.6 5.9 %copy-start.2 = (f32[8,128,128]{2,1,0:T(8,128)S(1)}, f32[8,128,128]{2,1,0:T(8,128)}, u32[]{:S(2)}) copy-start(f32[8,128,128]{2,1,0:T(8,128)} %grid_old.5) | copy-start | bytes 1572868
  0.7 5.9 %copy-start.1 = (bf16[2,8,3,128,128]{4,3,2,1,0:T(8,128)(2,1)S(1)}, bf16[2,8,3,128,128]{4,3,2,1,0:T(8,128)(2,1)}, u32[]{:S(2)}) copy-start(bf16[2,8,3,128,128]{4,3,2,1,0:T(8,128)(2,1)} %dens.5) | copy-start | bytes 4718596
  0.7 5.9 %copy-start.5 = (f32[8]{0:T(128)S(1)}, f32[8]{0:T(128)}, u32[]{:S(2)}) copy-start(f32[8]{0:T(128)} %absorption.7) | copy-start | bytes 100
  0.7 5.9 %copy-start.4 = (s32[8]{0:T(128)S(1)}, s32[8]{0:T(128)}, u32[]{:S(2)}) copy-start(s32[8]{0:T(128)} %leads.7) | copy-start | bytes 100
  0.7 5.9 %copy-start.3 = (s32[8,24]{1,0:T(8,128)S(1)}, s32[8,24]{1,0:T(8,128)}, u32[]{:S(2)}) copy-start(s32[8,24]{1,0:T(8,128)} %owners.1) | copy-start | bytes 2308
  2.0 9.1 %collective-permute-start.1 = (bf16[6,128,128]{2,1,0:T(8,128)(2,1)S(1)}, bf16[6,128,128]{2,1,0:T(8,128)(2,1)S(1)}, u32[]{:S(2)}, u32[]{:S(2)}) collective-permute-start(bf16[6,128,128]{2,1,0:T(8,128)(2,1)S(1)} %shard_map.87), channel_id=1, source_target_pairs={{1,2},{2,1},{3,4},{4,3},{5,6},{6,5},{7,8},{8,7},{9,10},{10,9},{11,... | collective-permute-start | bytes 589832 | tf_op jit(solution)/shard_map/ppermute | solution.py:560
  6.6 17.2 %slice-start = ((s8[12582912]{0:T(1024)(128)(4,1)}), s8[4194304]{0:T(1024)(128)(4,1)S(1)}, s32[]{:S(2)}) async-start(s8[12582912]{0:T(1024)(128)(4,1)} %bitcast), calls=%async_computation | async-start | bytes 8388608
  6.6 17.2 %slice-start.1 = ((s8[12582912]{0:T(1024)(128)(4,1)}), s8[4194304]{0:T(1024)(128)(4,1)S(1)}, s32[]{:S(2)}) async-start(s8[12582912]{0:T(1024)(128)(4,1)} %bitcast), calls=%async_computation.1 | async-start | bytes 8388608
  10.1 1.5 %collective-permute-start = (bf16[6,128,128]{2,1,0:T(8,128)(2,1)S(1)}, bf16[6,128,128]{2,1,0:T(8,128)(2,1)S(1)}, u32[]{:S(2)}, u32[]{:S(2)}) collective-permute-start(bf16[6,128,128]{2,1,0:T(8,128)(2,1)S(1)} %get-tuple-element.33), channel_id=1, source_target_pairs={{0,1},{1,0},{2,3},{3,2},{4,5},{5,4},{6,7},{7,6},{8,9},{9,8},{10,11... | collective-permute-start | bytes 589832 | tf_op jit(solution)/shard_map/ppermute | solution.py:556
  11.6 12.1 %slice-start.2 = ((s8[12582912]{0:T(1024)(128)(4,1)}), s8[4194304]{0:T(1024)(128)(4,1)S(1)}, s32[]{:S(2)}) async-start(s8[12582912]{0:T(1024)(128)(4,1)} %bitcast), calls=%async_computation.2 | async-start | bytes 8388608
  15.3 8.5 %collective-permute-start.2 = (bf16[208,128]{1,0:T(8,128)(2,1)S(1)}, bf16[208,128]{1,0:T(8,128)(2,1)S(1)}, u32[]{:S(2)}, u32[]{:S(2)}) collective-permute-start(bf16[208,128]{1,0:T(8,128)(2,1)S(1)} %get-tuple-element.39), channel_id=1, source_target_pairs={{0,16},{1,17},{2,18},{3,19},{4,20},{5,21},{6,22},{7,23},{8,24},{9,... | collective-permute-start | bytes 159752 | tf_op jit(solution)/shard_map/ppermute | solution.py:640
  17.9 8.7 %collective-permute-start.4 = (bf16[208,128]{1,0:T(8,128)(2,1)S(1)}, bf16[208,128]{1,0:T(8,128)(2,1)S(1)}, u32[]{:S(2)}, u32[]{:S(2)}) collective-permute-start(bf16[208,128]{1,0:T(8,128)(2,1)S(1)} %get-tuple-element.42), channel_id=1, source_target_pairs={{0,20},{1,21},{2,22},{3,23},{4,16},{5,17},{6,18},{7,19},{8,28},{9,... | collective-permute-start | bytes 159752 | tf_op jit(solution)/shard_map/ppermute | solution.py:640
  19.2 8.9 %collective-permute-start.5 = (bf16[208,128]{1,0:T(8,128)(2,1)S(1)}, bf16[208,128]{1,0:T(8,128)(2,1)S(1)}, u32[]{:S(2)}, u32[]{:S(2)}) collective-permute-start(bf16[208,128]{1,0:T(8,128)(2,1)S(1)} %get-tuple-element.43), channel_id=1, source_target_pairs={{0,24},{1,25},{2,26},{3,27},{4,28},{5,29},{6,30},{7,31},{8,16},{9,... | collective-permute-start | bytes 159752 | tf_op jit(solution)/shard_map/ppermute | solution.py:640
  22.5 11.1 %collective-permute-start.8 = (bf16[208,128]{1,0:T(8,128)(2,1)S(1)}, bf16[208,128]{1,0:T(8,128)(2,1)S(1)}, u32[]{:S(2)}, u32[]{:S(2)}) collective-permute-start(bf16[208,128]{1,0:T(8,128)(2,1)S(1)} %get-tuple-element.46), channel_id=1, source_target_pairs={{0,28},{1,29},{2,30},{3,31},{4,24},{5,25},{6,26},{7,27},{8,20},{9,... | collective-permute-start | bytes 159752 | tf_op jit(solution)/shard_map/ppermute | solution.py:640
  22.5 12.3 %collective-permute-start.9 = (bf16[208,128]{1,0:T(8,128)(2,1)S(1)}, bf16[208,128]{1,0:T(8,128)(2,1)S(1)}, u32[]{:S(2)}, u32[]{:S(2)}) collective-permute-start(bf16[208,128]{1,0:T(8,128)(2,1)S(1)} %get-tuple-element.47), channel_id=1, source_target_pairs={{0,4},{1,5},{2,6},{3,7},{4,0},{5,1},{6,2},{7,3},{8,12},{9,13},{10,... | collective-permute-start | bytes 159752 | tf_op jit(solution)/shard_map/ppermute | solution.py:640
  23.7 12.9 %collective-permute-start.10 = (bf16[208,128]{1,0:T(8,128)(2,1)S(1)}, bf16[208,128]{1,0:T(8,128)(2,1)S(1)}, u32[]{:S(2)}, u32[]{:S(2)}) collective-permute-start(bf16[208,128]{1,0:T(8,128)(2,1)S(1)} %get-tuple-element.48), channel_id=1, source_target_pairs={{0,8},{1,9},{2,10},{3,11},{4,12},{5,13},{6,14},{7,15},{8,0},{9,1},... | collective-permute-start | bytes 159752 | tf_op jit(solution)/shard_map/ppermute | solution.py:640
  26.6 10.1 %collective-permute-start.11 = (bf16[208,128]{1,0:T(8,128)(2,1)S(1)}, bf16[208,128]{1,0:T(8,128)(2,1)S(1)}, u32[]{:S(2)}, u32[]{:S(2)}) collective-permute-start(bf16[208,128]{1,0:T(8,128)(2,1)S(1)} %get-tuple-element.49), channel_id=1, source_target_pairs={{0,12},{1,13},{2,14},{3,15},{4,8},{5,9},{6,10},{7,11},{8,4},{9,5},... | collective-permute-start | bytes 159752 | tf_op jit(solution)/shard_map/ppermute | solution.py:640
  28.1 15.4 %collective-permute-start.3 = (bf16[208,128]{1,0:T(8,128)(2,1)S(1)}, bf16[208,128]{1,0:T(8,128)(2,1)S(1)}, u32[]{:S(2)}, u32[]{:S(2)}) collective-permute-start(bf16[208,128]{1,0:T(8,128)(2,1)S(1)} %get-tuple-element.41), channel_id=1, source_target_pairs={{0,16},{1,17},{2,18},{3,19},{4,20},{5,21},{6,22},{7,23},{8,24},{9,... | collective-permute-start | bytes 159752 | tf_op jit(solution)/shard_map/ppermute | solution.py:640
  33.7 10.1 %collective-permute-start.7 = (bf16[208,128]{1,0:T(8,128)(2,1)S(1)}, bf16[208,128]{1,0:T(8,128)(2,1)S(1)}, u32[]{:S(2)}, u32[]{:S(2)}) collective-permute-start(bf16[208,128]{1,0:T(8,128)(2,1)S(1)} %get-tuple-element.45), channel_id=1, source_target_pairs={{0,24},{1,25},{2,26},{3,27},{4,28},{5,29},{6,30},{7,31},{8,16},{9,... | collective-permute-start | bytes 159752 | tf_op jit(solution)/shard_map/ppermute | solution.py:640
  34.9 10.7 %collective-permute-start.6 = (bf16[208,128]{1,0:T(8,128)(2,1)S(1)}, bf16[208,128]{1,0:T(8,128)(2,1)S(1)}, u32[]{:S(2)}, u32[]{:S(2)}) collective-permute-start(bf16[208,128]{1,0:T(8,128)(2,1)S(1)} %get-tuple-element.44.unread), channel_id=1, source_target_pairs={{0,20},{1,21},{2,22},{3,23},{4,16},{5,17},{6,18},{7,19},{8,28},{9,... | collective-permute-start | bytes 159752 | tf_op jit(solution)/shard_map/ppermute | solution.py:640
  41.3 10.1 %collective-permute-start.12 = (bf16[208,128]{1,0:T(8,128)(2,1)S(1)}, bf16[208,128]{1,0:T(8,128)(2,1)S(1)}, u32[]{:S(2)}, u32[]{:S(2)}) collective-permute-start(bf16[208,128]{1,0:T(8,128)(2,1)S(1)} %get-tuple-element.50), channel_id=1, source_target_pairs={{0,28},{1,29},{2,30},{3,31},{4,24},{5,25},{6,26},{7,27},{8,20},{9,... | collective-permute-start | bytes 159752 | tf_op jit(solution)/shard_map/ppermute | solution.py:640
  42.9 8.5 %collective-permute-start.13 = (bf16[208,128]{1,0:T(8,128)(2,1)S(1)}, bf16[208,128]{1,0:T(8,128)(2,1)S(1)}, u32[]{:S(2)}, u32[]{:S(2)}) collective-permute-start(bf16[208,128]{1,0:T(8,128)(2,1)S(1)} %get-tuple-element.51), channel_id=1, source_target_pairs={{0,4},{1,5},{2,6},{3,7},{4,0},{5,1},{6,2},{7,3},{8,12},{9,13},{10,... | collective-permute-start | bytes 159752 | tf_op jit(solution)/shard_map/ppermute | solution.py:640
  43.5 7.9 %collective-permute-start.14 = (bf16[208,128]{1,0:T(8,128)(2,1)S(1)}, bf16[208,128]{1,0:T(8,128)(2,1)S(1)}, u32[]{:S(2)}, u32[]{:S(2)}) collective-permute-start(bf16[208,128]{1,0:T(8,128)(2,1)S(1)} %get-tuple-element.52), channel_id=1, source_target_pairs={{0,8},{1,9},{2,10},{3,11},{4,12},{5,13},{6,14},{7,15},{8,0},{9,1},... | collective-permute-start | bytes 159752 | tf_op jit(solution)/shard_map/ppermute | solution.py:640
  43.7 7.7 %collective-permute-start.15 = (bf16[208,128]{1,0:T(8,128)(2,1)S(1)}, bf16[208,128]{1,0:T(8,128)(2,1)S(1)}, u32[]{:S(2)}, u32[]{:S(2)}) collective-permute-start(bf16[208,128]{1,0:T(8,128)(2,1)S(1)} %get-tuple-element.53), channel_id=1, source_target_pairs={{0,12},{1,13},{2,14},{3,15},{4,8},{5,9},{6,10},{7,11},{8,4},{9,5},... | collective-permute-start | bytes 159752 | tf_op jit(solution)/shard_map/ppermute | solution.py:640
  45.6 14.5 %collective-permute-start.18 = (bf16[6,128,128]{2,1,0:T(8,128)(2,1)S(1)}, bf16[6,128,128]{2,1,0:T(8,128)(2,1)S(1)}, u32[]{:S(2)}, u32[]{:S(2)}) collective-permute-start(bf16[6,128,128]{2,1,0:T(8,128)(2,1)S(1)} %get-tuple-element.57), channel_id=1, source_target_pairs={{1,2},{2,1},{3,4},{4,3},{5,6},{6,5},{7,8},{8,7},{9,10},{10,9},{11,... | collective-permute-start | bytes 589832 | tf_op jit(solution)/shard_map/ppermute | solution.py:560
  52.6 7.5 %collective-permute-start.17 = (bf16[1,128,128]{2,1,0:T(8,128)(2,1)S(1)}, bf16[1,128,128]{2,1,0:T(8,128)(2,1)S(1)}, u32[]{:S(2)}, u32[]{:S(2)}) collective-permute-start(bf16[1,128,128]{2,1,0:T(8,128)(2,1)S(1)} %get-tuple-element.56), channel_id=1, source_target_pairs={{1,2},{2,1},{3,4},{4,3},{5,6},{6,5},{7,8},{8,7},{9,10},{10,9},{11,... | collective-permute-start | bytes 98312 | tf_op jit(solution)/shard_map/ppermute | solution.py:560
  56.8 3.3 %collective-permute-start.16 = (bf16[7,128,128]{2,1,0:T(8,128)(2,1)S(1)}, bf16[7,128,128]{2,1,0:T(8,128)(2,1)S(1)}, u32[]{:S(2)}, u32[]{:S(2)}) collective-permute-start(bf16[7,128,128]{2,1,0:T(8,128)(2,1)S(1)} %get-tuple-element.55), channel_id=1, source_target_pairs={{0,1},{1,0},{2,3},{3,2},{4,5},{5,4},{6,7},{7,6},{8,9},{9,8},{10,11... | collective-permute-start | bytes 688136 | tf_op jit(solution)/shard_map/ppermute | solution.py:556

commit v6 on v5

--- a/solution.py
+++ b/solution.py
@@ -655,7 +655,7 @@
             in_specs=[vmem, pl.BlockSpec(memory_space=pl.ANY)] + [vmem] * len(numbers),
         )(which, collocation, before, *(incoming[number] for number in numbers))
         arriving += [across(x, number) for number, x in zip(numbers, returned)]
-        before = returned[0]
+        before = half_b if numbers[-1] + 4 >= row_size - 1 else returned[0]
 
     term, diag_new, send_a, send_b = call(
         functools.partial(collect_kernel, count, orders),

time: 64.6 us -> 68 us (1.053)
  the two profiles are of different devices: /device:TPU:1 before, /device:TPU:15 now
where the time goes in v6:
time: 68 us; the launch traced here: 67.9 us
  starting transfers between devices  35.5 us (52%)
  Pallas kernels  26.5 us (39%)
  waiting for transfers between devices  4.67 us (7%)
  between operations  1.06 us (2%)
    ppermute x14, starting transfers between devices, across(): return lax.ppermute(x, ('row', 'col'), pairs)  18.4 us
    ppermute x3, starting transfers between devices, exchange_b(): lax.ppermute(x, ('row', 'col'), [(i, i + 1) if i % 2 else (i, i - 1) for...  17 us
    pallas_call x3, Pallas kernels, shards(): call(functools.partial(brick_kernel, points // 4, orders, numbers), (pack...  10.3 us
    pallas_call x1, Pallas kernels, shards(): call(functools.partial(second_outer_kernel, count), pltpu.HBM(density.sha...  3.72 us
    pallas_call x1, Pallas kernels, shards(): call(functools.partial(first_inner_kernel, count), (hp_shape, jax.ShapeDt...  3.52 us
    pallas_call x1, Pallas kernels, shards(): call(functools.partial(first_outer_kernel, count, orders), (jax.ShapeDtyp...  3.46 us
    pallas_call x1, Pallas kernels, shards(): call(functools.partial(second_inner_kernel, count), (jax.ShapeDtypeStruct...  3.17 us
    ppermute x14, waiting for transfers between devices, across(): return lax.ppermute(x, ('row', 'col'), pairs)  3.15 us
  transfers between devices with their start and end apart: 19, of which 3 were waited for; matrix products, arithmetic and copies ran while one was open for 0% of the time, Pallas kernels for 25%

profile of v6, /device:TPU:15, one launch (start us, length us, event | category | flops | bytes accessed | tf_op | source)
XLA Modules:
  0.0 67.9 jit_solution(10910537209134940376)
XLA Ops:
  0.6 0.0 copy-start
  0.6 0.0 copy-start.2
  0.7 0.0 copy-start.1
  0.7 0.0 copy-start.5
  0.7 0.0 copy-start.4
  0.7 0.0 copy-start.3
  0.7 1.3 %shard_map.87 = bf16[6,128,128]{2,1,0:T(8,128)(2,1)S(1)} custom-call(bf16[2,8,3,128,128]{4,3,2,1,0:T(8,128)(2,1)} %dens.5, bf16[2,8,3,128,128]{4,3,2,1,0:T(8,128)(2,1)} %core.11, f32[8,128,128]{2,1,0:T(8,128)} %grid_old.5), custom_call_target="tpu_custom_call" | custom-call | flops 1048576 | bytes 4194304 | tf_op jit(solution)/shard_map/pallas_call | solution.py:577
  2.0 3.7 %collective-permute-start.1 = (bf16[6,128,128]{2,1,0:T(8,128)(2,1)S(1)}, bf16[6,128,128]{2,1,0:T(8,128)(2,1)S(1)}, u32[]{:S(2)}, u32[]{:S(2)}) collective-permute-start(bf16[6,128,128]{2,1,0:T(8,128)(2,1)S(1)} %shard_map.87), channel_id=1, source_target_pairs={{1,2},{2,1},{3,4},{4,3},{5,6},{6,5},{7,8},{8,7},{9,10},{10,9},{11,... | collective-permute-start | bytes 589832 | tf_op jit(solution)/shard_map/ppermute | solution.py:560
  5.7 0.0 copy-done
  5.7 0.0 copy-done.2
  5.7 0.0 copy-done.1
  5.7 0.0 copy-done.5
  5.7 0.0 copy-done.4
  5.7 0.0 copy-done.3
  5.7 0.0 slice-start
  5.7 0.0 slice-start.1
  5.8 3.5 %shard_map.86 = (bf16[10,3,128,256]{3,2,1,0:T(8,128)(2,1)S(1)}, bf16[2,8,3,128,128]{4,3,2,1,0:T(8,128)(2,1)S(1)}, s32[8,24]{1,0:T(8,128)S(1)}, s32[8,24]{1,0:T(8,128)S(1)}, bf16[6,128,128]{2,1,0:T(8,128)(2,1)S(1)}) custom-call(s32[8]{0:T(128)S(1)} %copy-done.4, f32[8]{0:T(128)S(1)} %copy-done.5, bf16[2,8,3,128,128]{4,3,2,1,0:T(8,128)(2,1)S(1)} %copy-done.1, ...), custom_call_target="tpu_custom_call" | custom-call | flops 4294967296 | bytes 4194304 | tf_op jit(solution)/shard_map/pallas_call | solution.py:600
  9.3 0.1 collective-permute-start
  9.4 1.5 %collective-permute-done.1.got_b.core_b = bf16[6,128,128]{2,1,0:T(8,128)(2,1)S(1)} collective-permute-done((bf16[6,128,128]{2,1,0:T(8,128)(2,1)S(1)}, bf16[6,128,128]{2,1,0:T(8,128)(2,1)S(1)}, u32[]{:S(2)}, u32[]{:S(2)}) %collective-permute-start.1) | collective-permute-done | bytes 196640 | tf_op jit(solution)/shard_map/ppermute | solution.py:560
  10.9 0.0 collective-permute-done.got_a.core_a
  10.9 3.5 %shard_map.88 = (bf16[2,8,3,128,128]{4,3,2,1,0:T(8,128)(2,1)S(1)}, bf16[6,128,128]{2,1,0:T(8,128)(2,1)S(1)}, bf16[208,128]{1,0:T(8,128)(2,1)S(1)}, bf16[208,128]...) custom-call(s32[8]{0:T(128)S(1)} %copy-done.4, ...), custom_call_target="tpu_custom_call" | custom-call | flops 4294967296 | bytes 4194304 | tf_op jit(solution)/shard_map/pallas_call | solution.py:613
  14.4 0.8 %collective-permute-start.2 = (bf16[208,128]{1,0:T(8,128)(2,1)S(1)}, bf16[208,128]{1,0:T(8,128)(2,1)S(1)}, u32[]{:S(2)}, u32[]{:S(2)}) collective-permute-start(bf16[208,128]{1,0:T(8,128)(2,1)S(1)} %get-tuple-element.39), channel_id=1, source_target_pairs={{0,16},{1,17},{2,18},{3,19},{4,20},{5,21},{6,22},{7,23},{8,24},{9,... | collective-permute-start | bytes 159752 | tf_op jit(solution)/shard_map/ppermute | solution.py:640
  15.2 3.1 %collective-permute-start.8 = (bf16[6,128,128]{2,1,0:T(8,128)(2,1)S(1)}, bf16[6,128,128]{2,1,0:T(8,128)(2,1)S(1)}, u32[]{:S(2)}, u32[]{:S(2)}) collective-permute-start(bf16[6,128,128]{2,1,0:T(8,128)(2,1)S(1)} %get-tuple-element.46), channel_id=1, source_target_pairs={{1,2},{2,1},{3,4},{4,3},{5,6},{6,5},{7,8},{8,7},{9,10},{10,9},{11,... | collective-permute-start | bytes 589832 | tf_op jit(solution)/shard_map/ppermute | solution.py:560
  18.3 2.8 %collective-permute-start.4 = (bf16[208,128]{1,0:T(8,128)(2,1)S(1)}, bf16[208,128]{1,0:T(8,128)(2,1)S(1)}, u32[]{:S(2)}, u32[]{:S(2)}) collective-permute-start(bf16[208,128]{1,0:T(8,128)(2,1)S(1)} %get-tuple-element.42), channel_id=1, source_target_pairs={{0,20},{1,21},{2,22},{3,23},{4,16},{5,17},{6,18},{7,19},{8,28},{9,... | collective-permute-start | bytes 159752 | tf_op jit(solution)/shard_map/ppermute | solution.py:640
  21.1 1.3 %collective-permute-start.5 = (bf16[208,128]{1,0:T(8,128)(2,1)S(1)}, bf16[208,128]{1,0:T(8,128)(2,1)S(1)}, u32[]{:S(2)}, u32[]{:S(2)}) collective-permute-start(bf16[208,128]{1,0:T(8,128)(2,1)S(1)} %get-tuple-element.43), channel_id=1, source_target_pairs={{0,24},{1,25},{2,26},{3,27},{4,28},{5,29},{6,30},{7,31},{8,16},{9,... | collective-permute-start | bytes 159752 | tf_op jit(solution)/shard_map/ppermute | solution.py:640
  22.4 0.8 %collective-permute-start.9 = (bf16[208,128]{1,0:T(8,128)(2,1)S(1)}, bf16[208,128]{1,0:T(8,128)(2,1)S(1)}, u32[]{:S(2)}, u32[]{:S(2)}) collective-permute-start(bf16[208,128]{1,0:T(8,128)(2,1)S(1)} %get-tuple-element.47), channel_id=1, source_target_pairs={{0,28},{1,29},{2,30},{3,31},{4,24},{5,25},{6,26},{7,27},{8,20},{9,... | collective-permute-start | bytes 159752 | tf_op jit(solution)/shard_map/ppermute | solution.py:640
  23.2 0.0 collective-permute-done.2.rest_1_
  23.2 0.6 collective-permute-start.10
  23.8 0.0 slice-done
  23.8 0.0 slice-done.1
  23.8 0.0 slice-done.2
  23.8 2.8 %shard_map.89 = (bf16[208,128]{1,0:T(8,128)(2,1)S(1)}, bf16[208,128]{1,0:T(8,128)(2,1)S(1)}) custom-call(s32[8,24]{1,0:T(8,128)S(1)} %get-tuple-element.37.which.unread, bf16[24,2048,128]{2,1,0:T(8,128)(2,1)S(1)} %bitcast.1, s32[8,24]{1,0:T(8,128)S(1)} %get-tuple-element.37.which.unread, bf16[208,128]{1,0:T(8,128)(2,1)S(1)} %get-tuple-element.38.rest_0_, ...), custom_call_target="tpu_custom_call" | custom-call | flops 805306368 | bytes 4194304 | tf_op jit(solution)/shard_map/pallas_call | solution.py:649
  26.6 0.0 collective-permute-done.4.rest_0_
  26.6 2.1 %collective-permute-start.11 = (bf16[208,128]{1,0:T(8,128)(2,1)S(1)}, bf16[208,128]{1,0:T(8,128)(2,1)S(1)}, u32[]{:S(2)}, u32[]{:S(2)}) collective-permute-start(bf16[208,128]{1,0:T(8,128)(2,1)S(1)} %get-tuple-element.49), channel_id=1, source_target_pairs={{0,8},{1,9},{2,10},{3,11},{4,12},{5,13},{6,14},{7,15},{8,0},{9,1},... | collective-permute-start | bytes 159752 | tf_op jit(solution)/shard_map/ppermute | solution.py:640
  28.7 0.0 collective-permute-done.5.rest_1_
  28.7 0.8 %collective-permute-start.12 = (bf16[208,128]{1,0:T(8,128)(2,1)S(1)}, bf16[208,128]{1,0:T(8,128)(2,1)S(1)}, u32[]{:S(2)}, u32[]{:S(2)}) collective-permute-start(bf16[208,128]{1,0:T(8,128)(2,1)S(1)} %get-tuple-element.50), channel_id=1, source_target_pairs={{0,12},{1,13},{2,14},{3,15},{4,8},{5,9},{6,10},{7,11},{8,4},{9,5},... | collective-permute-start | bytes 159752 | tf_op jit(solution)/shard_map/ppermute | solution.py:640
  29.5 2.8 %shard_map.90 = (bf16[208,128]{1,0:T(8,128)(2,1)S(1)}, bf16[208,128]{1,0:T(8,128)(2,1)S(1)}) custom-call(s32[8,24]{1,0:T(8,128)S(1)} %get-tuple-element.37.which.unread, bf16[24,2048,128]{2,1,0:T(8,128)(2,1)S(1)} %bitcast.1, bf16[208,128]{1,0:T(8,128)(2,1)S(1)} %get-tuple-element.40.unread.rest_0_, bf16[208,128]{1,0:T(8,128)(2,1)S(1)} %collective-permute-done.4.rest_0_, ...), custom_call_target="tpu_custom_call" | custom-call | flops 805306368 | bytes 4194304 | tf_op jit(solution)/shard_map/pallas_call | solution.py:649
  32.3 0.0 collective-permute-done.9.rest_0_
  32.3 2.7 %collective-permute-start.3 = (bf16[208,128]{1,0:T(8,128)(2,1)S(1)}, bf16[208,128]{1,0:T(8,128)(2,1)S(1)}, u32[]{:S(2)}, u32[]{:S(2)}) collective-permute-start(bf16[208,128]{1,0:T(8,128)(2,1)S(1)} %get-tuple-element.41), channel_id=1, source_target_pairs={{0,16},{1,17},{2,18},{3,19},{4,20},{5,21},{6,22},{7,23},{8,24},{9,... | collective-permute-start | bytes 159752 | tf_op jit(solution)/shard_map/ppermute | solution.py:640
  35.0 0.0 collective-permute-done.10.rest_1_
  35.0 1.1 %collective-permute-start.6 = (bf16[208,128]{1,0:T(8,128)(2,1)S(1)}, bf16[208,128]{1,0:T(8,128)(2,1)S(1)}, u32[]{:S(2)}, u32[]{:S(2)}) collective-permute-start(bf16[208,128]{1,0:T(8,128)(2,1)S(1)} %get-tuple-element.44), channel_id=1, source_target_pairs={{0,20},{1,21},{2,22},{3,23},{4,16},{5,17},{6,18},{7,19},{8,28},{9,... | collective-permute-start | bytes 159752 | tf_op jit(solution)/shard_map/ppermute | solution.py:640
  36.2 0.0 collective-permute-done.11.rest_2_
  36.2 1.2 %collective-permute-start.7 = (bf16[208,128]{1,0:T(8,128)(2,1)S(1)}, bf16[208,128]{1,0:T(8,128)(2,1)S(1)}, u32[]{:S(2)}, u32[]{:S(2)}) collective-permute-start(bf16[208,128]{1,0:T(8,128)(2,1)S(1)} %get-tuple-element.45), channel_id=1, source_target_pairs={{0,24},{1,25},{2,26},{3,27},{4,28},{5,29},{6,30},{7,31},{8,16},{9,... | collective-permute-start | bytes 159752 | tf_op jit(solution)/shard_map/ppermute | solution.py:640
  37.3 0.0 collective-permute-done.12.rest_3_
  37.4 0.0 collective-permute-done.8.unread.half_b
  37.4 4.6 %shard_map.91 = (bf16[208,128]{1,0:T(8,128)(2,1)S(1)}, bf16[208,128]{1,0:T(8,128)(2,1)S(1)}, bf16[208,128]{1,0:T(8,128)(2,1)S(1)}, bf16[208,128]{1,0:T(8,128)(2,1)S(1)}) custom-call(s32[8,24]{1,0:T(8,128)S(1)} %get-tuple-element.37.which.unread, bf16[24,2048,128]{2,1,0:T(8,128)(2,1)S(1)} %bitcast.1, ...), custom_call_target="tpu_custom_call" | custom-call | flops 1610612736 | bytes 4194304 | tf_op jit(solution)/shard_map/pallas_call | solution.py:649
  42.0 0.3 collective-permute-start.13
  42.3 1.2 %collective-permute-start.14 = (bf16[208,128]{1,0:T(8,128)(2,1)S(1)}, bf16[208,128]{1,0:T(8,128)(2,1)S(1)}, u32[]{:S(2)}, u32[]{:S(2)}) collective-permute-start(bf16[208,128]{1,0:T(8,128)(2,1)S(1)} %get-tuple-element.52), channel_id=1, source_target_pairs={{0,4},{1,5},{2,6},{3,7},{4,0},{5,1},{6,2},{7,3},{8,12},{9,13},{10,... | collective-permute-start | bytes 159752 | tf_op jit(solution)/shard_map/ppermute | solution.py:640
  43.5 0.0 collective-permute-done.3.rest_1_
  43.5 2.0 %collective-permute-start.15 = (bf16[208,128]{1,0:T(8,128)(2,1)S(1)}, bf16[208,128]{1,0:T(8,128)(2,1)S(1)}, u32[]{:S(2)}, u32[]{:S(2)}) collective-permute-start(bf16[208,128]{1,0:T(8,128)(2,1)S(1)} %get-tuple-element.53), channel_id=1, source_target_pairs={{0,8},{1,9},{2,10},{3,11},{4,12},{5,13},{6,14},{7,15},{8,0},{9,1},... | collective-permute-start | bytes 159752 | tf_op jit(solution)/shard_map/ppermute | solution.py:640
  45.5 0.0 collective-permute-done.6.rest_2_
  45.5 0.8 %collective-permute-start.16 = (bf16[208,128]{1,0:T(8,128)(2,1)S(1)}, bf16[208,128]{1,0:T(8,128)(2,1)S(1)}, u32[]{:S(2)}, u32[]{:S(2)}) collective-permute-start(bf16[208,128]{1,0:T(8,128)(2,1)S(1)} %get-tuple-element.54), channel_id=1, source_target_pairs={{0,12},{1,13},{2,14},{3,15},{4,8},{5,9},{6,10},{7,11},{8,4},{9,5},... | collective-permute-start | bytes 159752 | tf_op jit(solution)/shard_map/ppermute | solution.py:640
  46.3 0.0 collective-permute-done.7.rest_3_
  46.3 0.0 collective-permute-done.13.rest_4_
  46.3 0.0 collective-permute-done.14.rest_5_
  46.3 1.1 %collective-permute-done.15.rest_6_ = bf16[208,128]{1,0:T(8,128)(2,1)S(1)} collective-permute-done((bf16[208,128]{1,0:T(8,128)(2,1)S(1)}, bf16[208,128]{1,0:T(8,128)(2,1)S(1)}, u32[]{:S(2)}, u32[]{:S(2)}) %collective-permute-start.15) | collective-permute-done | bytes 53280 | tf_op jit(solution)/shard_map/ppermute | solution.py:640
  47.4 2.0 %collective-permute-done.16.rest_7_ = bf16[208,128]{1,0:T(8,128)(2,1)S(1)} collective-permute-done((bf16[208,128]{1,0:T(8,128)(2,1)S(1)}, bf16[208,128]{1,0:T(8,128)(2,1)S(1)}, u32[]{:S(2)}, u32[]{:S(2)}) %collective-permute-start.16) | collective-permute-done | bytes 53280 | tf_op jit(solution)/shard_map/ppermute | solution.py:640
  49.4 1.1 %shard_map.92 = (f32[8,128,128]{2,1,0:T(8,128)S(1)}, bf16[8,128,128]{2,1,0:T(8,128)(2,1)S(1)}, bf16[7,128,128]{2,1,0:T(8,128)(2,1)S(1)}, bf16[1,128,128]{2,1,0:T(8,128)(2,1)S(1)}) custom-call(s32[8,24]{1,0:T(8,128)S(1)} %get-tuple-element.32.place, bf16[2,8,3,128,128]{4,3,2,1,0:T(8,128)(2,1)S(1)} %copy-done, ...), custom_call_target="tpu_custom_call" | custom-call | flops 1048576 | bytes 4194304 | tf_op jit(solution)/shard_map/pallas_call | solution.py:660
  50.5 10.2 %collective-permute-start.18 = (bf16[1,128,128]{2,1,0:T(8,128)(2,1)S(1)}, bf16[1,128,128]{2,1,0:T(8,128)(2,1)S(1)}, u32[]{:S(2)}, u32[]{:S(2)}) collective-permute-start(bf16[1,128,128]{2,1,0:T(8,128)(2,1)S(1)} %get-tuple-element.57), channel_id=1, source_target_pairs={{1,2},{2,1},{3,4},{4,3},{5,6},{6,5},{7,8},{8,7},{9,10},{10,9},{11,... | collective-permute-start | bytes 98312 | tf_op jit(solution)/shard_map/ppermute | solution.py:560
  60.7 0.1 collective-permute-start.17
  60.8 3.2 %shard_map.93 = (bf16[2,4,3,128,128]{4,3,2,1,0:T(8,128)(2,1)S(1)}, bf16[10,3,128,256]{3,2,1,0:T(8,128)(2,1)S(1)}, f32[8,128,128]{2,1,0:T(8,128)}) custom-call(s32[8]{0:T(128)S(1)} %copy-done.4, f32[8]{0:T(128)S(1)} %copy-done.5, bf16[2,8,3,128,128]{4,3,2,1,0:T(8,128)(2,1)S(1)} %get-tuple-element.36.half, bf16[2,8,3,128,128]{4,3,2,1,0:T(8,128)(2,1)S(1)} %copy-done, ...), custom_call_target="tpu_custom_call" | custom-call | flops 4294967296 | bytes 4194304 | tf_op jit(solution)/shard_map/pallas_call | solution.py:677
  63.9 0.0 collective-permute-done.18.got_b
  64.0 0.0 collective-permute-done.17.got_a
  64.0 3.7 %shard_map.94 = bf16[2,8,3,128,128]{4,3,2,1,0:T(8,128)(2,1)} custom-call(s32[8]{0:T(128)S(1)} %copy-done.4, f32[8]{0:T(128)S(1)} %copy-done.5, bf16[2,8,3,128,128]{4,3,2,1,0:T(8,128)(2,1)S(1)} %get-tuple-element.36.half, bf16[2,8,3,128,128]{4,3,2,1,0:T(8,128)(2,1)S(1)} %copy-done, bf16[8,128,128]{2,1,0:T(8,128)(2,1)S(1)} %get-tuple-element.55.diag_new, ...), custom_call_target="tpu_custom_call" | custom-call | flops 4294967296 | bytes 4194304 | tf_op jit(solution)/shard_map/pallas_call | solution.py:691
  (2 shorter events, 0.0 us)
Async XLA Ops:
  0.6 5.0 %copy-start = (bf16[2,8,3,128,128]{4,3,2,1,0:T(8,128)(2,1)S(1)}, bf16[2,8,3,128,128]{4,3,2,1,0:T(8,128)(2,1)}, u32[]{:S(2)}) copy-start(bf16[2,8,3,128,128]{4,3,2,1,0:T(8,128)(2,1)} %core.11) | copy-start | bytes 4718596
  0.6 5.0 %copy-start.2 = (f32[8,128,128]{2,1,0:T(8,128)S(1)}, f32[8,128,128]{2,1,0:T(8,128)}, u32[]{:S(2)}) copy-start(f32[8,128,128]{2,1,0:T(8,128)} %grid_old.5) | copy-start | bytes 1572868
  0.7 5.0 %copy-start.1 = (bf16[2,8,3,128,128]{4,3,2,1,0:T(8,128)(2,1)S(1)}, bf16[2,8,3,128,128]{4,3,2,1,0:T(8,128)(2,1)}, u32[]{:S(2)}) copy-start(bf16[2,8,3,128,128]{4,3,2,1,0:T(8,128)(2,1)} %dens.5) | copy-start | bytes 4718596
  0.7 5.0 %copy-start.5 = (f32[8]{0:T(128)S(1)}, f32[8]{0:T(128)}, u32[]{:S(2)}) copy-start(f32[8]{0:T(128)} %absorption.7) | copy-start | bytes 100
  0.7 5.0 %copy-start.4 = (s32[8]{0:T(128)S(1)}, s32[8]{0:T(128)}, u32[]{:S(2)}) copy-start(s32[8]{0:T(128)} %leads.7) | copy-start | bytes 100
  0.7 5.0 %copy-start.3 = (s32[8,24]{1,0:T(8,128)S(1)}, s32[8,24]{1,0:T(8,128)}, u32[]{:S(2)}) copy-start(s32[8,24]{1,0:T(8,128)} %owners.1) | copy-start | bytes 2308
  2.0 8.9 %collective-permute-start.1 = (bf16[6,128,128]{2,1,0:T(8,128)(2,1)S(1)}, bf16[6,128,128]{2,1,0:T(8,128)(2,1)S(1)}, u32[]{:S(2)}, u32[]{:S(2)}) collective-permute-start(bf16[6,128,128]{2,1,0:T(8,128)(2,1)S(1)} %shard_map.87), channel_id=1, source_target_pairs={{1,2},{2,1},{3,4},{4,3},{5,6},{6,5},{7,8},{8,7},{9,10},{10,9},{11,... | collective-permute-start | bytes 589832 | tf_op jit(solution)/shard_map/ppermute | solution.py:560
  5.7 18.0 %slice-start = ((s8[12582912]{0:T(1024)(128)(4,1)}), s8[4194304]{0:T(1024)(128)(4,1)S(1)}, s32[]{:S(2)}) async-start(s8[12582912]{0:T(1024)(128)(4,1)} %bitcast), calls=%async_computation | async-start | bytes 8388608
  5.7 18.0 %slice-start.1 = ((s8[12582912]{0:T(1024)(128)(4,1)}), s8[4194304]{0:T(1024)(128)(4,1)S(1)}, s32[]{:S(2)}) async-start(s8[12582912]{0:T(1024)(128)(4,1)} %bitcast), calls=%async_computation.1 | async-start | bytes 8388608
  9.3 1.6 %collective-permute-start = (bf16[6,128,128]{2,1,0:T(8,128)(2,1)S(1)}, bf16[6,128,128]{2,1,0:T(8,128)(2,1)S(1)}, u32[]{:S(2)}, u32[]{:S(2)}) collective-permute-start(bf16[6,128,128]{2,1,0:T(8,128)(2,1)S(1)} %get-tuple-element.33), channel_id=1, source_target_pairs={{0,1},{1,0},{2,3},{3,2},{4,5},{5,4},{6,7},{7,6},{8,9},{9,8},{10,11... | collective-permute-start | bytes 589832 | tf_op jit(solution)/shard_map/ppermute | solution.py:556
  10.9 12.9 %slice-start.2 = ((s8[12582912]{0:T(1024)(128)(4,1)}), s8[4194304]{0:T(1024)(128)(4,1)S(1)}, s32[]{:S(2)}) async-start(s8[12582912]{0:T(1024)(128)(4,1)} %bitcast), calls=%async_computation.2 | async-start | bytes 8388608
  14.4 8.8 %collective-permute-start.2 = (bf16[208,128]{1,0:T(8,128)(2,1)S(1)}, bf16[208,128]{1,0:T(8,128)(2,1)S(1)}, u32[]{:S(2)}, u32[]{:S(2)}) collective-permute-start(bf16[208,128]{1,0:T(8,128)(2,1)S(1)} %get-tuple-element.39), channel_id=1, source_target_pairs={{0,16},{1,17},{2,18},{3,19},{4,20},{5,21},{6,22},{7,23},{8,24},{9,... | collective-permute-start | bytes 159752 | tf_op jit(solution)/shard_map/ppermute | solution.py:640
  15.2 22.2 %collective-permute-start.8 = (bf16[6,128,128]{2,1,0:T(8,128)(2,1)S(1)}, bf16[6,128,128]{2,1,0:T(8,128)(2,1)S(1)}, u32[]{:S(2)}, u32[]{:S(2)}) collective-permute-start(bf16[6,128,128]{2,1,0:T(8,128)(2,1)S(1)} %get-tuple-element.46), channel_id=1, source_target_pairs={{1,2},{2,1},{3,4},{4,3},{5,6},{6,5},{7,8},{8,7},{9,10},{10,9},{11,... | collective-permute-start | bytes 589832 | tf_op jit(solution)/shard_map/ppermute | solution.py:560
  18.3 8.3 %collective-permute-start.4 = (bf16[208,128]{1,0:T(8,128)(2,1)S(1)}, bf16[208,128]{1,0:T(8,128)(2,1)S(1)}, u32[]{:S(2)}, u32[]{:S(2)}) collective-permute-start(bf16[208,128]{1,0:T(8,128)(2,1)S(1)} %get-tuple-element.42), channel_id=1, source_target_pairs={{0,20},{1,21},{2,22},{3,23},{4,16},{5,17},{6,18},{7,19},{8,28},{9,... | collective-permute-start | bytes 159752 | tf_op jit(solution)/shard_map/ppermute | solution.py:640
  21.1 7.6 %collective-permute-start.5 = (bf16[208,128]{1,0:T(8,128)(2,1)S(1)}, bf16[208,128]{1,0:T(8,128)(2,1)S(1)}, u32[]{:S(2)}, u32[]{:S(2)}) collective-permute-start(bf16[208,128]{1,0:T(8,128)(2,1)S(1)} %get-tuple-element.43), channel_id=1, source_target_pairs={{0,24},{1,25},{2,26},{3,27},{4,28},{5,29},{6,30},{7,31},{8,16},{9,... | collective-permute-start | bytes 159752 | tf_op jit(solution)/shard_map/ppermute | solution.py:640
  22.4 9.9 %collective-permute-start.9 = (bf16[208,128]{1,0:T(8,128)(2,1)S(1)}, bf16[208,128]{1,0:T(8,128)(2,1)S(1)}, u32[]{:S(2)}, u32[]{:S(2)}) collective-permute-start(bf16[208,128]{1,0:T(8,128)(2,1)S(1)} %get-tuple-element.47), channel_id=1, source_target_pairs={{0,28},{1,29},{2,30},{3,31},{4,24},{5,25},{6,26},{7,27},{8,20},{9,... | collective-permute-start | bytes 159752 | tf_op jit(solution)/shard_map/ppermute | solution.py:640
  23.2 11.9 %collective-permute-start.10 = (bf16[208,128]{1,0:T(8,128)(2,1)S(1)}, bf16[208,128]{1,0:T(8,128)(2,1)S(1)}, u32[]{:S(2)}, u32[]{:S(2)}) collective-permute-start(bf16[208,128]{1,0:T(8,128)(2,1)S(1)} %get-tuple-element.48), channel_id=1, source_target_pairs={{0,4},{1,5},{2,6},{3,7},{4,0},{5,1},{6,2},{7,3},{8,12},{9,13},{10,... | collective-permute-start | bytes 159752 | tf_op jit(solution)/shard_map/ppermute | solution.py:640
  26.6 9.5 %collective-permute-start.11 = (bf16[208,128]{1,0:T(8,128)(2,1)S(1)}, bf16[208,128]{1,0:T(8,128)(2,1)S(1)}, u32[]{:S(2)}, u32[]{:S(2)}) collective-permute-start(bf16[208,128]{1,0:T(8,128)(2,1)S(1)} %get-tuple-element.49), channel_id=1, source_target_pairs={{0,8},{1,9},{2,10},{3,11},{4,12},{5,13},{6,14},{7,15},{8,0},{9,1},... | collective-permute-start | bytes 159752 | tf_op jit(solution)/shard_map/ppermute | solution.py:640
  28.7 8.6 %collective-permute-start.12 = (bf16[208,128]{1,0:T(8,128)(2,1)S(1)}, bf16[208,128]{1,0:T(8,128)(2,1)S(1)}, u32[]{:S(2)}, u32[]{:S(2)}) collective-permute-start(bf16[208,128]{1,0:T(8,128)(2,1)S(1)} %get-tuple-element.50), channel_id=1, source_target_pairs={{0,12},{1,13},{2,14},{3,15},{4,8},{5,9},{6,10},{7,11},{8,4},{9,5},... | collective-permute-start | bytes 159752 | tf_op jit(solution)/shard_map/ppermute | solution.py:640
  32.3 11.2 %collective-permute-start.3 = (bf16[208,128]{1,0:T(8,128)(2,1)S(1)}, bf16[208,128]{1,0:T(8,128)(2,1)S(1)}, u32[]{:S(2)}, u32[]{:S(2)}) collective-permute-start(bf16[208,128]{1,0:T(8,128)(2,1)S(1)} %get-tuple-element.41), channel_id=1, source_target_pairs={{0,16},{1,17},{2,18},{3,19},{4,20},{5,21},{6,22},{7,23},{8,24},{9,... | collective-permute-start | bytes 159752 | tf_op jit(solution)/shard_map/ppermute | solution.py:640
  35.0 10.5 %collective-permute-start.6 = (bf16[208,128]{1,0:T(8,128)(2,1)S(1)}, bf16[208,128]{1,0:T(8,128)(2,1)S(1)}, u32[]{:S(2)}, u32[]{:S(2)}) collective-permute-start(bf16[208,128]{1,0:T(8,128)(2,1)S(1)} %get-tuple-element.44), channel_id=1, source_target_pairs={{0,20},{1,21},{2,22},{3,23},{4,16},{5,17},{6,18},{7,19},{8,28},{9,... | collective-permute-start | bytes 159752 | tf_op jit(solution)/shard_map/ppermute | solution.py:640
  36.2 10.1 %collective-permute-start.7 = (bf16[208,128]{1,0:T(8,128)(2,1)S(1)}, bf16[208,128]{1,0:T(8,128)(2,1)S(1)}, u32[]{:S(2)}, u32[]{:S(2)}) collective-permute-start(bf16[208,128]{1,0:T(8,128)(2,1)S(1)} %get-tuple-element.45), channel_id=1, source_target_pairs={{0,24},{1,25},{2,26},{3,27},{4,28},{5,29},{6,30},{7,31},{8,16},{9,... | collective-permute-start | bytes 159752 | tf_op jit(solution)/shard_map/ppermute | solution.py:640
  42.0 4.3 %collective-permute-start.13 = (bf16[208,128]{1,0:T(8,128)(2,1)S(1)}, bf16[208,128]{1,0:T(8,128)(2,1)S(1)}, u32[]{:S(2)}, u32[]{:S(2)}) collective-permute-start(bf16[208,128]{1,0:T(8,128)(2,1)S(1)} %get-tuple-element.51), channel_id=1, source_target_pairs={{0,28},{1,29},{2,30},{3,31},{4,24},{5,25},{6,26},{7,27},{8,20},{9,... | collective-permute-start | bytes 159752 | tf_op jit(solution)/shard_map/ppermute | solution.py:640
  42.3 4.0 %collective-permute-start.14 = (bf16[208,128]{1,0:T(8,128)(2,1)S(1)}, bf16[208,128]{1,0:T(8,128)(2,1)S(1)}, u32[]{:S(2)}, u32[]{:S(2)}) collective-permute-start(bf16[208,128]{1,0:T(8,128)(2,1)S(1)} %get-tuple-element.52), channel_id=1, source_target_pairs={{0,4},{1,5},{2,6},{3,7},{4,0},{5,1},{6,2},{7,3},{8,12},{9,13},{10,... | collective-permute-start | bytes 159752 | tf_op jit(solution)/shard_map/ppermute | solution.py:640
  43.5 3.9 %collective-permute-start.15 = (bf16[208,128]{1,0:T(8,128)(2,1)S(1)}, bf16[208,128]{1,0:T(8,128)(2,1)S(1)}, u32[]{:S(2)}, u32[]{:S(2)}) collective-permute-start(bf16[208,128]{1,0:T(8,128)(2,1)S(1)} %get-tuple-element.53), channel_id=1, source_target_pairs={{0,8},{1,9},{2,10},{3,11},{4,12},{5,13},{6,14},{7,15},{8,0},{9,1},... | collective-permute-start | bytes 159752 | tf_op jit(solution)/shard_map/ppermute | solution.py:640
  45.5 3.9 %collective-permute-start.16 = (bf16[208,128]{1,0:T(8,128)(2,1)S(1)}, bf16[208,128]{1,0:T(8,128)(2,1)S(1)}, u32[]{:S(2)}, u32[]{:S(2)}) collective-permute-start(bf16[208,128]{1,0:T(8,128)(2,1)S(1)} %get-tuple-element.54), channel_id=1, source_target_pairs={{0,12},{1,13},{2,14},{3,15},{4,8},{5,9},{6,10},{7,11},{8,4},{9,5},... | collective-permute-start | bytes 159752 | tf_op jit(solution)/shard_map/ppermute | solution.py:640
  50.5 13.4 %collective-permute-start.18 = (bf16[1,128,128]{2,1,0:T(8,128)(2,1)S(1)}, bf16[1,128,128]{2,1,0:T(8,128)(2,1)S(1)}, u32[]{:S(2)}, u32[]{:S(2)}) collective-permute-start(bf16[1,128,128]{2,1,0:T(8,128)(2,1)S(1)} %get-tuple-element.57), channel_id=1, source_target_pairs={{1,2},{2,1},{3,4},{4,3},{5,6},{6,5},{7,8},{8,7},{9,10},{10,9},{11,... | collective-permute-start | bytes 98312 | tf_op jit(solution)/shard_map/ppermute | solution.py:560
  60.7 3.3 %collective-permute-start.17 = (bf16[7,128,128]{2,1,0:T(8,128)(2,1)S(1)}, bf16[7,128,128]{2,1,0:T(8,128)(2,1)S(1)}, u32[]{:S(2)}, u32[]{:S(2)}) collective-permute-start(bf16[7,128,128]{2,1,0:T(8,128)(2,1)S(1)} %get-tuple-element.56), channel_id=1, source_target_pairs={{0,1},{1,0},{2,3},{3,2},{4,5},{5,4},{6,7},{7,6},{8,9},{9,8},{10,11... | collective-permute-start | bytes 688136 | tf_op jit(solution)/shard_map/ppermute | solution.py:556
